TPU v7x, 32 devices: a whole 2x2x4 slice. The times are simulated.
32 devices in a mesh: rep: 8 (over z, core), shard: 4 (over y, x).
Axes of the slice: x: 2, y: 2, z: 4, core: 2. Of those that a mesh axis runs over, the one named last changes fastest.
Arguments:
- hidden: bfloat16 [16384, 1536], P(('rep', 'shard')), may hold values from -6 to 6
- out_grad: bfloat16 [16384, 1536], P(('rep', 'shard')), may hold values from -6 to 6
- norm_gain: bfloat16 [1536], P('shard'), may hold values from 0.5 to 1.5
- in_w: bfloat16 [1536, 6448], P('shard'), may hold values from -0.15625 to 0.15625
- conv_w: bfloat16 [3328, 4], P('shard'), may hold values from -3 to 3
- conv_b: bfloat16 [3328], P('shard'), may hold values from -0.5 to 0.5
- dt_bias: bfloat16 [48], P('shard'), may hold values from -7 to -2.5
- a_log: bfloat16 [48], P('shard'), may hold values from 0 to 2.5
- skip: bfloat16 [48], P('shard'), may hold values from 0.5 to 1.5
- out_gain: bfloat16 [3072], P('shard'), may hold values from 0.5 to 1.5
- out_w: bfloat16 [3072, 1536], P('shard'), may hold values from -0.109375 to 0.109375
- lengths: int32 [32], P(('rep', 'shard')), may hold values from 256 to 512, as said below
- offsets: int32 [32], P(('rep', 'shard')), may hold values from 0 to 256, as said below
Outputs:
- block_out: bfloat16 [16384, 1536], P(('rep', 'shard'))
- hidden_grad: float32 [16384, 1536], P(('rep', 'shard'))
- norm_gain_grad: float32 [1536], P('shard')
- in_w_grad: float32 [1536, 6448], P('shard')
- conv_w_grad: float32 [3328, 4], P('shard')
- conv_b_grad: float32 [3328], P('shard')
- dt_bias_grad: float32 [48], P('shard')
- a_log_grad: float32 [48], P('shard')
- skip_grad: float32 [48], P('shard')
- out_gain_grad: float32 [3072], P('shard')
- out_w_grad: float32 [3072, 1536], P('shard')
Inputs may be any that keep to these rules, and one draw needn't show every extreme that they name: `lengths`: in every draw some device's sequence fills all 512 slots, and another device's sequence holds exactly 256 tokens. offsets + lengths <= 512 for every device; in every draw the device with 256 live tokens has its sequence end at its last slot.
All inputs are finite; a program needn't handle non-finite values.
Results may differ from a plain program's by a relative error of at most 0.012.
The roundings to bfloat16 on the way count: a program that leaves them out, or rounds other values in their place, can miss the bound.
Values may be sent and summed in bfloat16 or wider, within the bound.
No kernel may reach another device: no remote copies, remote signals or barrier semaphores. Data moves between devices by JAX's collectives and lax.ppermute only.
A program may use at most 256 MiB of HBM per device.

v0:
```python
import functools

import jax
import jax.numpy as jnp
from jax import lax
from jax.experimental import pallas as pl
from jax.experimental.pallas import tpu as pltpu
from jax.sharding import PartitionSpec as P

HEADS = 48
HEADDIM = 64
DSTATE = 128
CONV = 4
SPAN = 256
DI = 3072
CC = 3328
TILE = 256
GROUPS = DI // TILE
PER = TILE // HEADDIM
CHUNK = 64
LANES = 128
epsilon = 1e-05
FAR = -1e30
LOG2E = 1.4426950408889634
PACK = 4 * PER

BF = jnp.bfloat16
F32 = jnp.float32
MIB = 1 << 20


def dot(lhs, rhs):
    return jnp.dot(lhs, rhs, preferred_element_type=F32)


def dot_nt(lhs, rhs):
    return lax.dot_general(lhs, rhs, (((1,), (1,)), ((), ())), preferred_element_type=F32)


def dot_tn(lhs, rhs):
    return lax.dot_general(lhs, rhs, (((0,), (0,)), ((), ())), preferred_element_type=F32)


def sigmoid(value):
    return 0.5 * jnp.tanh(0.5 * value) + 0.5


def pieces(value):
    high = value.astype(BF)
    rest = value - high.astype(F32)
    middle = rest.astype(BF)
    low = (rest - middle.astype(F32)).astype(BF)
    return high, middle, low


def fine_dot(lhs, rhs, product):
    high, middle, low = pieces(lhs)
    return product(high, rhs) + (product(middle, rhs) + product(low, rhs))


def row_ids(start, shape):
    return start + lax.broadcasted_iota(jnp.int32, shape, 0)


def live_rows(meta, start, shape):
    ids = row_ids(start, shape)
    return (ids >= meta[1]) & (ids < meta[1] + meta[2])


def gather_lanes(target, blocks, table, at):
    for j, block in enumerate(blocks):
        width = block.shape[1]
        lanes = pl.ds(pl.multiple_of(table[at + j] * width, LANES), width)
        target[0 : block.shape[0], lanes] = block[...]


def call(
    body, name, meta, operands, in_specs, outs, out_specs, scratch, grid, flops, moved, filled=None
):
    if filled:
        first = len(operands) + 1
        operands, extra = operands + tuple(filled.values()), len(filled)
        in_specs = in_specs + [pl.BlockSpec(memory_space=pl.ANY)] * extra
        aliases = {first + n: place for n, place in enumerate(filled)}
        inner, many = body, first - 1

        def body(meta, *refs):
            return inner(meta, *refs[:many], *refs[many + extra :])
    else:
        aliases = {}
    return pl.pallas_call(
        body,
        name=name,
        grid_spec=pltpu.PrefetchScalarGridSpec(
            num_scalar_prefetch=1,
            grid=(grid,),
            in_specs=in_specs,
            out_specs=out_specs,
            scratch_shapes=scratch,
        ),
        out_shape=outs,
        input_output_aliases=aliases,
        compiler_params=pltpu.CompilerParams(vmem_limit_bytes=60 * MIB),
        cost_estimate=pl.CostEstimate(flops=flops, bytes_accessed=moved, transcendentals=0),
    )(meta, *operands)


def whole(shape):
    rank = len(shape)
    return pl.BlockSpec(shape, lambda i, meta: (0,) * rank)


def tiles(rows, width, shift=0, last=None):
    def index(i, meta):
        at = i + shift
        if last is not None:
            at = jnp.clip(at, 0, last)
        return (0, at)

    return pl.BlockSpec((rows, width), index)


def shape_of(shape, kind=F32):
    return jax.ShapeDtypeStruct(shape, kind)


TABLE = 4
UNITS = 4
OUT_TABLE = TABLE + 2 * UNITS
WIDE = 512
WIDES = DI // WIDE


def own_tile(i, meta):
    half = WIDES // 2
    return jnp.where(i < half, meta[0] * half + i, (1 - meta[0]) * half + i - half)


def live_lanes(meta, live):
    live[...] = jnp.where(live_rows(meta, 0, live.shape), 1.0, 0.0)


def convolve(low, taps, live, shifted, masked, signal, slope, begin):
    for lane in range(0, low.shape[1], LANES):
        cut = slice(begin + lane, begin + lane + LANES)
        tile = (begin + lane) // LANES
        for at in range(0, low.shape[0], CHUNK):
            part = low[at : at + CHUNK, lane : lane + LANES].astype(BF).astype(F32)
            part = part * live[at : at + CHUNK, :]
            masked[at : at + CHUNK, cut] = part.astype(BF)
            shifted[tile, 8 + at : 8 + at + CHUNK, :] = part
        for at in range(0, low.shape[0], CHUNK):
            out = taps[4:5, cut]
            for k in range(CONV):
                out = out + shifted[tile, at + 5 + k : at + 5 + k + CHUNK, :] * taps[k : k + 1, cut]
            sigma = sigmoid(out)
            out = out * sigma
            here = live[at : at + CHUNK, :]
            signal[at : at + CHUNK, cut] = (out * here).astype(BF)
            slope[at : at + CHUNK, cut] = (sigma + out * (1.0 - sigma)) * here


def conv_body(meta, x, taps, taps_keys, steps, *refs):
    count = UNITS
    own, rest, key_rows, dts = (refs[n * count : (n + 1) * count] for n in range(4))
    (masked, signal, slope, masked_keys, keys, slope_keys, columns, rows, trio,
     weight, weight_dt, shifted, live) = refs[4 * count :]
    tokens = x.shape[0]
    step = pl.program_id(0)

    @pl.when(step == 0)
    def _():
        shifted[:, 0:8, :] = jnp.zeros((WIDE // LANES, 8, LANES), F32)
        live_lanes(meta, live)
        gather_lanes(weight, key_rows, meta, TABLE)
        gather_lanes(weight_dt, dts, meta, TABLE)
        low = dot_nt(x[...], weight[0:TILE, :])
        raw = dot_nt(x[...], weight_dt[...]).astype(BF).astype(F32)
        convolve(low, taps_keys, live, shifted, masked_keys, keys, slope_keys, 0)
        raw = jnp.concatenate([raw, jnp.zeros((tokens, LANES - raw.shape[1]), F32)], axis=1)
        pre = raw + steps[0:1, :]
        size = jnp.maximum(pre, 0.0) + jnp.log1p(jnp.exp(-jnp.abs(pre)))
        rate = size * steps[1:2, :]
        lower = row_ids(0, (SPAN, SPAN)) >= lax.broadcasted_iota(jnp.int32, (SPAN, SPAN), 1)
        lower = jnp.where(lower, 1.0, 0.0).astype(BF)
        trio[0] = pre
        trio[1] = size
        for at in range(0, tokens, SPAN):
            high, middle, small = pieces(rate[at : at + SPAN])
            trio[2, at : at + SPAN, :] = dot(lower, high) + (dot(lower, middle) + dot(lower, small))
        log = trio[2] * LOG2E
        less = log - jnp.log(size) * LOG2E
        factor = jnp.concatenate(
            [jnp.exp2(log[SPAN - 1 : SPAN] - less[:SPAN]), jnp.exp2(log[SPAN:])], axis=0
        )
        high = factor.astype(BF).astype(F32)
        rest_factor = factor - high
        less_rows = less.T
        log_rows = log.T
        for g in range(GROUPS):
            a, b = g * PER, (g + 1) * PER
            columns[g] = jnp.concatenate(
                [log[:, a:b], less[:, a:b], high[:, a:b], rest_factor[:, a:b]], axis=1
            )
            rows[g] = jnp.concatenate([log_rows[a:b], less_rows[a:b]], axis=0)

    @pl.when((step > 0) & (step <= WIDES // 2))
    def _():
        gather_lanes(weight, own, meta, TABLE)

    @pl.when(step > WIDES // 2)
    def _():
        gather_lanes(weight, rest, meta, TABLE + count)

    @pl.when(step > 0)
    def _():
        lows = [dot_nt(x[...], weight[at : at + TILE, :]) for at in range(0, WIDE, TILE)]
        for n, low in enumerate(lows):
            convolve(low, taps, live, shifted, masked, signal, slope, n * TILE)


def conv_forward(meta, x, taps, steps, own, rest, local):
    tokens, width = x.shape
    count = UNITS
    part = width // count
    half = WIDES // 2

    def natural(i, meta):
        return own_tile(jnp.maximum(i - 1, 0), meta)

    def tile(rows):
        return pl.BlockSpec((rows, WIDE), lambda i, meta: (0, natural(i, meta)))

    def late(i):
        return jnp.maximum(i - 1 - half, 0)

    own_spec = pl.BlockSpec((WIDE, part), lambda i, meta: (jnp.clip(i - 1, 0, half - 1), 0))
    rest_spec = pl.BlockSpec((WIDE, part), lambda i, meta: (late(i), 0))
    local_spec = pl.BlockSpec(
        (WIDE, part), lambda i, meta: (WIDES + (1 - meta[0]) * half + late(i), 0)
    )
    key_spec = pl.BlockSpec((TILE, part), lambda i, meta: (half * WIDE // TILE, 0))
    dt_spec = pl.BlockSpec((64, part), lambda i, meta: ((half * WIDE + TILE) // 64, 0))
    return call(
        conv_body, "conv_forward", meta,
        (x, taps, taps, steps) + tuple(own) + (() if local is None else (local,)) + tuple(rest)
        + tuple(own) * 2,
        [
            whole((tokens, width)), tile(8), pl.BlockSpec((8, TILE), lambda i, meta: (0, DI // TILE)),
            whole((8, LANES)),
        ]
        + [own_spec] * count
        + [rest_spec if local is None else local_spec] + [rest_spec] * (count - 1)
        + [key_spec] * count + [dt_spec] * count,
        [
            shape_of((tokens, DI), BF), shape_of((tokens, DI), BF), shape_of((tokens, DI)),
            shape_of((tokens, TILE), BF), shape_of((tokens, TILE), BF), shape_of((tokens, TILE)),
            shape_of((GROUPS, tokens, PACK)), shape_of((GROUPS, 2 * PER, tokens)),
            shape_of((3, tokens, LANES)),
        ],
        [
            tile(tokens), tile(tokens), tile(tokens),
            whole((tokens, TILE)), whole((tokens, TILE)), whole((tokens, TILE)),
            whole((GROUPS, tokens, PACK)), whole((GROUPS, 2 * PER, tokens)),
            whole((3, tokens, LANES)),
        ],
        [
            pltpu.VMEM((WIDE, width), BF), pltpu.VMEM((64, width), BF),
            pltpu.VMEM((WIDE // LANES, tokens + 8, LANES), F32), pltpu.VMEM((tokens, LANES), F32),
        ],
        1 + WIDES, 2 * tokens * width * CC, 24 * MIB,
    )


def lane_half(shape, half):
    ids = lax.broadcasted_iota(jnp.int32, shape, 1)
    return (ids >= HEADDIM) if half else (ids < HEADDIM)


def heads_apart(value, ones):
    return jnp.concatenate([value * ones[0:1], value * ones[1:2]], axis=0)


def heads_together(stacked):
    middle = stacked.shape[0] // 2
    upper = stacked[:middle]
    return jnp.where(lane_half(upper.shape, 0), upper, stacked[middle:])


def head_lanes(shape, width):
    lane = lax.broadcasted_iota(jnp.int32, shape, 1) // width
    row = lax.broadcasted_iota(jnp.int32, shape, 0) % PER
    return jnp.where(lane == row, 1.0, 0.0).astype(BF)


def scan_body(
    meta, content, keys, columns, rows, skip, out, entering,
    scores, write_rows, mixes, blocked, spread,
):
    half = SPAN // 2

    @pl.when(pl.program_id(0) == 0)
    def _():
        for span in range(2):
            at = span * SPAN
            scores[span] = dot_nt(keys[at : at + SPAN, DSTATE:], keys[at : at + SPAN, :DSTATE])
        write_rows[...] = keys[0:SPAN, :DSTATE].astype(F32).T.astype(BF)
        mixes[...] = jnp.zeros_like(mixes)
        after = row_ids(0, blocked.shape) >= lax.broadcasted_iota(jnp.int32, blocked.shape, 1)
        blocked[...] = jnp.where(after, 0.0, FAR)
        spread[...] = head_lanes(spread.shape, HEADDIM)

    factor = dot(columns[0, :, 2 * PER :].astype(BF), spread[...])
    first = content[0:SPAN, :].astype(F32)
    state = dot(write_rows[...], (first * factor[:SPAN]).astype(BF)).astype(BF)
    entering[0] = state
    out[0:SPAN, :] = skip[...] * first
    carried = dot(keys[SPAN:, DSTATE:], state) * factor[SPAN:]
    out[SPAN:, :] = carried + skip[...] * content[SPAN:, :].astype(F32)
    for pair in range(PER // 2):
        lanes = slice(pair * 2 * HEADDIM, (pair + 1) * 2 * HEADDIM)
        for h in range(2):
            n = 2 * pair + h
            for span in range(2):
                for at in range(0, SPAN, CHUNK):
                    row = span * SPAN + at
                    corner = at // half * half
                    log = columns[0, row : row + CHUNK, n : n + 1]
                    for begin in range(0, corner + half, half):
                        cut = slice(begin, begin + half)
                        less = rows[0, PER + n : PER + n + 1, span * SPAN + begin : span * SPAN + begin + half]
                        decay = log - less
                        if begin == corner:
                            decay = decay + blocked[at - begin : at - begin + CHUNK, :]
                        mix = scores[span, at : at + CHUNK, cut] * jnp.exp2(decay)
                        mixes[pair, span, h * SPAN + at : h * SPAN + at + CHUNK, cut] = mix.astype(BF)
        for span in range(2):
            at = span * SPAN
            value = content[at : at + SPAN, lanes]
            out[at : at + SPAN, lanes] += heads_together(dot(mixes[pair, span], value))


def scan_forward(meta, signal, keys, columns, rows, skip):
    tokens = signal.shape[0]
    return call(
        scan_body, "scan_forward", meta, (signal, keys, columns, rows, skip),
        [
            tiles(tokens, TILE), whole((tokens, TILE)),
            pl.BlockSpec((1, tokens, PACK), lambda i, meta: (i, 0, 0)),
            pl.BlockSpec((1, 2 * PER, tokens), lambda i, meta: (i, 0, 0)),
            tiles(1, TILE),
        ],
        [shape_of((tokens, DI)), shape_of((GROUPS, DSTATE, TILE), BF)],
        [tiles(tokens, TILE), pl.BlockSpec((1, DSTATE, TILE), lambda i, meta: (i, 0, 0))],
        [
            pltpu.VMEM((2, SPAN, SPAN), F32), pltpu.VMEM((DSTATE, SPAN), BF),
            pltpu.VMEM((PER // 2, 2, 2 * SPAN, SPAN), BF), pltpu.VMEM((SPAN // 2, SPAN // 2), F32),
            pltpu.VMEM((2 * PER, TILE), BF),
        ],
        GROUPS, 10 * 10**9, 12 * MIB,
    )


def gate_body(meta, x, mixed, gain, *refs):
    count = UNITS
    own, rest = refs[:count], refs[count : 2 * count]
    gate, normed, theirs, scale, weight, gated, total = refs[2 * count :]
    step = pl.program_id(0)
    tokens = x.shape[0]

    @pl.when(step < WIDES // 2)
    def _():
        gather_lanes(weight, own, meta, TABLE)

    @pl.when(step >= WIDES // 2)
    def _():
        gather_lanes(weight, rest, meta, TABLE + count)

    @pl.when(step == 0)
    def _():
        total[...] = jnp.zeros_like(total)

    here = own_tile(step, meta) * WIDE
    lows = [dot_nt(x[...], weight[at : at + TILE, :]).astype(BF) for at in range(0, WIDE, TILE)]
    for n, low in enumerate(lows):
        lanes = slice(n * TILE, (n + 1) * TILE)
        place = pl.ds(pl.multiple_of(here + n * TILE, TILE), TILE)
        gate[:, lanes] = low
        for at in range(0, tokens, CHUNK):
            part = low[at : at + CHUNK].astype(F32)
            part = mixed[at : at + CHUNK, lanes] * (part * sigmoid(part))
            gated[at : at + CHUNK, place] = part
            square = part * part
            total[at : at + CHUNK, :] += square[:, :LANES] + square[:, LANES:]

    @pl.when(step == pl.num_programs(0) - 1)
    def _():
        mean = jnp.sum(total[...], axis=1, keepdims=True) / DI
        scale[...] = lax.rsqrt(mean + epsilon)

        def finish(n, carry):
            place = pl.ds(pl.multiple_of(n * CHUNK, CHUNK), CHUNK)
            factor = jnp.broadcast_to(scale[place, :], (CHUNK, LANES))
            for at in range(0, DI, LANES):
                part = gated[place, at : at + LANES] * factor * gain[:, at : at + LANES]
                normed[place, at : at + LANES] = part.astype(BF)
            return carry

        lax.fori_loop(0, tokens // CHUNK, finish, 0)
        half = DI // (2 * count)
        for k in range(count):
            other = pl.multiple_of((2 * k + 1 - meta[0]) * half, LANES)
            theirs[:, k * half : (k + 1) * half] = normed[:, pl.ds(other, half)]


def gate_forward(meta, x, mixed, gain, own, rest, local):
    tokens, width = x.shape
    count = UNITS
    part = width // count
    half = WIDES // 2
    tile_spec = pl.BlockSpec((tokens, WIDE), lambda i, meta: (0, own_tile(i, meta)))
    own_spec = pl.BlockSpec((WIDE, part), lambda i, meta: (jnp.minimum(i, half - 1), 0))
    rest_spec = pl.BlockSpec((WIDE, part), lambda i, meta: (jnp.maximum(i - half, 0), 0))
    local_spec = pl.BlockSpec(
        (WIDE, part), lambda i, meta: ((1 - meta[0]) * half + jnp.maximum(i - half, 0), 0)
    )
    return call(
        gate_body, "gate_forward", meta,
        (x, mixed, gain) + tuple(own) + (() if local is None else (local,)) + tuple(rest),
        [whole((tokens, width)), tile_spec, whole((1, DI))] + [own_spec] * count
        + [rest_spec if local is None else local_spec] + [rest_spec] * (count - 1),
        [
            shape_of((tokens, DI), BF), shape_of((tokens, DI), BF), shape_of((tokens, DI // 2), BF),
            shape_of((tokens, 1)),
        ],
        [tile_spec, whole((tokens, DI)), whole((tokens, DI // 2)), whole((tokens, 1))],
        [
            pltpu.VMEM((WIDE, width), BF), pltpu.VMEM((tokens, DI), F32),
            pltpu.VMEM((tokens, LANES), F32),
        ],
        WIDES, 2 * tokens * width * DI, 28 * MIB,
    )


def out_body(meta, *refs):
    count = UNITS
    normed, pulled, hidden = refs[0:2], refs[2], refs[3]
    block, back, total, weight, branch = refs[-5:]
    refs = refs[4:-5]
    many = len(refs) // 2
    sides = refs[:many], refs[many:]
    step = pl.program_id(0)
    tokens = pulled.shape[0]
    half = DI // (2 * count)

    @pl.when(step == 0)
    def _():
        total[...] = jnp.zeros_like(total)

    for j in range(count):
        @pl.when(step == j)
        def _(j=j):
            for side, parts in enumerate(sides):
                weight[side * half : (side + 1) * half, :] = parts[j][...]

    normed_both = jnp.concatenate([normed[0][...], normed[1][...]], axis=1)
    grads = dot_nt(pulled[...], weight[...]).astype(BF)
    more = dot(normed_both, weight[...])

    @pl.when(step == 0)
    def _():
        branch[...] = more

    @pl.when((step > 0) & (step < count - 1))
    def _():
        branch[...] += more

    for side in range(2):
        at = meta[OUT_TABLE + side * count + step] * half
        back[:, pl.ds(pl.multiple_of(at, LANES), half)] = grads[:, side * half : (side + 1) * half]
    for at in range(0, tokens, CHUNK):
        sums = None
        for lane in range(0, 2 * half, LANES):
            one = grads[at : at + CHUNK, lane : lane + LANES].astype(F32)
            one = one * normed_both[at : at + CHUNK, lane : lane + LANES].astype(F32)
            sums = one if sums is None else sums + one
        total[at : at + CHUNK, :] += sums

    @pl.when(step == count - 1)
    def _():
        for at in range(0, tokens, CHUNK):
            part = branch[at : at + CHUNK, :] + more[at : at + CHUNK, :]
            part = jnp.where(live_rows(meta, at, part.shape), part, 0.0)
            block[at : at + CHUNK, :] = (hidden[at : at + CHUNK, :].astype(F32) + part).astype(BF)


def out_forward(meta, normed, pulled, hidden, own, rest, local):
    tokens, width = hidden.shape
    count = UNITS
    half = DI // (2 * count)

    def columns(side):
        return pl.BlockSpec(
            (tokens, half), lambda i, meta: (0, meta[OUT_TABLE + side * count + i])
        )

    def local_spec(side):
        return pl.BlockSpec((half, width), lambda i, meta: (meta[0] if side == 0 else 1 - meta[0], 0))

    first = () if local is None else (local,)

    def weight_specs(side):
        if local is None:
            return [whole((half, width))] * count
        return [local_spec(side)] + [whole(part.shape) for part in own]

    return call(
        out_body, "out_forward", meta,
        (normed, normed, pulled, hidden) + (first + tuple(own) + first + tuple(rest)),
        [columns(0), columns(1), whole((tokens, width)), whole((tokens, width))]
        + weight_specs(0) + weight_specs(1),
        [shape_of((tokens, width), BF), shape_of((tokens, DI), BF), shape_of((tokens, LANES))],
        [whole((tokens, width)), whole((tokens, DI)), whole((tokens, LANES))],
        [pltpu.VMEM((2 * half, width), BF), pltpu.VMEM((tokens, width), F32)],
        count, 4 * tokens * width * DI, 24 * MIB,
    )


STEPS = 4


def norm_back_body(
    meta, back, total, mixed, gate, scale, gain, grad_gate, theirs, grad_mixed, grad_gain
):
    step = pl.program_id(0)
    tokens, width = back.shape
    grad_gain[...] = jnp.zeros_like(grad_gain)

    def one(n, carry):
        rows = pl.ds(pl.multiple_of(n * CHUNK, CHUNK), CHUNK)
        r = jnp.broadcast_to(scale[rows, :], (CHUNK, LANES))
        mean = jnp.sum(total[rows, :], axis=1, keepdims=True) / DI
        factor = r * r * mean
        for at in range(0, width, LANES):
            cut = slice(at, at + LANES)
            z = gate[rows, cut].astype(F32)
            sigma = sigmoid(z)
            silu = z * sigma
            out = mixed[rows, cut]
            gated = out * silu
            grad = back[rows, cut].astype(F32) * r
            grad_gain[:, cut] += fold(grad * gated)
            grad = grad * gain[:, cut] - gated * factor
            grad_mixed[rows, cut] = (grad * silu).astype(BF)
            grad_gate[rows, cut] = ((grad * out) * (sigma + silu * (1.0 - sigma))).astype(BF)
        return carry

    lax.fori_loop(0, tokens // CHUNK, one, 0)

    @pl.when(step // (STEPS // 2) == 1 - meta[0])
    def _():
        theirs[...] = grad_gate[...]


def norm_back(meta, back, total, mixed, gate, scale, gain):
    tokens = back.shape[0]
    width = DI // STEPS

    def tile(rows):
        return pl.BlockSpec((rows, width), lambda i, meta: (0, i))

    theirs_spec = pl.BlockSpec(
        (tokens, width),
        lambda i, meta: (0, jnp.clip(i - (1 - meta[0]) * (STEPS // 2), 0, STEPS // 2 - 1)),
    )
    return call(
        norm_back_body, "norm_back", meta, (back, total, mixed, gate, scale, gain),
        [tile(tokens), whole((tokens, LANES)), tile(tokens), tile(tokens), whole((tokens, 1)), tile(1)],
        [
            shape_of((tokens, DI), BF), shape_of((tokens, DI // 2), BF), shape_of((tokens, DI), BF),
            shape_of((8, DI)),
        ],
        [tile(tokens), theirs_spec, tile(tokens), tile(8)],
        [], STEPS, 10**9, 24 * MIB,
    )


def rows_product_body(meta, mine, theirs, pulled, pulled_rest, send, keep):
    total = dot_tn(mine[...], pulled[...]) + dot_tn(theirs[...], pulled_rest[...])
    total = total.astype(BF)
    sent = pl.num_programs(0) // 2

    @pl.when(pl.program_id(0) < sent)
    def _():
        send[0] = total

    @pl.when(pl.program_id(0) >= sent)
    def _():
        keep[0] = total


def rows_product(meta, normed, arrived, arrived_at, pulled, pulled_rest, units):
    tokens, width = pulled.shape
    unit = DI // (2 * UNITS)
    upper = units // 2

    def which(i):
        return lax.rem(i + upper, units)

    result = shape_of((upper, unit, width), BF)
    return call(
        rows_product_body, "rows_product", meta, (normed, arrived, pulled, pulled_rest),
        [
            pl.BlockSpec((tokens, unit), lambda i, meta: (0, meta[OUT_TABLE + which(i)])),
            pl.BlockSpec((tokens, unit), lambda i, meta: (0, meta[arrived_at + which(i)])),
            whole((tokens, width)), whole((tokens, width)),
        ],
        [result, result],
        [
            pl.BlockSpec((1, unit, width), lambda i, meta: (jnp.minimum(i, upper - 1), 0, 0)),
            pl.BlockSpec((1, unit, width), lambda i, meta: (jnp.maximum(i - upper, 0), 0, 0)),
        ],
        [], units, 4 * tokens * width * unit * units, 12 * MIB,
    )


def columns_product_body(plan, meta, *refs):
    parts = len(plan)
    mine, theirs = refs[:parts], refs[parts : 2 * parts]
    here, there, send, keep, right, right_rest = refs[2 * parts :]
    step = pl.program_id(0)
    width = here.shape[1] // UNITS

    @pl.when(step == 0)
    def _():
        for j in range(UNITS):
            lanes = pl.ds(pl.multiple_of(meta[TABLE + j] * width, LANES), width)
            right[:, j * width : (j + 1) * width] = here[:, lanes]
            right_rest[:, j * width : (j + 1) * width] = there[:, lanes]

    for (begin, steps), a, b in zip(plan, mine, theirs):
        @pl.when((step >= begin) & (step < begin + steps))
        def _(a=a, b=b):
            total = (dot_tn(a[...], right[...]) + dot_tn(b[...], right_rest[...])).astype(BF)
            for k in range(UNITS // 2):
                keep[k] = total[:, k * width : (k + 1) * width]
                other = UNITS // 2 + k
                send[k] = total[:, other * width : (other + 1) * width]


def columns_product(meta, parts, normed, normed_rest):
    tokens, width = normed.shape
    part = width // UNITS
    plan, step, mine_specs, theirs_specs = [], 0, [], []

    def spec(begin, steps, start):
        return pl.BlockSpec(
            (tokens, TILE), lambda i, meta: (0, start(meta) + jnp.clip(i - begin, 0, steps - 1))
        )

    for matrix, start, steps, arrived in parts:
        plan.append((step, steps))
        mine_specs.append(spec(step, steps, start))
        theirs_specs.append(spec(step, steps, lambda meta: 0))
        step += steps
    result = shape_of((UNITS // 2, step * TILE, part), BF)
    result_spec = pl.BlockSpec((UNITS // 2, TILE, part), lambda i, meta: (0, i, 0))
    return call(
        functools.partial(columns_product_body, tuple(plan)), "columns_product", meta,
        tuple(p[0] for p in parts) + tuple(p[3] for p in parts) + (normed, normed_rest),
        mine_specs + theirs_specs + [whole((tokens, width))] * 2,
        [result, result], [result_spec, result_spec],
        [pltpu.VMEM((tokens, width), BF), pltpu.VMEM((tokens, width), BF)],
        step, 1, 1,
    )


def conv_back(meta, masked, taps, result, sums, live, grad_conv):
    tokens = masked.shape[0]
    grad_conv[:, tokens:, :] = jnp.zeros((TILE // LANES, 8, LANES), F32)
    sums[...] = jnp.zeros_like(sums)
    for lane in range(0, TILE, LANES):
        cut = slice(lane, lane + LANES)
        totals = [jnp.zeros((8, LANES), F32) for _ in range(CONV + 1)]
        for at in range(0, tokens, CHUNK):
            near = [
                grad_conv[lane // LANES, at + 3 - k : at + 3 - k + CHUNK, :] for k in range(CONV)
            ]
            value = masked[at : at + CHUNK, cut].astype(F32)
            out = near[0] * taps[0:1, cut]
            for k in range(1, CONV):
                out = out + near[k] * taps[k : k + 1, cut]
            result[at : at + CHUNK, cut] = (out * live[at : at + CHUNK, :]).astype(BF)
            for k in range(CONV):
                totals[k] = totals[k] + fold(near[k] * value)
            totals[CONV] = totals[CONV] + fold(near[CONV - 1])
        for k in range(CONV + 1):
            sums[k : k + 1, cut] = jnp.sum(totals[k], axis=0, keepdims=True)


def fold(value):
    return jnp.sum(value.reshape(value.shape[0] // 8, 8, value.shape[1]), axis=0)


def scan_back_body(
    meta, content, keys, grad_out, mixed, entering, columns, rows, skip, masked, slope, taps,
    scores_in, write_in, read_in,
    result, theirs, sums, grad_columns, grad_scores, grad_write, grad_read,
    scores, read_rows, live, grad_conv, mixes, mix_grads, blocked, spread,
):
    half = SPAN // 2

    @pl.when(pl.program_id(0) == 0)
    def _():
        for span in range(2):
            at = span * SPAN
            scores[span] = dot_nt(keys[at : at + SPAN, :DSTATE], keys[at : at + SPAN, DSTATE:])
        read_rows[...] = keys[SPAN:, DSTATE:].astype(F32).T.astype(BF)
        grad_scores[...] = scores_in[...]
        grad_write[...] = write_in[...]
        grad_read[...] = read_in[...]
        mixes[...] = jnp.zeros_like(mixes)
        live_lanes(meta, live)
        after = row_ids(0, blocked.shape) <= lax.broadcasted_iota(jnp.int32, blocked.shape, 1)
        blocked[...] = jnp.where(after, 0.0, FAR)
        spread[...] = head_lanes(spread.shape, HEADDIM)

    def heads_sum(value):
        high = value.astype(BF)
        low = (value - high.astype(F32)).astype(BF)
        return dot_nt(high, spread[...]) + dot_nt(low, spread[...])

    for pair in range(PER // 2):
        lanes = slice(pair * 2 * HEADDIM, (pair + 1) * 2 * HEADDIM)
        ones = spread[2 * pair : 2 * pair + 2, lanes]
        for span in range(2):
            cut = slice(span * SPAN, (span + 1) * SPAN)
            mix_grads[pair, span] = dot_nt(heads_apart(content[cut, lanes], ones), grad_out[cut, lanes])

    factor = dot(columns[0, :, 2 * PER :].astype(BF), spread[...])
    grown = (grad_out[SPAN:, :].astype(F32) * factor[SPAN:]).astype(BF)
    grad_state = dot(read_rows[...], grown).astype(BF)
    grad_read[...] += dot_nt(grown, entering[0])
    worth = (content[0:SPAN, :].astype(F32) * factor[:SPAN]).astype(BF)
    grad_write[...] += dot_nt(worth, grad_state)
    from_state = dot(keys[0:SPAN, :DSTATE], grad_state) * factor[:SPAN]

    for pair in range(PER // 2):
        for h in range(2):
            n = 2 * pair + h
            for span in range(2):
                top = span * SPAN
                for at in range(0, SPAN, CHUNK):
                    less = columns[0, top + at : top + at + CHUNK, PER + n : PER + n + 1]
                    corner = at // half * half
                    for begin in range(corner, SPAN, half):
                        cut = slice(begin, begin + half)
                        decay = rows[0, n : n + 1, top + begin : top + begin + half] - less
                        if begin == corner:
                            decay = decay + blocked[at - begin : at - begin + CHUNK, :]
                        decay = jnp.exp2(decay)
                        row = h * SPAN + at
                        mix = scores[span, at : at + CHUNK, cut] * decay
                        mixes[pair, span, row : row + CHUNK, cut] = mix.astype(BF)
                        change = mix_grads[pair, span, row : row + CHUNK, cut] * decay
                        grad_scores[span, at : at + CHUNK, cut] += change

    lane = lax.broadcasted_iota(jnp.int32, (SPAN, 2 * PER), 1) < PER
    final = row_ids(0, lane.shape) == SPAN - 1
    skips = jnp.zeros((8, TILE), F32)
    for span in range(2):
        cut = slice(span * SPAN, (span + 1) * SPAN)
        value = content[cut, :].astype(F32)
        pull = grad_out[cut, :].astype(F32)
        both = []
        for pair in range(PER // 2):
            lanes = slice(pair * 2 * HEADDIM, (pair + 1) * 2 * HEADDIM)
            both.append(heads_together(dot(mixes[pair, span], grad_out[cut, lanes])))
        both = jnp.concatenate(both, axis=1)
        if span == 0:
            ended = jnp.sum(fold(value * from_state), axis=0, keepdims=True)
            both = both + from_state
        skipped = skip[...] * value
        skips = skips + fold(pull * value)
        written = heads_sum(value * both)
        read = heads_sum(pull * (mixed[cut, :] - skipped))
        if span == 0:
            ended = heads_sum(jnp.broadcast_to(ended, (8, TILE)))[0:1]
            read = read + jnp.where(final, ended, 0.0)
        grad_columns[0, cut, :] = jnp.where(lane, written, read)
        both = (both + skip[...] * pull) * slope[cut, :]
        for k in range(TILE // LANES):
            grad_conv[k, cut, :] = both[:, k * LANES : (k + 1) * LANES]

    conv_back(meta, masked, taps, result, sums, live, grad_conv)
    sums[5:6, :] = jnp.sum(skips, axis=0, keepdims=True)
    half_steps = pl.num_programs(0) // 2
    at_half = pl.program_id(0) // half_steps

    @pl.when(at_half == 1 - meta[0])
    def _():
        theirs[...] = result[...]


def scan_backward(
    meta, signal, keys, grad_out, mixed, entering, columns, rows, skip, masked, slope, taps, kept,
    first, count,
):
    tokens = signal.shape[0]

    def group(*shape):
        return pl.BlockSpec((1,) + shape, lambda i, meta: (i + first, 0, 0))

    def fresh(*shape):
        return pl.BlockSpec((1,) + shape, lambda i, meta: (i, 0, 0))

    kept_specs = [whole((2, SPAN, SPAN)), whole((SPAN, DSTATE)), whole((SPAN, DSTATE))]
    return call(
        scan_back_body, "scan_backward", meta,
        (signal, keys, grad_out, mixed, entering, columns, rows, skip, masked, slope, taps)
        + tuple(kept),
        [
            tiles(tokens, TILE, first), whole((tokens, TILE)),
            tiles(tokens, TILE, first), tiles(tokens, TILE, first), group(DSTATE, TILE),
            group(tokens, PACK),
            group(2 * PER, tokens), tiles(1, TILE, first), tiles(tokens, TILE, first),
            tiles(tokens, TILE, first), tiles(8, TILE, first),
        ]
        + kept_specs,
        [
            shape_of((tokens, count * TILE), BF), shape_of((tokens, count // 2 * TILE), BF),
            shape_of((8, count * TILE)),
            shape_of((count, tokens, 2 * PER)),
            shape_of((2, SPAN, SPAN)), shape_of((SPAN, DSTATE)), shape_of((SPAN, DSTATE)),
        ],
        [
            tiles(tokens, TILE),
            pl.BlockSpec(
                (tokens, TILE),
                lambda i, meta: (0, jnp.clip(i - (1 - meta[0]) * (count // 2), 0, count // 2 - 1)),
            ),
            tiles(8, TILE), fresh(tokens, 2 * PER),
        ]
        + kept_specs,
        [
            pltpu.VMEM((2, SPAN, SPAN), F32), pltpu.VMEM((DSTATE, SPAN), BF),
            pltpu.VMEM((tokens, LANES), F32), pltpu.VMEM((TILE // LANES, tokens + 8, LANES), F32),
            pltpu.VMEM((PER // 2, 2, 2 * SPAN, SPAN), BF),
            pltpu.VMEM((PER // 2, 2, 2 * SPAN, SPAN), F32),
            pltpu.VMEM((SPAN // 2, SPAN // 2), F32), pltpu.VMEM((2 * PER, TILE), BF),
        ],
        count, 3 * 10**9 * count, count * MIB,
    )


def tail_body(parts, meta, *refs):
    keys, masked, slope, taps, trio, steps, grad_scores, grad_write, grad_read = refs[:9]
    grad_columns = refs[9 : 9 + parts]
    result, sums, raw, small, packs, live, grad_conv = refs[9 + parts :]
    tokens = keys.shape[0]
    for span in range(2):
        at = span * SPAN
        write = keys[at : at + SPAN, :DSTATE]
        read = keys[at : at + SPAN, DSTATE:]
        to_write = fine_dot(grad_scores[span], read, dot)
        to_read = fine_dot(grad_scores[span], write, dot_tn)
        if span == 0:
            to_write = to_write + grad_write[...]
        else:
            to_read = to_read + grad_read[...]
        cut = slice(at, at + SPAN)
        grad_conv[0, cut, :] = to_write * slope[cut, :DSTATE]
        grad_conv[1, cut, :] = to_read * slope[cut, DSTATE:]
    live_lanes(meta, live)
    conv_back(meta, masked, taps, result, sums, live, grad_conv)

    blank = jnp.zeros((tokens, LANES - HEADS), F32)
    of_step, of_log = [], []
    for column_ref in grad_columns:
        for g in range(column_ref.shape[0]):
            of_step.append(column_ref[g, :, :PER])
            of_log.append(column_ref[g, :, PER:])
    grad_size = jnp.concatenate(of_step + [blank], axis=1)
    grad_log = jnp.concatenate(of_log + [blank], axis=1) - grad_size
    upper = row_ids(0, (SPAN, SPAN)) <= lax.broadcasted_iota(jnp.int32, (SPAN, SPAN), 1)
    upper = jnp.where(upper, 1.0, 0.0).astype(BF)
    rates = []
    for at in range(0, tokens, SPAN):
        high, middle, low = pieces(grad_log[at : at + SPAN])
        rates.append(dot(upper, high) + (dot(upper, middle) + dot(upper, low)))
    grad_rate = jnp.concatenate(rates, axis=0)
    decay_rate = steps[1:2, :]
    sigma = jax.nn.sigmoid(trio[0])
    size = trio[1]
    tiny = size > 0.0
    share = jnp.where(tiny, sigma / jnp.where(tiny, size, 1.0), 1.0)
    grad_raw = grad_size * share + grad_rate * decay_rate * sigma
    raw[...] = grad_raw.astype(BF)
    small[...] = jnp.zeros_like(small)
    small[0:1, :] = jnp.sum(grad_raw, axis=0, keepdims=True)
    small[1:2, :] = jnp.sum(grad_rate * trio[1], axis=0, keepdims=True) * decay_rate
    for side in range(2):
        at = meta[0] if side == 0 else 1 - meta[0]
        packs[side, :, :LANES] = result[:, pl.ds(pl.multiple_of(at * LANES, LANES), LANES)]
        packs[side, :, LANES:] = raw[...]


def tail_backward(meta, keys, masked, slope, taps, trio, steps, kept, grad_columns):
    tokens = keys.shape[0]
    last = DI // TILE
    key_spec = whole((tokens, TILE))
    return call(
        functools.partial(tail_body, len(grad_columns)), "tail_backward", meta,
        (keys, masked, slope, taps, trio, steps) + tuple(kept) + tuple(grad_columns),
        [
            key_spec, key_spec, key_spec, pl.BlockSpec((8, TILE), lambda i, meta: (0, last)),
            whole((3, tokens, LANES)), whole((8, LANES)), whole((2, SPAN, SPAN)),
            whole((SPAN, DSTATE)), whole((SPAN, DSTATE)),
        ]
        + [whole(part.shape) for part in grad_columns],
        [
            shape_of((tokens, TILE), BF), shape_of((8, TILE)), shape_of((tokens, LANES), BF),
            shape_of((8, LANES)), shape_of((2, tokens, TILE), BF),
        ],
        [
            whole((tokens, TILE)), whole((8, TILE)), whole((tokens, LANES)), whole((8, LANES)),
            whole((2, tokens, TILE)),
        ],
        [pltpu.VMEM((tokens, LANES), F32), pltpu.VMEM((TILE // LANES, tokens + 8, LANES), F32)],
        1, 1, 1,
    )


def input_body(plan, first, last, meta, *refs):
    count = UNITS
    grads = refs[: len(plan)]
    refs = refs[len(plan) :]
    if not first:
        start, refs = refs[0], refs[1:]
    blocks = []
    for begin, steps, half in plan:
        own, refs = refs[:count], refs[count:]
        rest = None
        if half is not None:
            rest, refs = refs[:count], refs[count:]
        blocks.append((own, rest))
    step = pl.program_id(0)

    if last:
        hidden, out_grad, scale, gain, result, gain_grad, weight, weight_dt, total, folded = refs
    else:
        total, weight = refs

    @pl.when(step == 0)
    def _():
        total[...] = jnp.zeros_like(total) if first else start[...]

    for n, (begin, steps, half) in enumerate(plan):
        @pl.when((step >= begin) & (step < begin + steps))
        def _(n=n, half=half):
            own, rest = blocks[n]
            rows = own[0].shape[0]
            if grads[n].shape[1] == LANES:
                weight_dt[...] = jnp.zeros_like(weight_dt)
                gather_lanes(weight_dt, own, meta, TABLE)
                total[...] += dot(grads[n][...], weight_dt[...])
                return
            if half is None:
                gather_lanes(weight, own, meta, TABLE)
            else:
                @pl.when(meta[0] == half)
                def _():
                    gather_lanes(weight, own, meta, TABLE)

                @pl.when(meta[0] != half)
                def _():
                    gather_lanes(weight, rest, meta, TABLE + count)

            total[...] += dot(grads[n][...], weight[0:rows, :])

    if not last:
        return

    @pl.when(step == pl.num_programs(0) - 1)
    def _():
        tokens, width = hidden.shape
        folded[...] = jnp.zeros_like(folded)

        def finish(n, carry):
            rows = pl.ds(pl.multiple_of(n * 32, 32), 32)
            r = jnp.broadcast_to(scale[rows, :], (32, LANES))
            sums = jnp.zeros((32, LANES), F32)
            for at in range(0, width, LANES):
                cut = slice(at, at + LANES)
                both = total[rows, cut] * hidden[rows, cut].astype(F32)
                folded[:, cut] += fold(both * r)
                sums = sums + both * gain[:, cut]
            mean = jnp.sum(sums, axis=1, keepdims=True) / width
            factor = r * r * r * mean
            for at in range(0, width, LANES):
                cut = slice(at, at + LANES)
                value = r * (total[rows, cut] * gain[:, cut]) - hidden[rows, cut].astype(F32) * factor
                result[rows, cut] = value + out_grad[rows, cut].astype(F32)
            return carry

        lax.fori_loop(0, tokens // 32, finish, 0)
        gain_grad[...] = jnp.sum(folded[...], axis=0, keepdims=True)


def input_backward(meta, start, parts, tokens, width, last=None):
    part = width // UNITS
    plan, step, grad_specs, block_specs, grads, blocks = [], 0, [], [], [], []

    def grad_spec(columns, begin, steps, first):
        return pl.BlockSpec(
            (tokens, columns), lambda i, meta: (0, first + jnp.clip(i - begin, 0, steps - 1))
        )

    def row_spec(rows, begin, steps, first, when):
        def index(i, meta):
            at = first + jnp.clip(i - begin, 0, steps - 1)
            return (at if when is None else jnp.where(when(meta), at, first), 0)

        return pl.BlockSpec((rows, part), index)

    def is_half(half):
        return lambda meta: meta[0] == half

    def not_half(half):
        return lambda meta: meta[0] != half

    for grad, grad_first, steps, half, own, own_first, rest, rest_first, local_first in parts:
        columns = WIDE if half is not None else grad.shape[1]
        row_tile = 64 if columns == LANES else columns
        plan.append((step, steps, half))
        grads.append(grad)
        grad_specs.append(grad_spec(columns, step, steps, grad_first))
        when = None if half is None else is_half(half)
        for matrix in own:
            blocks.append(matrix)
            block_specs.append(row_spec(row_tile, step, steps, own_first, when))
        if half is not None:
            for j, matrix in enumerate(rest):
                blocks.append(matrix)
                row = local_first if j == 0 else rest_first
                block_specs.append(row_spec(row_tile, step, steps, row, not_half(half)))
        step += steps
    more, more_specs = (), []
    outs, out_specs = [shape_of((tokens, width))], [whole((tokens, width))]
    scratch = [pltpu.VMEM((WIDE, width), BF)]
    if last is not None:
        more = tuple(last)
        more_specs = [whole((tokens, width))] * 2 + [whole((tokens, 1)), whole((1, width))]
        outs.append(shape_of((1, width)))
        out_specs.append(whole((1, width)))
        scratch += [
            pltpu.VMEM((LANES, width), BF), pltpu.VMEM((tokens, width), F32),
            pltpu.VMEM((8, width), F32),
        ]
    first = start is None
    return call(
        functools.partial(input_body, tuple(plan), first, last is not None),
        "input_backward", meta,
        tuple(grads) + (() if first else (start,)) + tuple(blocks) + more,
        grad_specs + ([] if first else [whole((tokens, width))]) + block_specs + more_specs,
        outs, out_specs, scratch,
        step, 10**10 if last is None else 10**11, 20 * MIB,
    )


def place_body(halves, last, meta, own, other, out):
    step = pl.program_id(0)

    def put(which, row, rows, at):
        @pl.when(meta[0] == which)
        def _():
            out[at : at + rows, :] = own[row : row + rows, :].astype(F32)

        @pl.when(meta[0] != which)
        def _():
            out[at : at + rows, :] = other[row : row + rows, :].astype(F32)

    for half in range(2):
        @pl.when(step == half)
        def _(half=half):
            put(half, 0, halves, 0)

    if last:
        @pl.when(step == 2)
        def _():
            put(0, halves, LANES, 0)
            put(1, halves, LANES, LANES)
            put(0, halves + LANES, LANES, 2 * LANES)


def place_rows(meta, own, other, halves, first, total, filled, last):
    length, width = own.shape
    return call(
        functools.partial(place_body, halves, last), "place_rows", meta, (own, other),
        [whole((length, width)), whole((length, width))],
        shape_of((total, width)),
        pl.BlockSpec((halves, width), lambda i, meta: (first + i, 0)),
        [], 3 if last else 2, 1, 1, None if filled is None else {0: filled},
    )


NEAR = 8


def mirrored(j, count):
    if count != 4:
        return j
    result, bit, other = 0, 1, count // 2
    while bit < count:
        if j & bit:
            result |= other
        bit, other = bit * 2, other // 2
    return result


def hop(x, bit):
    reps, count = lax.axis_size("rep"), lax.axis_size("shard")
    pairs = []
    for r in range(reps):
        flip = bit if r % 2 == 0 else mirrored(bit, count)
        pairs += [(r * count + s, r * count + (s ^ flip)) for s in range(count)]
    return lax.ppermute(x, ("rep", "shard"), pairs)


def swap(x):
    return lax.ppermute(x, "rep", [(r, r ^ 1) for r in range(lax.axis_size("rep"))])


def across(x, bit):
    return lax.ppermute(x, "shard", [(s, s ^ bit) for s in range(lax.axis_size("shard"))])


def along(x, pairs):
    return lax.ppermute(x, "rep", [(2 * a + k, 2 * b + k) for a, b in pairs for k in range(2)])


def settle(keep, arrived):
    middle = keep.shape[0] // 2
    if middle == 0:
        return None, keep.astype(F32) + arrived.astype(F32)
    held = (keep.astype(F32) + arrived.astype(F32)).astype(BF)
    return held[middle:], held[:middle]


def finish_stages(send, keep):
    while send is not None:
        send, keep = settle(keep, hop(send, send.shape[0]))
    return keep[0]


def inward(held):
    if lax.axis_size("rep") // 2 != 4:
        return held, None
    return held, along(held.astype(BF), [(0, 1), (3, 2)])


def middle(state):
    held, arrived = state
    if arrived is None:
        return held, None
    inner = (held + arrived.astype(F32)).astype(BF)
    return inner, along(inner, [(1, 2), (2, 1)])


def outward(state):
    inner, arrived = state
    if arrived is None:
        chips = lax.axis_size("rep") // 2
        total, bit = inner.astype(BF), 1
        while bit < chips:
            more = along(total, [(k, k ^ bit) for k in range(chips)])
            total = (total.astype(F32) + more.astype(F32)).astype(BF)
            bit *= 2
        return total, None
    total = (inner.astype(F32) + arrived.astype(F32)).astype(BF)
    return total, along(total, [(1, 0), (2, 3)])


def summed(state):
    total, arrived = state
    if arrived is None:
        return total
    place = lax.axis_index("rep") // 2
    return jnp.where((place == 1) | (place == 2), total, arrived)


def in_order(own, other, core):
    return [jnp.where(core == 0, own, other), jnp.where(core == 0, other, own)]


def hold(values):
    leaves, tree = jax.tree.flatten(values)
    return jax.tree.unflatten(tree, lax.optimization_barrier(tuple(leaves)))


def add_up(rows):
    while len(rows) > 1:
        rows = [a + b for a, b in zip(rows[::2], rows[1::2])]
    return rows[0]


def group_rows(vector, shard, count):
    rows = [lax.dynamic_slice_in_dim(vector, shard ^ j, 1, 0) for j in range(count)]
    return rows[:1] + [across(row, j) for j, row in enumerate(rows) if j]


def chips_sum(row):
    chips = lax.axis_size("rep") // 2
    return add_up(
        [row] + [along(row, [(k, k ^ d) for k in range(chips)]) for d in range(1, chips)]
    )


def join_lanes(blocks, shard):
    return [
        jnp.concatenate(in_order(blocks[j], blocks[j + 1], shard % 2), axis=1)
        for j in range(0, len(blocks), 2)
    ]


def split_lanes(units, shard):
    half = units.shape[2] // 2
    pairs = in_order(units[:, :, :half], units[:, :, half:], shard % 2)
    return jnp.stack(pairs, axis=1).reshape(2 * units.shape[0], units.shape[1], half)


def pad_lanes(matrix):
    return jnp.pad(matrix, ((0, 0), (0, LANES - matrix.shape[1])))


def shards(
    hidden,
    out_grad,
    norm_gain,
    in_w,
    conv_w,
    conv_b,
    dt_bias,
    a_log,
    skip,
    out_gain,
    out_w,
    lengths,
    offsets,
):
    core = lax.axis_index("rep") % 2
    shard = lax.axis_index("shard")
    count = lax.axis_size("shard")
    tokens, width = hidden.shape
    bits = []
    while 2 ** len(bits) < count:
        bits.append(2 ** len(bits))

    local = in_w.T
    half = DI // 2
    piece = jnp.concatenate(
        [
            lax.dynamic_slice_in_dim(local, DI + core * half, half, 0),
            local[2 * DI :],
            jnp.zeros((16, local.shape[1]), BF),
        ],
        axis=0,
    )
    gate_piece = lax.dynamic_slice_in_dim(local, core * half, half, 0)
    out_piece = lax.dynamic_slice_in_dim(out_w, core * (out_w.shape[0] // 2), out_w.shape[0] // 2, 0)

    def spread(first):
        blocks = [first]
        for bit in bits:
            blocks = blocks + [hop(block, bit) for block in blocks]
        return blocks

    paired = count == 4
    small = (norm_gain, conv_w.T, conv_b, dt_bias, a_log, skip, out_gain)
    packed = jnp.concatenate([part.reshape(-1) for part in small])
    everyone = [packed] + [
        lax.ppermute(
            packed, ("rep", "shard"),
            [
                (r * count + s, r * count + (s ^ (j if r % 2 == 0 else mirrored(j, count))))
                for r in range(lax.axis_size("rep"))
                for s in range(count)
            ],
        )
        for j in range(1, count)
    ]
    piece, everyone = hold((piece, everyone))
    everyone = jnp.stack(everyone).astype(F32)
    order = [jnp.where(core == 0, j, mirrored(j, count)) for j in range(count)]
    whose = jnp.stack(order)[jnp.arange(count) ^ shard]
    same = (whose[:, None] == jnp.arange(count)[None]).astype(F32)
    everyone = jnp.sum(same[:, :, None] * everyone[None], axis=1)
    parts, start = [], 0
    for part in small:
        cut = everyone[:, start : start + part.size].reshape((count,) + part.shape)
        cut = jnp.moveaxis(cut, 0, -2)
        parts.append(cut.reshape(part.shape[:-1] + (-1,)))
        start += part.size
    conv_own = spread(piece)
    gate_piece, conv_own = hold((gate_piece, conv_own))
    if paired:
        conv_rest = [swap(block) for block in conv_own[1:]]
        gate_near = hop(gate_piece, 1), hop(gate_piece, 2)
        out_local, in_local = out_w, local
    else:
        gate_own = spread(gate_piece)
        out_piece, gate_own = hold((out_piece, gate_own))
        out_own = spread(out_piece)
        conv_rest = rest_conv = join_lanes([swap(block) for block in conv_own], shard)
        gate_rest = rest_gate = join_lanes([swap(block) for block in gate_own], shard)
        conv_own, gate_own = join_lanes(conv_own, shard), join_lanes(gate_own, shard)
        out_full = [jnp.concatenate(in_order(block, swap(block), core), axis=0) for block in out_own]
        out_one, out_two = out_full[:UNITS], out_full[UNITS:]
        out_local = in_local = None

    gain_one, kernel, bias_conv, bias_step, log_rate, skip_full, gain_two = parts
    decay_rate = -jnp.exp(log_rate)

    mine = order
    other = [jnp.where(core == 0, mirrored(j, count), j) for j in range(count)]
    mine, other = [shard ^ j for j in mine], [shard ^ j for j in other]
    if paired:
        out_units = [2 * j + core for j in mine] + [2 * j + 1 - core for j in other]
    else:
        out_units = mine
        mine = other = [j // 2 for j in mine[::2]]
    meta = jnp.stack(
        [core, offsets[0], lengths[0], shard] + mine + other + out_units
    ).astype(jnp.int32)
    taps = jnp.concatenate([kernel, bias_conv[None], jnp.zeros((3, CC), F32)], axis=0)
    steps = jnp.concatenate(
        [pad_lanes(jnp.stack([bias_step, decay_rate])), jnp.zeros((6, LANES), F32)], axis=0
    )
    skip_lanes = jnp.repeat(skip_full, HEADDIM)[None]

    positions = jnp.arange(tokens, dtype=jnp.int32)
    live_mask = ((positions >= offsets[0]) & (positions < offsets[0] + lengths[0])).astype(F32)
    hidden_full = hidden.astype(F32)
    inv_rms = lax.rsqrt(jnp.mean(hidden_full * hidden_full, axis=1, keepdims=True) + epsilon)
    normed = (hidden_full * inv_rms * gain_one).astype(BF)
    pulled = (out_grad.astype(F32) * live_mask[:, None]).astype(BF)
    normed_rest = swap(normed)
    pulled_rest = swap(pulled)

    (masked, signal, slope, masked_keys, keys, slope_keys, columns, rows, trio) = conv_forward(
        meta, normed, taps, steps, conv_own, conv_rest, in_local
    )
    if paired:
        gate_near, signal = hold((gate_near, signal))
        gate_own = [gate_piece, *gate_near, hop(gate_near[0], 2)]
    mixed, entering = scan_forward(meta, signal, keys, columns, rows, skip_lanes)
    if paired:
        out_piece, gate_far, mixed = hold((out_piece, gate_own[3], mixed))
        gate_own[3] = gate_far
        gate_rest = [swap(block) for block in gate_own[1:]]
        rest_conv, rest_gate = [local] + conv_rest, [local] + gate_rest
        out_near = hop(out_piece, 1), hop(out_piece, 2)
    gate, normed_out, out_theirs, scale = gate_forward(
        meta, normed, mixed, gain_two[None], gate_own, gate_rest, in_local
    )
    out_arrived = swap(out_theirs if paired else normed_out)
    if paired:
        out_near, normed_out = hold((out_near, normed_out))
        out_one = [*out_near, hop(out_near[0], 2)]
        out_two = [swap(block) for block in out_one]

    upper = count // 2
    out_pulls = (pulled, pulled_rest)
    if not paired:
        cut = core * (width // 2)
        out_pulls = [lax.dynamic_slice_in_dim(x, cut, width // 2, 1) for x in out_pulls]

    def product(parts):
        send, keep = columns_product(meta, parts, normed, normed_rest)
        return (send, keep) if paired else (split_lanes(send, shard), split_lanes(keep, shard))

    out_send, out_keep = rows_product(
        meta, normed_out, out_arrived, TABLE if paired else OUT_TABLE, *out_pulls, count
    )
    out_send, out_keep, normed_out = hold((out_send, out_keep, normed_out))
    out_there = hop(out_send, upper)
    block_out, back, total = out_forward(
        meta, normed_out, pulled, hidden, out_one, out_two, out_local
    )
    out_there, total = hold((out_there, total))
    out_send, out_keep = settle(out_keep, out_there)
    out_there = hop(out_send, upper // 2)
    out_keep, total = hold((out_keep, total))
    grad_gate, gate_theirs, grad_mixed, grad_gain_two = norm_back(
        meta, back, total, mixed, gate, scale, gain_two[None]
    )

    gate_theirs, out_there = hold((gate_theirs, out_there))
    gate_arrived = swap(gate_theirs)
    out_line = inward(finish_stages(*settle(out_keep, out_there)))
    out_held, gate_arrived = hold((out_line[0], gate_arrived))
    gate_parts = [(grad_gate, lambda meta: meta[0] * (GROUPS // 2), GROUPS // 2, gate_arrived)]
    gate_send, gate_keep = product(gate_parts)
    gate_send, gate_keep, grad_mixed = hold((gate_send, gate_keep, grad_mixed))
    gate_there = hop(gate_send, upper)
    kept = (
        jnp.zeros((2, SPAN, SPAN), F32),
        jnp.zeros((SPAN, DSTATE), F32),
        jnp.zeros((SPAN, DSTATE), F32),
    )
    near, far = NEAR, GROUPS - NEAR
    part = WIDES // 2
    over = near * TILE // WIDE - part

    def gate_part(half):
        at = half * part
        return [(grad_gate, at, part, half, gate_own, 0, rest_gate, 0, at if paired else 0)]

    def conv_part(grad, grad_first, steps, half, first):
        local_first = WIDES + half * part + first if paired else first
        return [(grad, grad_first, steps, half, conv_own, first, rest_conv, first, local_first)]

    grad_near, near_theirs, sums_near, columns_near, *kept = scan_backward(
        meta, signal, keys, grad_mixed, mixed, entering, columns, rows, skip_lanes, masked, slope, taps,
        kept, 0, near,
    )
    gate_there, near_theirs, out_arrived = hold((gate_there, near_theirs, out_line[1]))
    near_arrived = swap(near_theirs)
    gate_send, gate_keep = settle(gate_keep, gate_there)
    gate_there = hop(gate_send, upper // 2)
    gate_keep, out_arrived = hold((gate_keep, out_arrived))
    out_line = middle((out_held, out_arrived))
    near_arrived, gate_keep, out_inner = hold((near_arrived, gate_keep, out_line[0]))
    near_parts = [(grad_near, lambda meta: meta[0] * (near // 2), near // 2, near_arrived)]
    near_send, near_keep = product(near_parts)
    near_there = hop(near_send, upper)
    near_keep, kept, grad_mixed = hold((near_keep, kept, grad_mixed))
    grad_far, far_theirs, sums_far, columns_far, *kept = scan_backward(
        meta, signal, keys, grad_mixed, mixed, entering, columns, rows, skip_lanes, masked, slope, taps,
        kept, near, far,
    )
    far_theirs, gate_there = hold((far_theirs, gate_there))
    far_arrived = swap(far_theirs)
    gate_line = inward(finish_stages(*settle(gate_keep, gate_there)))
    gate_held, kept = hold((gate_line[0], kept))
    grad_keys, sums_keys, grad_raw, grad_steps, packs = tail_backward(
        meta, keys, masked_keys, slope_keys, taps, trio, steps, kept, (columns_near, columns_far),
    )
    packs, near_there = hold((packs, near_there))
    packs_arrived = swap(packs[1])
    near_send, near_keep = settle(near_keep, near_there)
    near_there = hop(near_send, upper // 2)
    packs, packs_arrived, near_keep = hold((packs, packs_arrived, near_keep))
    far_parts = [
        (grad_far, lambda meta: meta[0] * (far // 2), far // 2, far_arrived),
        (packs[0], lambda meta: 0, 1, packs_arrived),
    ]
    far_send, far_keep = product(far_parts)
    far_there = hop(far_send, upper)
    far_keep, gate_arrived, near_there, out_arrived = hold(
        (far_keep, gate_line[1], near_there, out_line[1])
    )
    gate_line = middle((gate_held, gate_arrived))
    near_line = inward(finish_stages(*settle(near_keep, near_there)))
    out_line = outward((out_inner, out_arrived))
    gate_inner, near_held, out_done, grad_gate = hold(
        (gate_line[0], near_line[0], out_line[0], grad_gate)
    )
    (partial,) = input_backward(meta, None, gate_part(0) + gate_part(1), tokens, width)
    partial, far_there = hold((partial, far_there))
    far_send, far_keep = settle(far_keep, far_there)
    far_there = hop(far_send, upper // 2)
    far_keep, near_arrived, small_grads = hold(
        (far_keep, near_line[1], (sums_near, sums_far, sums_keys, grad_steps, grad_gain_two))
    )
    sums_near, sums_far, sums_keys, grad_steps, grad_gain_two = small_grads
    sums = jnp.concatenate([sums_near, sums_far, sums_keys], axis=1)
    grads = (
        sums[:CONV].reshape(CONV, count, -1).transpose(1, 0, 2).reshape(count, -1),
        sums[CONV].reshape(count, -1),
        grad_steps[0, :HEADS].reshape(count, -1),
        grad_steps[1, :HEADS].reshape(count, -1),
        jnp.sum(sums[5, :DI].reshape(HEADS, HEADDIM), axis=1).reshape(count, -1),
        jnp.sum(grad_gain_two, axis=0).reshape(count, -1),
    )
    vector = jnp.concatenate(grads, axis=1)
    far_there, far_keep, partial, vector = hold((far_there, far_keep, partial, vector))
    vector_there = swap(vector)
    far_line = inward(finish_stages(*settle(far_keep, far_there)))
    far_held, gate_arrived, out_arrived = hold((far_line[0], gate_line[1], out_line[1]))
    gate_line = outward((gate_inner, gate_arrived))
    near_line = middle((near_held, near_arrived))
    out_total = summed((out_done, out_arrived))
    out_other = swap(out_total)
    far_held, gate_done, near_inner, out_total, partial = hold(
        (far_held, gate_line[0], near_line[0], out_total, partial)
    )
    (partial,) = input_backward(
        meta, partial,
        conv_part(grad_near, 0, part, 0, 0)
        + conv_part(grad_near, part, over, 1, 0)
        + conv_part(grad_far, 0, part - over, 1, over),
        tokens, width,
    )
    partial, far_arrived = hold((partial, far_line[1]))
    far_line = middle((far_held, far_arrived))
    far_inner, near_arrived, gate_arrived, out_other, vector_there = hold(
        (far_line[0], near_line[1], gate_line[1], out_other, vector_there)
    )
    spread_rows = group_rows(vector + vector_there, shard, count)
    near_line = outward((near_inner, near_arrived))
    gate_total = summed((gate_done, gate_arrived))
    gate_other = swap(gate_total)
    far_inner, near_done, gate_total, partial = hold((far_inner, near_line[0], gate_total, partial))
    hidden_grad, grad_gain_one = input_backward(
        meta, partial,
        [
            (grad_keys, 0, 1, None, conv_own, DI // 2 // TILE, None, 0, 0),
            (grad_raw, 0, 1, None, conv_own, (DI // 2 + TILE) // 64, None, 0, 0),
        ],
        tokens, width, (hidden, out_grad, inv_rms, gain_one[None]),
    )
    grad_gain_one, far_arrived, gate_other, spread_rows, near_arrived = hold(
        (grad_gain_one, far_line[1], gate_other, spread_rows, near_line[1])
    )
    far_line = outward((far_inner, far_arrived))
    row = chips_sum(add_up(spread_rows))[0]
    far_done, grad_gain_one, gate_other = hold((far_line[0], grad_gain_one, gate_other))
    vector = grad_gain_one[0].reshape(count, -1)
    gain_row = add_up(group_rows(vector + swap(vector), shard, count))
    all_rows = local.shape[0]
    rows_so_far = place_rows(meta, gate_total, gate_other, DI // 2, 0, all_rows, None, False)
    gain_row, row, far_arrived, rows_so_far = hold((gain_row, row, far_line[1], rows_so_far))
    gain_row = chips_sum(gain_row)[0]
    far_total = summed((far_done, far_arrived))
    far_other = swap(far_total)
    near_total = summed((near_done, near_arrived))
    near_other = swap(near_total)
    wide = near // 2 * TILE
    rows_so_far = place_rows(
        meta, near_total, near_other, wide, DI // wide, all_rows, rows_so_far, False
    )
    wide = far // 2 * TILE
    rows_so_far = place_rows(
        meta, far_total, far_other, wide, (DI + near * TILE) // wide, all_rows, rows_so_far, True
    )
    in_w_grad = rows_so_far.T

    out_w_grad = jnp.concatenate(
        in_order(out_total, out_other, core), axis=0 if paired else 1
    ).astype(F32)
    found, start = [], 0
    for part in grads:
        found.append(row[start : start + part.shape[1]])
        start += part.shape[1]
    return (
        block_out,
        hidden_grad,
        gain_row,
        in_w_grad,
        found[0].reshape(CONV, -1).T,
        found[1],
        found[2],
        found[3],
        found[4],
        found[5],
        out_w_grad,
    )


def solution(mesh):
    return jax.shard_map(
        shards,
        mesh=mesh,
        in_specs=(
            P(("rep", "shard"), None),
            P(("rep", "shard"), None),
            P("shard"),
            P("shard", None),
            P("shard", None),
            P("shard"),
            P("shard"),
            P("shard"),
            P("shard"),
            P("shard"),
            P("shard", None),
            P(("rep", "shard")),
            P(("rep", "shard")),
        ),
        out_specs=(
            P(("rep", "shard"), None),
            P(("rep", "shard"), None),
            P("shard"),
            P("shard", None),
            P("shard", None),
            P("shard"),
            P("shard"),
            P("shard"),
            P("shard"),
            P("shard"),
            P("shard", None),
        ),
        check_vma=False,
    )
```

profile of v0, /device:TPU:0, one launch (start us, length us, event | category | flops | bytes accessed | tf_op | source)
XLA Modules:
  0.0 477.4 jit_solution(13022625158044991445)
XLA Ops:
  1.4 4.1 concatenate.29
  5.6 2.9 collective-permute-start
  11.0 2.9 dynamic-slice_bitcast_fusion
  14.6 1.8 collective-permute-start.3
  20.7 25.6 %collective-permute-done.3.refs_1_.refs_9_.refs_13_.refs_5_.refs_21_.refs_4_.refs_8_ = bf16[1856,384]{1,0:T(8,128)(2,1)S(1)} collective-permute-done((bf16[1856,384]{1,0:T(8,128)(2,1)S(1)}, bf16[1856,384]{1,0:T(8,128)(2,1)S(1)}, u32[]{:S(2)}, u32[]{:S(2)}) %collective-permute-start.3) | collective-permute-done | bytes 1425440 | tf_op jit(solution)/shard_map/ppermute | solution.py:1127
  46.3 3.3 collective-permute-start.5
  49.6 1.8 fusion
  52.4 14.2 %collective-permute-done.5.refs_3_.refs_11_.refs_15_.refs_7_.refs_23_.refs_6_.refs_10_ = bf16[1856,384]{1,0:T(8,128)(2,1)} collective-permute-done((bf16[1856,384]{1,0:T(8,128)(2,1)S(1)}, bf16[1856,384]{1,0:T(8,128)(2,1)}, u32[]{:S(2)}, u32[]{:S(2)}) %collective-permute-start.5) | collective-permute-done | bytes 1425440 | tf_op jit(solution)/shard_map/ppermute | solution.py:1127
  69.1 2.0 collective-permute-start.7
  72.0 3.0 fusion.2.x.refs_2_.refs_4_
  76.1 24.4 %conv_forward.1 = (bf16[512,3072]{1,0:T(8,128)(2,1)}, bf16[512,3072]{1,0:T(8,128)(2,1)}, f32[512,3072]{1,0:T(8,128)}, bf16[512,256]{1,0:T(8,128)(2,1)}, bf16[512...) custom-call(s32[20]{0:T(128)} %stack.90.meta, ...), custom_call_target="tpu_custom_call" | custom-call | flops 5234491392 | bytes 25165824 | tf_op jit(solution)/shard_map/conv_forward/pallas_call | solution.py:91
  100.7 2.3 constant_dynamic-slice_fusion.8
  104.4 15.7 %scan_forward.1 = (f32[512,3072]{1,0:T(8,128)}, bf16[12,128,256]{2,1,0:T(8,128)(2,1)}) custom-call(s32[20]{0:T(128)} %stack.90.meta, bf16[512,3072]{1,0:T(8,128)(2,1)} %get-tuple-element.186.content, bf16[512,256]{1,0:T(8,128)(2,1)} %get-tuple-element.187.keys.refs_0_, f32[12,512,16]{2,1,0:T(8,128)} %get-tuple-element.188.columns, ...), custom_call_target="tpu_custom_call" | custom-call | flops 10000000000 | bytes 12582912 | tf_op jit(solution)/shard_map/scan_forward/pallas_call | solution.py:91
  124.5 17.1 %gate_forward.1 = (bf16[512,3072]{1,0:T(8,128)(2,1)}, bf16[512,3072]{1,0:T(8,128)(2,1)}, bf16[512,1536]{1,0:T(8,128)(2,1)}, f32[512,1]{1,0:T(8,128)}) custom-call(s32[20]{0:T(128)} %stack.90.meta, bf16[512,1536]{1,0:T(8,128)(2,1)} %fusion.2.x.refs_2_.refs_4_, f32[512,3072]{1,0:T(8,128)} %get-tuple-element.192.mixed, f32[1,3072]{1,0:T(1,128)} %bitcast.76, ...), custom_call_target="tpu_custom_call" | custom-call | flops 4831838208 | bytes 29360128 | tf_op jit(solution)/shard_map/gate_forward/pallas_call | solution.py:91
  141.7 8.7 %collective-permute-done.12.refs_5_ = bf16[384,1536]{1,0:T(8,128)(2,1)} collective-permute-done((bf16[384,1536]{1,0:T(8,128)(2,1)}, bf16[384,1536]{1,0:T(8,128)(2,1)}, u32[]{:S(2)}, u32[]{:S(2)}) %collective-permute-start.12) | collective-permute-done | bytes 1179680 | tf_op jit(solution)/shard_map/ppermute | solution.py:1127
  150.4 1.8 collective-permute-start.19
  153.3 10.5 %rows_product.1 = (bf16[2,384,1536]{2,1,0:T(8,128)(2,1)}, bf16[2,384,1536]{2,1,0:T(8,128)(2,1)}) custom-call(s32[20]{0:T(128)} %stack.90.meta, bf16[512,3072]{1,0:T(8,128)(2,1)} %get-tuple-element.200.mine.refs_0_.refs_1_, bf16[512,1536]{1,0:T(8,128)(2,1)} %collective-permute-done.17.theirs, bf16[512,1536]{1,0:T(8,128)(2,1)} %copy-done.11, ...), custom_call_target="tpu_custom_call" | custom-call | flops 4831838208 | bytes 12582912 | tf_op jit(solution)/shard_map/rows_product/pallas_call | solution.py:91
  164.6 2.3 collective-permute-done.19.refs_7_
  167.2 1.7 collective-permute-done.21.refs_10_
  170.7 21.7 %out_forward.1 = (bf16[512,1536]{1,0:T(8,128)(2,1)}, bf16[512,3072]{1,0:T(8,128)(2,1)}, f32[512,128]{1,0:T(8,128)}) custom-call(s32[20]{0:T(128)} %stack.90.meta, bf16[512,3072]{1,0:T(8,128)(2,1)} %get-tuple-element.200.mine.refs_0_.refs_1_, bf16[512,3072]{1,0:T(8,128)(2,1)} %get-tuple-element.200.mine.refs_0_.refs_1_, bf16[512,1536]{1,0:T(8,128)(2,1)} %copy-done.11, ...), custom_call_target="tpu_custom_call" | custom-call | flops 9663676416 | bytes 25165824 | tf_op jit(solution)/shard_map/out_forward/pallas_call | solution.py:91
  193.0 2.3 add_convert_fusion.1
  198.0 12.1 %norm_back.1 = (bf16[512,3072]{1,0:T(8,128)(2,1)}, bf16[512,1536]{1,0:T(8,128)(2,1)}, bf16[512,3072]{1,0:T(8,128)(2,1)}, f32[8,3072]{1,0:T(8,128)}) custom-call(s32[20]{0:T(128)} %stack.90.meta, bf16[512,3072]{1,0:T(8,128)(2,1)} %get-tuple-element.207.back, f32[512,128]{1,0:T(8,128)} %get-tuple-element.213.total, f32[512,3072]{1,0:T(8,128)} %get-tuple-element.192.mixed, ...), custom_call_target="tpu_custom_call" | custom-call | flops 1000000000 | bytes 25165824 | tf_op jit(solution)/shard_map/norm_back/pallas_call | solution.py:91
  210.1 2.6 collective-permute-done.24
  214.2 3.8 fusion.13
  221.7 10.7 %columns_product.3 = (bf16[2,1536,384]{2,1,0:T(8,128)(2,1)}, bf16[2,1536,384]{2,1,0:T(8,128)(2,1)}) custom-call(s32[20]{0:T(128)} %stack.90.meta, bf16[512,3072]{1,0:T(8,128)(2,1)} %get-tuple-element.278.refs_0_.refs_1_, bf16[512,1536]{1,0:T(8,128)(2,1)} %copy-done.12, bf16[512,1536]{1,0:T(8,128)(2,1)} %fusion.2.x.refs_2_.refs_4_, bf16[512,1536]{1,0:T(8,128)(2,1)} %copy-done.4), custom_call_target="tpu_custom_call" | custom-call | flops 1 | bytes 1 | tf_op jit(solution)/shard_map/columns_product/pallas_call | solution.py:91
  233.7 3.5 collective-permute-start.28
  238.7 22.5 %scan_backward.2 = (bf16[512,2048]{1,0:T(8,128)(2,1)}, bf16[512,1024]{1,0:T(8,128)(2,1)}, f32[8,2048]{1,0:T(8,128)}, f32[8,512,8]{2,1,0:T(8,128)}, f32[2,256,256...) custom-call(s32[20]{0:T(128)} %stack.90.meta, bf16[512,3072]{1,0:T(8,128)(2,1)} %get-tuple-element.186.content, ...), custom_call_target="tpu_custom_call" | custom-call | flops 24000000000 | bytes 8388608 | tf_op jit(solution)/shard_map/scan_backward/pallas_call | solution.py:91
  261.3 1.9 collective-permute-done.28
  264.2 2.2 add_convert_fusion
  269.2 1.7 collective-permute-start.36
  270.9 8.8 %columns_product.4 = (bf16[2,1024,384]{2,1,0:T(8,128)(2,1)}, bf16[2,1024,384]{2,1,0:T(8,128)(2,1)}) custom-call(s32[20]{0:T(128)} %stack.90.meta, bf16[512,2048]{1,0:T(8,128)(2,1)} %get-tuple-element.239.refs_0_.refs_1_, bf16[512,1024]{1,0:T(8,128)(2,1)} %collective-permute-done.29.refs_1_, bf16[512,1536]{1,0:T(8,128)(2,1)} %fusion.2.x.refs_2_.refs_4_, ...), custom_call_target="tpu_custom_call" | custom-call | flops 1 | bytes 1 | tf_op jit(solution)/shard_map/columns_product/pallas_call | solution.py:91
  280.5 13.1 %scan_backward.3 = (bf16[512,1024]{1,0:T(8,128)(2,1)}, bf16[512,512]{1,0:T(8,128)(2,1)}, f32[8,1024]{1,0:T(8,128)}, f32[4,512,8]{2,1,0:T(8,128)}, f32[2,256,256]...) custom-call(s32[20]{0:T(128)} %stack.90.meta, bf16[512,3072]{1,0:T(8,128)(2,1)} %get-tuple-element.186.content, ...), custom_call_target="tpu_custom_call" | custom-call | flops 12000000000 | bytes 4194304 | tf_op jit(solution)/shard_map/scan_backward/pallas_call | solution.py:91
  294.7 2.9 fusion.14
  297.6 7.2 %collective-permute-start.34 = (bf16[1536,384]{1,0:T(8,128)(2,1)}, bf16[1536,384]{1,0:T(8,128)(2,1)}, u32[]{:S(2)}, u32[]{:S(2)}) collective-permute-start(bf16[1536,384]{1,0:T(8,128)(2,1)} %get-tuple-element.343), channel_id=1, source_target_pairs={{0,8},{4,12},{24,16},{28,20},{1,9},{5,13},{25,17},{29,21},{2,10},{... | collective-permute-start | bytes 3538952 | tf_op jit(solution)/shard_map/ppermute | solution.py:1139
  304.8 6.6 %tail_backward.1 = (bf16[512,256]{1,0:T(8,128)(2,1)}, f32[8,256]{1,0:T(8,128)}, bf16[512,128]{1,0:T(8,128)(2,1)}, f32[8,128]{1,0:T(8,128)}, bf16[2,512,256]{2,1,0:T(8,128)(2,1)}) custom-call(s32[20]{0:T(128)} %stack.90.meta, bf16[512,256]{1,0:T(8,128)(2,1)} %get-tuple-element.187.keys.refs_0_, bf16[512,256]{1,0:T(8,128)(2,1)} %get-tuple-element.204.refs_1_, ...), custom_call_target="tpu_custom_call" | custom-call | flops 1 | bytes 1 | tf_op jit(solution)/shard_map/tail_backward/pallas_call | solution.py:91
  311.3 2.3 add_convert_fusion.2
  318.6 1.7 slice_bitcast_fusion.refs_1_
  320.3 7.2 %columns_product.5 = (bf16[2,768,384]{2,1,0:T(8,128)(2,1)}, bf16[2,768,384]{2,1,0:T(8,128)(2,1)}) custom-call(s32[20]{0:T(128)} %stack.90.meta, bf16[512,1024]{1,0:T(8,128)(2,1)} %get-tuple-element.261.refs_0_.refs_2_, bf16[512,256]{1,0:T(8,128)(2,1)} %slice_bitcast_fusion.refs_1_, bf16[512,512]{1,0:T(8,128)(2,1)} %collective-permute-done.33.refs_2_, ...), custom_call_target="tpu_custom_call" | custom-call | flops 1 | bytes 1 | tf_op jit(solution)/shard_map/columns_product/pallas_call | solution.py:91
  328.8 2.6 add_convert_fusion.6
  332.2 2.6 add_convert_fusion.5
  336.0 2.3 fusion.12
  338.3 7.0 %collective-permute-start.39 = (bf16[1024,384]{1,0:T(8,128)(2,1)}, bf16[1024,384]{1,0:T(8,128)(2,1)}, u32[]{:S(2)}, u32[]{:S(2)}) collective-permute-start(bf16[1024,384]{1,0:T(8,128)(2,1)} %get-tuple-element.351), channel_id=1, source_target_pairs={{0,8},{4,12},{24,16},{28,20},{1,9},{5,13},{25,17},{29,21},{2,10},{... | collective-permute-start | bytes 2359304 | tf_op jit(solution)/shard_map/ppermute | solution.py:1139
  345.3 15.0 %input_backward.3.refs_3_ = f32[512,1536]{1,0:T(8,128)} custom-call(s32[20]{0:T(128)} %stack.90.meta, bf16[512,3072]{1,0:T(8,128)(2,1)} %get-tuple-element.278.refs_0_.refs_1_, bf16[512,3072]{1,0:T(8,128)(2,1)} %get-tuple-element.278.refs_0_.refs_1_, bf16[1536,384]{1,0:T(8,128)(2,1)} %get-tuple-element.175.refs_0_.refs_2_.refs_10_, ...), custom_call_target="tpu_custom_call" | custom-call | flops 10000000000 | bytes 20971520 | tf_op jit(solution)/shard_map/input_backward/pallas_call | solution.py:91
  360.4 1.9 add_convert_fusion.4
  363.2 1.7 collective-permute-start.38
  369.2 2.2 add_convert_fusion.9
  371.3 1.6 collective-permute-start.43
  373.7 2.0 fusion.11
  380.2 6.4 %collective-permute-start.42 = (bf16[768,384]{1,0:T(8,128)(2,1)}, bf16[768,384]{1,0:T(8,128)(2,1)}, u32[]{:S(2)}, u32[]{:S(2)}) collective-permute-start(bf16[768,384]{1,0:T(8,128)(2,1)} %get-tuple-element.355), channel_id=1, source_target_pairs={{0,8},{4,12},{24,16},{28,20},{1,9},{5,13},{25,17},{29,21},{2,10},{... | collective-permute-start | bytes 1769480 | tf_op jit(solution)/shard_map/ppermute | solution.py:1139
  386.8 17.3 %input_backward.4.refs_2_ = f32[512,1536]{1,0:T(8,128)} custom-call(s32[20]{0:T(128)} %stack.90.meta, bf16[512,2048]{1,0:T(8,128)(2,1)} %get-tuple-element.239.refs_0_.refs_1_, bf16[512,2048]{1,0:T(8,128)(2,1)} %get-tuple-element.239.refs_0_.refs_1_, bf16[512,1024]{1,0:T(8,128)(2,1)} %get-tuple-element.261.refs_0_.refs_2_, ...), custom_call_target="tpu_custom_call" | custom-call | flops 10000000000 | bytes 20971520 | tf_op jit(solution)/shard_map/input_backward/pallas_call | solution.py:91
  404.1 2.0 add_convert_fusion.11
  406.8 2.5 broadcast_select_fusion.2.own
  409.6 2.4 add_convert_fusion.8
  416.3 9.7 %input_backward.5 = (f32[512,1536]{1,0:T(8,128)}, f32[1,1536]{1,0:T(1,128)}) custom-call(s32[20]{0:T(128)} %stack.90.meta, bf16[512,256]{1,0:T(8,128)(2,1)} %get-tuple-element.259.refs_0_, bf16[512,128]{1,0:T(8,128)(2,1)} %get-tuple-element.260.refs_1_, f32[512,1536]{1,0:T(8,128)} %input_backward.4.refs_2_, bf16[1856,384]{1,0:T(8,128)(2,1)} %copy-done, ...), custom_call_target="tpu_custom_call" | custom-call | flops 99999997952 | bytes 20971520 | tf_op jit(solution)/shard_map/input_backward/pallas_call | solution.py:91
  429.6 1.9 collective-permute-done.51
  431.5 2.4 collective-permute-done.52
  433.9 2.0 add_convert_fusion.10
  438.4 4.5 collective-permute-start.58
  447.7 4.7 place_rows.3.refs_2_
  453.8 4.1 collective-permute-done.59
  458.0 2.0 broadcast_select_fusion.5.refs_0_
  460.0 2.8 maximum_convert_fusion
  469.6 3.8 place_rows.4.refs_2_
  473.4 3.7 place_rows.5
  (264 shorter events, 82.3 us)
Async XLA Ops:
  5.6 8.8 %collective-permute-start = (bf16[5348]{0:T(1024)(128)(2,1)S(1)}, bf16[5348]{0:T(1024)(128)(2,1)S(1)}, u32[]{:S(2)}, u32[]{:S(2)}) collective-permute-start(bf16[5348]{0:T(1024)(128)(2,1)S(1)} %concatenate.29), channel_id=1, source_target_pairs={{0,1},{1,0},{2,3},{3,2},{4,6},{5,7},{6,4},{7,5},{8,9},{9,8},{10,11... | collective-permute-start | bytes 32096 | tf_op jit(solution)/shard_map/ppermute | solution.py:1282
  8.5 5.9 %collective-permute-start.1 = (bf16[5348]{0:T(1024)(128)(2,1)S(1)}, bf16[5348]{0:T(1024)(128)(2,1)S(1)}, u32[]{:S(2)}, u32[]{:S(2)}) collective-permute-start(bf16[5348]{0:T(1024)(128)(2,1)S(1)} %concatenate.29), channel_id=1, source_target_pairs={{0,2},{1,3},{2,0},{3,1},{4,5},{5,4},{6,7},{7,6},{8,10},{9,11},{10,... | collective-permute-start | bytes 32096 | tf_op jit(solution)/shard_map/ppermute | solution.py:1282
  10.0 4.6 collective-permute-start.2
  14.6 31.7 %collective-permute-start.3 = (bf16[1856,384]{1,0:T(8,128)(2,1)S(1)}, bf16[1856,384]{1,0:T(8,128)(2,1)S(1)}, u32[]{:S(2)}, u32[]{:S(2)}) collective-permute-start(bf16[1856,384]{1,0:T(8,128)(2,1)S(1)} %maximum_maximum_fusion.refs_0_.refs_8_.refs_12_.refs_4_.refs_20_.refs_3_.refs_7_), channel_id=1, source_target_pairs={{0,1},{1,0},{2,3},{3,2},{4,6},{5,7},{6,4},{7,5},{8,9},{9,8},{10,11... | collective-permute-start | bytes 4276232 | tf_op jit(solution)/shard_map/ppermute | solution.py:1127
  19.2 33.2 %collective-permute-start.4 = (bf16[1856,384]{1,0:T(8,128)(2,1)S(1)}, bf16[1856,384]{1,0:T(8,128)(2,1)}, u32[]{:S(2)}, u32[]{:S(2)}) collective-permute-start(bf16[1856,384]{1,0:T(8,128)(2,1)S(1)} %maximum_maximum_fusion.refs_0_.refs_8_.refs_12_.refs_4_.refs_20_.refs_3_.refs_7_), channel_id=1, source_target_pairs={{0,2},{1,3},{2,0},{3,1},{4,5},{5,4},{6,7},{7,6},{8,10},{9,11},{10,... | collective-permute-start | bytes 4276232 | tf_op jit(solution)/shard_map/ppermute | solution.py:1127
  46.3 20.2 %collective-permute-start.5 = (bf16[1856,384]{1,0:T(8,128)(2,1)S(1)}, bf16[1856,384]{1,0:T(8,128)(2,1)}, u32[]{:S(2)}, u32[]{:S(2)}) collective-permute-start(bf16[1856,384]{1,0:T(8,128)(2,1)S(1)} %collective-permute-done.3.refs_1_.refs_9_.refs_13_.refs_5_.refs_21_.refs_4_.refs_8_), channel_id=1, source_target_pairs={{0,2},{1,3},{2,0},{3,1},{4,5},{5,4},{6,7},{7,6},{8,10},{9,11},{10,... | collective-permute-start | bytes 4276232 | tf_op jit(solution)/shard_map/ppermute | solution.py:1127
  66.6 8.4 %collective-permute-start.8 = (bf16[1856,384]{1,0:T(8,128)(2,1)S(1)}, bf16[1856,384]{1,0:T(8,128)(2,1)S(1)}, u32[]{:S(2)}, u32[]{:S(2)}) collective-permute-start(bf16[1856,384]{1,0:T(8,128)(2,1)S(1)} %collective-permute-done.3.refs_1_.refs_9_.refs_13_.refs_5_.refs_21_.refs_4_.refs_8_), channel_id=1, source_target_pairs={{0,4},{4,0},{8,12},{12,8},{16,20},{20,16},{24,28},{28,24},{1,5},{5... | collective-permute-start | bytes 4276232 | tf_op jit(solution)/shard_map/ppermute | solution.py:1131
  66.6 8.4 %collective-permute-start.9 = (bf16[1856,384]{1,0:T(8,128)(2,1)}, bf16[1856,384]{1,0:T(8,128)(2,1)}, u32[]{:S(2)}, u32[]{:S(2)}) collective-permute-start(bf16[1856,384]{1,0:T(8,128)(2,1)} %collective-permute-done.4.refs_2_.refs_10_.refs_14_.refs_6_.refs_22_.refs_5_.refs_9_), channel_id=1, source_target_pairs={{0,4},{4,0},{8,12},{12,8},{16,20},{20,16},{24,28},{28,24},{1,5},{5... | collective-permute-start | bytes 4276232 | tf_op jit(solution)/shard_map/ppermute | solution.py:1131
  67.1 7.9 %collective-permute-start.10 = (bf16[1856,384]{1,0:T(8,128)(2,1)}, bf16[1856,384]{1,0:T(8,128)(2,1)}, u32[]{:S(2)}, u32[]{:S(2)}) collective-permute-start(bf16[1856,384]{1,0:T(8,128)(2,1)} %collective-permute-done.5.refs_3_.refs_11_.refs_15_.refs_7_.refs_23_.refs_6_.refs_10_), channel_id=1, source_target_pairs={{0,4},{4,0},{8,12},{12,8},{16,20},{20,16},{24,28},{28,24},{1,5},{5... | collective-permute-start | bytes 4276232 | tf_op jit(solution)/shard_map/ppermute | solution.py:1131
  67.8 32.7 %collective-permute-start.6 = (bf16[1536,384]{1,0:T(8,128)(2,1)}, bf16[1536,384]{1,0:T(8,128)(2,1)}, u32[]{:S(2)}, u32[]{:S(2)}) collective-permute-start(bf16[1536,384]{1,0:T(8,128)(2,1)} %get-tuple-element.175.refs_0_.refs_2_.refs_10_), channel_id=1, source_target_pairs={{0,1},{1,0},{2,3},{3,2},{4,6},{5,7},{6,4},{7,5},{8,9},{9,8},{10,11... | collective-permute-start | bytes 3538952 | tf_op jit(solution)/shard_map/ppermute | solution.py:1127
  69.1 31.4 %collective-permute-start.7 = (bf16[1536,384]{1,0:T(8,128)(2,1)}, bf16[1536,384]{1,0:T(8,128)(2,1)}, u32[]{:S(2)}, u32[]{:S(2)}) collective-permute-start(bf16[1536,384]{1,0:T(8,128)(2,1)} %get-tuple-element.175.refs_0_.refs_2_.refs_10_), channel_id=1, source_target_pairs={{0,2},{1,3},{2,0},{3,1},{4,5},{5,4},{6,7},{7,6},{8,10},{9,11},{10,... | collective-permute-start | bytes 3538952 | tf_op jit(solution)/shard_map/ppermute | solution.py:1127
  100.6 19.6 %collective-permute-start.11 = (bf16[1536,384]{1,0:T(8,128)(2,1)}, bf16[1536,384]{1,0:T(8,128)(2,1)}, u32[]{:S(2)}, u32[]{:S(2)}) collective-permute-start(bf16[1536,384]{1,0:T(8,128)(2,1)} %collective-permute-done.6.refs_1_.refs_3_.refs_11_), channel_id=1, source_target_pairs={{0,2},{1,3},{2,0},{3,1},{4,5},{5,4},{6,7},{7,6},{8,10},{9,11},{10,... | collective-permute-start | bytes 3538952 | tf_op jit(solution)/shard_map/ppermute | solution.py:1127
  103.9 19.3 %collective-permute-start.14 = (bf16[1536,384]{1,0:T(8,128)(2,1)}, bf16[1536,384]{1,0:T(8,128)(2,1)}, u32[]{:S(2)}, u32[]{:S(2)}) collective-permute-start(bf16[1536,384]{1,0:T(8,128)(2,1)} %collective-permute-done.6.refs_1_.refs_3_.refs_11_), channel_id=1, source_target_pairs={{0,4},{4,0},{8,12},{12,8},{16,20},{20,16},{24,28},{28,24},{1,5},{5... | collective-permute-start | bytes 3538952 | tf_op jit(solution)/shard_map/ppermute | solution.py:1131
  104.2 20.3 %collective-permute-start.15 = (bf16[1536,384]{1,0:T(8,128)(2,1)}, bf16[1536,384]{1,0:T(8,128)(2,1)}, u32[]{:S(2)}, u32[]{:S(2)}) collective-permute-start(bf16[1536,384]{1,0:T(8,128)(2,1)} %collective-permute-done.7.refs_2_.refs_4_.refs_12_), channel_id=1, source_target_pairs={{0,4},{4,0},{8,12},{12,8},{16,20},{20,16},{24,28},{28,24},{1,5},{5... | collective-permute-start | bytes 3538952 | tf_op jit(solution)/shard_map/ppermute | solution.py:1131
  120.1 4.3 collective-permute-start.16
  120.8 31.4 %collective-permute-start.18 = (bf16[512,1536]{1,0:T(8,128)(2,1)S(1)}, bf16[512,1536]{1,0:T(8,128)(2,1)S(1)}, u32[]{:S(2)}, u32[]{:S(2)}) collective-permute-start(bf16[512,1536]{1,0:T(8,128)(2,1)S(1)} %multiply_convert_fusion.pulled.refs_2_), channel_id=1, source_target_pairs={{0,4},{4,0},{8,12},{12,8},{16,20},{20,16},{24,28},{28,24},{1,5},{5... | collective-permute-start | bytes 4718600 | tf_op jit(solution)/shard_map/ppermute | solution.py:1131
  121.9 28.4 %collective-permute-start.12 = (bf16[384,1536]{1,0:T(8,128)(2,1)}, bf16[384,1536]{1,0:T(8,128)(2,1)}, u32[]{:S(2)}, u32[]{:S(2)}) collective-permute-start(bf16[384,1536]{1,0:T(8,128)(2,1)} %constant_dynamic-slice_fusion.8), channel_id=1, source_target_pairs={{0,1},{1,0},{2,3},{3,2},{4,6},{5,7},{6,4},{7,5},{8,9},{9,8},{10,11... | collective-permute-start | bytes 3538952 | tf_op jit(solution)/shard_map/ppermute | solution.py:1127
  123.3 27.1 %collective-permute-start.13 = (bf16[384,1536]{1,0:T(8,128)(2,1)}, bf16[384,1536]{1,0:T(8,128)(2,1)}, u32[]{:S(2)}, u32[]{:S(2)}) collective-permute-start(bf16[384,1536]{1,0:T(8,128)(2,1)} %constant_dynamic-slice_fusion.8), channel_id=1, source_target_pairs={{0,2},{1,3},{2,0},{3,1},{4,5},{5,4},{6,7},{7,6},{8,10},{9,11},{10,... | collective-permute-start | bytes 3538952 | tf_op jit(solution)/shard_map/ppermute | solution.py:1127
  141.6 10.6 %collective-permute-start.17 = (bf16[512,1536]{1,0:T(8,128)(2,1)}, bf16[512,1536]{1,0:T(8,128)(2,1)}, u32[]{:S(2)}, u32[]{:S(2)}) collective-permute-start(bf16[512,1536]{1,0:T(8,128)(2,1)} %get-tuple-element.197), channel_id=1, source_target_pairs={{0,4},{4,0},{8,12},{12,8},{16,20},{20,16},{24,28},{28,24},{1,5},{5... | collective-permute-start | bytes 4718600 | tf_op jit(solution)/shard_map/ppermute | solution.py:1131
  150.4 16.5 %collective-permute-start.19 = (bf16[384,1536]{1,0:T(8,128)(2,1)}, bf16[384,1536]{1,0:T(8,128)(2,1)}, u32[]{:S(2)}, u32[]{:S(2)}) collective-permute-start(bf16[384,1536]{1,0:T(8,128)(2,1)} %collective-permute-done.12.refs_5_), channel_id=1, source_target_pairs={{0,2},{1,3},{2,0},{3,1},{4,5},{5,4},{6,7},{7,6},{8,10},{9,11},{10,... | collective-permute-start | bytes 3538952 | tf_op jit(solution)/shard_map/ppermute | solution.py:1127
  163.8 29.2 %collective-permute-start.23 = (bf16[2,384,1536]{2,1,0:T(8,128)(2,1)}, bf16[2,384,1536]{2,1,0:T(8,128)(2,1)}, u32[]{:S(2)}, u32[]{:S(2)}) collective-permute-start(bf16[2,384,1536]{2,1,0:T(8,128)(2,1)} %get-tuple-element.209), channel_id=1, source_target_pairs={{0,2},{1,3},{2,0},{3,1},{4,5},{5,4},{6,7},{7,6},{8,10},{9,11},{10,... | collective-permute-start | bytes 7077896 | tf_op jit(solution)/shard_map/ppermute | solution.py:1127
  164.1 4.7 collective-permute-start.21
  166.9 3.8 collective-permute-start.22
  196.4 16.2 %collective-permute-start.24 = (bf16[1,384,1536]{2,1,0:T(8,128)(2,1)S(1)}, bf16[1,384,1536]{2,1,0:T(8,128)(2,1)S(1)}, u32[]{:S(2)}, u32[]{:S(2)}) collective-permute-start(bf16[1,384,1536]{2,1,0:T(8,128)(2,1)S(1)} %get-tuple-element.349), channel_id=1, source_target_pairs={{0,1},{1,0},{2,3},{3,2},{4,6},{5,7},{6,4},{7,5},{8,9},{9,8},{10,11... | collective-permute-start | bytes 3538952 | tf_op jit(solution)/shard_map/ppermute | solution.py:1127
  213.7 5.8 %collective-permute-start.25 = (bf16[512,1536]{1,0:T(8,128)(2,1)}, bf16[512,1536]{1,0:T(8,128)(2,1)S(1)}, u32[]{:S(2)}, u32[]{:S(2)}) collective-permute-start(bf16[512,1536]{1,0:T(8,128)(2,1)} %get-tuple-element.220), channel_id=1, source_target_pairs={{0,4},{4,0},{8,12},{12,8},{16,20},{20,16},{24,28},{28,24},{1,5},{5... | collective-permute-start | bytes 4718600 | tf_op jit(solution)/shard_map/ppermute | solution.py:1131
  213.7 5.8 %collective-permute-start.26 = (bf16[512,1536]{1,0:T(8,128)(2,1)S(1)}, bf16[512,1536]{1,0:T(8,128)(2,1)S(1)}, u32[]{:S(2)}, u32[]{:S(2)}) collective-permute-start(bf16[512,1536]{1,0:T(8,128)(2,1)S(1)} %copy-done.1), channel_id=1, source_target_pairs={{0,4},{4,0},{8,12},{12,8},{16,20},{20,16},{24,28},{28,24},{1,5},{5... | collective-permute-start | bytes 4718600 | tf_op jit(solution)/shard_map/ppermute | solution.py:1131
  232.5 30.7 %collective-permute-start.27 = (bf16[2,1536,384]{2,1,0:T(8,128)(2,1)}, bf16[2,1536,384]{2,1,0:T(8,128)(2,1)}, u32[]{:S(2)}, u32[]{:S(2)}) collective-permute-start(bf16[2,1536,384]{2,1,0:T(8,128)(2,1)} %get-tuple-element.225), channel_id=1, source_target_pairs={{0,2},{1,3},{2,0},{3,1},{4,5},{5,4},{6,7},{7,6},{8,10},{9,11},{10,... | collective-permute-start | bytes 7077896 | tf_op jit(solution)/shard_map/ppermute | solution.py:1127
  233.7 29.5 %collective-permute-start.28 = (bf16[384,1536]{1,0:T(8,128)(2,1)}, bf16[384,1536]{1,0:T(8,128)(2,1)S(1)}, u32[]{:S(2)}, u32[]{:S(2)}) collective-permute-start(bf16[384,1536]{1,0:T(8,128)(2,1)} %get-tuple-element.347), channel_id=1, source_target_pairs={{0,8},{4,12},{24,16},{28,20},{1,9},{5,13},{25,17},{29,21},{2,10},{... | collective-permute-start | bytes 3538952 | tf_op jit(solution)/shard_map/ppermute | solution.py:1139
  263.2 7.7 %collective-permute-start.29 = (bf16[512,1024]{1,0:T(8,128)(2,1)}, bf16[512,1024]{1,0:T(8,128)(2,1)}, u32[]{:S(2)}, u32[]{:S(2)}) collective-permute-start(bf16[512,1024]{1,0:T(8,128)(2,1)} %get-tuple-element.231), channel_id=1, source_target_pairs={{0,4},{4,0},{8,12},{12,8},{16,20},{20,16},{24,28},{28,24},{1,5},{5... | collective-permute-start | bytes 3145736 | tf_op jit(solution)/shard_map/ppermute | solution.py:1131
  267.8 25.9 %collective-permute-start.30 = (bf16[1,1536,384]{2,1,0:T(8,128)(2,1)S(1)}, bf16[1,1536,384]{2,1,0:T(8,128)(2,1)S(1)}, u32[]{:S(2)}, u32[]{:S(2)}) collective-permute-start(bf16[1,1536,384]{2,1,0:T(8,128)(2,1)S(1)} %get-tuple-element.345), channel_id=1, source_target_pairs={{0,1},{1,0},{2,3},{3,2},{4,6},{5,7},{6,4},{7,5},{8,9},{9,8},{10,11... | collective-permute-start | bytes 3538952 | tf_op jit(solution)/shard_map/ppermute | solution.py:1127
  269.2 59.5 %collective-permute-start.36 = (bf16[384,1536]{1,0:T(8,128)(2,1)S(1)}, bf16[384,1536]{1,0:T(8,128)(2,1)}, u32[]{:S(2)}, u32[]{:S(2)}) collective-permute-start(bf16[384,1536]{1,0:T(8,128)(2,1)S(1)} %add_convert_fusion.7), channel_id=1, source_target_pairs={{8,16},{12,20},{16,8},{20,12},{9,17},{13,21},{17,9},{21,13},{10,18... | collective-permute-start | bytes 3538952 | tf_op jit(solution)/shard_map/ppermute | solution.py:1139
  279.7 31.6 %collective-permute-start.31 = (bf16[2,1024,384]{2,1,0:T(8,128)(2,1)}, bf16[2,1024,384]{2,1,0:T(8,128)(2,1)}, u32[]{:S(2)}, u32[]{:S(2)}) collective-permute-start(bf16[2,1024,384]{2,1,0:T(8,128)(2,1)} %get-tuple-element.263), channel_id=1, source_target_pairs={{0,2},{1,3},{2,0},{3,1},{4,5},{5,4},{6,7},{7,6},{8,10},{9,11},{10,... | collective-permute-start | bytes 4718600 | tf_op jit(solution)/shard_map/ppermute | solution.py:1127
  297.6 31.2 %collective-permute-start.34 = (bf16[1536,384]{1,0:T(8,128)(2,1)}, bf16[1536,384]{1,0:T(8,128)(2,1)}, u32[]{:S(2)}, u32[]{:S(2)}) collective-permute-start(bf16[1536,384]{1,0:T(8,128)(2,1)} %get-tuple-element.343), channel_id=1, source_target_pairs={{0,8},{4,12},{24,16},{28,20},{1,9},{5,13},{25,17},{29,21},{2,10},{... | collective-permute-start | bytes 3538952 | tf_op jit(solution)/shard_map/ppermute | solution.py:1139
  315.0 13.8 %collective-permute-start.35 = (bf16[1,1024,384]{2,1,0:T(8,128)(2,1)}, bf16[1,1024,384]{2,1,0:T(8,128)(2,1)}, u32[]{:S(2)}, u32[]{:S(2)}) collective-permute-start(bf16[1,1024,384]{2,1,0:T(8,128)(2,1)} %get-tuple-element.353), channel_id=1, source_target_pairs={{0,1},{1,0},{2,3},{3,2},{4,6},{5,7},{6,4},{7,5},{8,9},{9,8},{10,11... | collective-permute-start | bytes 2359304 | tf_op jit(solution)/shard_map/ppermute | solution.py:1127
  315.9 4.4 collective-permute-start.33
  327.5 32.8 %collective-permute-start.37 = (bf16[2,768,384]{2,1,0:T(8,128)(2,1)}, bf16[2,768,384]{2,1,0:T(8,128)(2,1)}, u32[]{:S(2)}, u32[]{:S(2)}) collective-permute-start(bf16[2,768,384]{2,1,0:T(8,128)(2,1)} %get-tuple-element.279), channel_id=1, source_target_pairs={{0,2},{1,3},{2,0},{3,1},{4,5},{5,4},{6,7},{7,6},{8,10},{9,11},{10,... | collective-permute-start | bytes 3538952 | tf_op jit(solution)/shard_map/ppermute | solution.py:1127
  331.3 44.4 %collective-permute-start.40 = (bf16[1536,384]{1,0:T(8,128)(2,1)}, bf16[1536,384]{1,0:T(8,128)(2,1)S(1)}, u32[]{:S(2)}, u32[]{:S(2)}) collective-permute-start(bf16[1536,384]{1,0:T(8,128)(2,1)} %add_convert_fusion.6), channel_id=1, source_target_pairs={{8,16},{12,20},{16,8},{20,12},{9,17},{13,21},{17,9},{21,13},{10,18... | collective-permute-start | bytes 3538952 | tf_op jit(solution)/shard_map/ppermute | solution.py:1139
  334.8 40.9 %collective-permute-start.41 = (bf16[384,1536]{1,0:T(8,128)(2,1)}, bf16[384,1536]{1,0:T(8,128)(2,1)}, u32[]{:S(2)}, u32[]{:S(2)}) collective-permute-start(bf16[384,1536]{1,0:T(8,128)(2,1)} %add_convert_fusion.5), channel_id=1, source_target_pairs={{8,0},{12,4},{16,24},{20,28},{9,1},{13,5},{17,25},{21,29},{10,2},{... | collective-permute-start | bytes 3538952 | tf_op jit(solution)/shard_map/ppermute | solution.py:1139
  338.3 26.6 %collective-permute-start.39 = (bf16[1024,384]{1,0:T(8,128)(2,1)}, bf16[1024,384]{1,0:T(8,128)(2,1)}, u32[]{:S(2)}, u32[]{:S(2)}) collective-permute-start(bf16[1024,384]{1,0:T(8,128)(2,1)} %get-tuple-element.351), channel_id=1, source_target_pairs={{0,8},{4,12},{24,16},{28,20},{1,9},{5,13},{25,17},{29,21},{2,10},{... | collective-permute-start | bytes 2359304 | tf_op jit(solution)/shard_map/ppermute | solution.py:1139
  363.2 10.4 %collective-permute-start.38 = (bf16[1,768,384]{2,1,0:T(8,128)(2,1)}, bf16[1,768,384]{2,1,0:T(8,128)(2,1)}, u32[]{:S(2)}, u32[]{:S(2)}) collective-permute-start(bf16[1,768,384]{2,1,0:T(8,128)(2,1)} %get-tuple-element.358), channel_id=1, source_target_pairs={{0,1},{1,0},{2,3},{3,2},{4,6},{5,7},{6,4},{7,5},{8,9},{9,8},{10,11... | collective-permute-start | bytes 1769480 | tf_op jit(solution)/shard_map/ppermute | solution.py:1127
  371.3 35.5 %collective-permute-start.43 = (bf16[1024,384]{1,0:T(8,128)(2,1)}, bf16[1024,384]{1,0:T(8,128)(2,1)}, u32[]{:S(2)}, u32[]{:S(2)}) collective-permute-start(bf16[1024,384]{1,0:T(8,128)(2,1)} %add_convert_fusion.9), channel_id=1, source_target_pairs={{8,16},{12,20},{16,8},{20,12},{9,17},{13,21},{17,9},{21,13},{10,18... | collective-permute-start | bytes 2359304 | tf_op jit(solution)/shard_map/ppermute | solution.py:1139
  377.3 29.5 %collective-permute-start.44 = (bf16[1536,384]{1,0:T(8,128)(2,1)S(1)}, bf16[1536,384]{1,0:T(8,128)(2,1)}, u32[]{:S(2)}, u32[]{:S(2)}) collective-permute-start(bf16[1536,384]{1,0:T(8,128)(2,1)S(1)} %add_convert_fusion.3), channel_id=1, source_target_pairs={{8,0},{12,4},{16,24},{20,28},{9,1},{13,5},{17,25},{21,29},{10,2},{... | collective-permute-start | bytes 3538952 | tf_op jit(solution)/shard_map/ppermute | solution.py:1139
  380.1 26.7 %collective-permute-start.45 = (bf16[384,1536]{1,0:T(8,128)(2,1)S(1)}, bf16[384,1536]{1,0:T(8,128)(2,1)}, u32[]{:S(2)}, u32[]{:S(2)}) collective-permute-start(bf16[384,1536]{1,0:T(8,128)(2,1)S(1)} %broadcast_select_fusion.3), channel_id=1, source_target_pairs={{0,4},{4,0},{8,12},{12,8},{16,20},{20,16},{24,28},{28,24},{1,5},{5... | collective-permute-start | bytes 3538952 | tf_op jit(solution)/shard_map/ppermute | solution.py:1131
  380.2 23.9 %collective-permute-start.42 = (bf16[768,384]{1,0:T(8,128)(2,1)}, bf16[768,384]{1,0:T(8,128)(2,1)}, u32[]{:S(2)}, u32[]{:S(2)}) collective-permute-start(bf16[768,384]{1,0:T(8,128)(2,1)} %get-tuple-element.355), channel_id=1, source_target_pairs={{0,8},{4,12},{24,16},{28,20},{1,9},{5,13},{25,17},{29,21},{2,10},{... | collective-permute-start | bytes 1769480 | tf_op jit(solution)/shard_map/ppermute | solution.py:1139
  386.6 20.2 %collective-permute-start.46 = (f32[4,4964]{1,0:T(4,128)S(1)}, f32[4,4964]{1,0:T(4,128)S(1)}, u32[]{:S(2)}, u32[]{:S(2)}) collective-permute-start(f32[4,4964]{1,0:T(4,128)S(1)} %copy-done.20), channel_id=1, source_target_pairs={{0,4},{4,0},{8,12},{12,8},{16,20},{20,16},{24,28},{28,24},{1,5},{5... | collective-permute-start | bytes 238280 | tf_op jit(solution)/shard_map/ppermute | solution.py:1131
  406.1 19.9 %collective-permute-start.47 = (bf16[768,384]{1,0:T(8,128)(2,1)}, bf16[768,384]{1,0:T(8,128)(2,1)S(1)}, u32[]{:S(2)}, u32[]{:S(2)}) collective-permute-start(bf16[768,384]{1,0:T(8,128)(2,1)} %add_convert_fusion.11), channel_id=1, source_target_pairs={{8,16},{12,20},{16,8},{20,12},{9,17},{13,21},{17,9},{21,13},{10,18... | collective-permute-start | bytes 1769480 | tf_op jit(solution)/shard_map/ppermute | solution.py:1139
  409.3 24.6 %collective-permute-start.48 = (bf16[1536,384]{1,0:T(8,128)(2,1)}, bf16[1536,384]{1,0:T(8,128)(2,1)}, u32[]{:S(2)}, u32[]{:S(2)}) collective-permute-start(bf16[1536,384]{1,0:T(8,128)(2,1)} %broadcast_select_fusion.2.own), channel_id=1, source_target_pairs={{0,4},{4,0},{8,12},{12,8},{16,20},{20,16},{24,28},{28,24},{1,5},{5... | collective-permute-start | bytes 3538952 | tf_op jit(solution)/shard_map/ppermute | solution.py:1131
  412.0 21.9 %collective-permute-start.52 = (bf16[1024,384]{1,0:T(8,128)(2,1)}, bf16[1024,384]{1,0:T(8,128)(2,1)}, u32[]{:S(2)}, u32[]{:S(2)}) collective-permute-start(bf16[1024,384]{1,0:T(8,128)(2,1)} %add_convert_fusion.8), channel_id=1, source_target_pairs={{8,0},{12,4},{16,24},{20,28},{9,1},{13,5},{17,25},{21,29},{10,2},{... | collective-permute-start | bytes 2359304 | tf_op jit(solution)/shard_map/ppermute | solution.py:1139
  414.0 15.5 %collective-permute-start.49 = (f32[1,4964]{1,0:T(1,128)S(1)}, f32[1,4964]{1,0:T(1,128)S(1)}, u32[]{:S(2)}, u32[]{:S(2)}) collective-permute-start(f32[1,4964]{1,0:T(1,128)S(1)} %get-tuple-element.366), channel_id=1, source_target_pairs={{0,1},{1,0},{2,3},{3,2},{4,5},{5,4},{6,7},{7,6},{8,9},{9,8},{10,11... | collective-permute-start | bytes 59576 | tf_op jit(solution)/shard_map/ppermute | solution.py:1135
  415.5 14.1 %collective-permute-start.50 = (f32[1,4964]{1,0:T(1,128)S(1)}, f32[1,4964]{1,0:T(1,128)S(1)}, u32[]{:S(2)}, u32[]{:S(2)}) collective-permute-start(f32[1,4964]{1,0:T(1,128)S(1)} %get-tuple-element.365), channel_id=1, source_target_pairs={{0,2},{1,3},{2,0},{3,1},{4,6},{5,7},{6,4},{7,5},{8,10},{9,11},{10,... | collective-permute-start | bytes 59576 | tf_op jit(solution)/shard_map/ppermute | solution.py:1135
  426.8 4.7 collective-permute-start.51
  435.9 22.1 %collective-permute-start.60 = (bf16[768,384]{1,0:T(8,128)(2,1)}, bf16[768,384]{1,0:T(8,128)(2,1)}, u32[]{:S(2)}, u32[]{:S(2)}) collective-permute-start(bf16[768,384]{1,0:T(8,128)(2,1)} %add_convert_fusion.10), channel_id=1, source_target_pairs={{8,0},{12,4},{16,24},{20,28},{9,1},{13,5},{17,25},{21,29},{10,2},{... | collective-permute-start | bytes 1769480 | tf_op jit(solution)/shard_map/ppermute | solution.py:1139
  437.5 5.4 %collective-permute-start.53 = (f32[4,384]{1,0:T(4,128)S(1)}, f32[4,384]{1,0:T(4,128)S(1)}, u32[]{:S(2)}, u32[]{:S(2)}) collective-permute-start(f32[4,384]{1,0:T(4,128)S(1)} %reshape_squeeze.19), channel_id=1, source_target_pairs={{0,4},{4,0},{8,12},{12,8},{16,20},{20,16},{24,28},{28,24},{1,5},{5... | collective-permute-start | bytes 18440 | tf_op jit(solution)/shard_map/ppermute | solution.py:1131
  438.4 15.5 %collective-permute-start.58 = (f32[1,4964]{1,0:T(1,128)S(1)}, f32[1,4964]{1,0:T(1,128)S(1)}, u32[]{:S(2)}, u32[]{:S(2)}) collective-permute-start(f32[1,4964]{1,0:T(1,128)S(1)} %add_add_fusion), channel_id=1, source_target_pairs={{0,16},{4,20},{8,24},{12,28},{16,0},{20,4},{24,8},{28,12},{1,17},{... | collective-permute-start | bytes 59576 | tf_op jit(solution)/shard_map/ppermute | solution.py:1139
  442.9 9.5 %collective-permute-start.54 = (f32[1,384]{1,0:T(1,128)S(1)}, f32[1,384]{1,0:T(1,128)S(1)}, u32[]{:S(2)}, u32[]{:S(2)}) collective-permute-start(f32[1,384]{1,0:T(1,128)S(1)} %get-tuple-element.373), channel_id=1, source_target_pairs={{0,1},{1,0},{2,3},{3,2},{4,5},{5,4},{6,7},{7,6},{8,9},{9,8},{10,11... | collective-permute-start | bytes 4616 | tf_op jit(solution)/shard_map/ppermute | solution.py:1135
  444.5 9.3 %collective-permute-start.55 = (f32[1,384]{1,0:T(1,128)S(1)}, f32[1,384]{1,0:T(1,128)S(1)}, u32[]{:S(2)}, u32[]{:S(2)}) collective-permute-start(f32[1,384]{1,0:T(1,128)S(1)} %get-tuple-element.372), channel_id=1, source_target_pairs={{0,2},{1,3},{2,0},{3,1},{4,6},{5,7},{6,4},{7,5},{8,10},{9,11},{10,... | collective-permute-start | bytes 4616 | tf_op jit(solution)/shard_map/ppermute | solution.py:1135
  445.3 8.5 %collective-permute-start.56 = (f32[1,384]{1,0:T(1,128)S(1)}, f32[1,384]{1,0:T(1,128)S(1)}, u32[]{:S(2)}, u32[]{:S(2)}) collective-permute-start(f32[1,384]{1,0:T(1,128)S(1)} %get-tuple-element.371), channel_id=1, source_target_pairs={{0,3},{1,2},{2,1},{3,0},{4,7},{5,6},{6,5},{7,4},{8,11},{9,10},{10,... | collective-permute-start | bytes 4616 | tf_op jit(solution)/shard_map/ppermute | solution.py:1135
  452.4 5.6 %collective-permute-start.59 = (f32[1,4964]{1,0:T(1,128)S(1)}, f32[1,4964]{1,0:T(1,128)S(1)}, u32[]{:S(2)}, u32[]{:S(2)}) collective-permute-start(f32[1,4964]{1,0:T(1,128)S(1)} %add_add_fusion), channel_id=1, source_target_pairs={{0,24},{4,28},{8,16},{12,20},{16,8},{20,12},{24,0},{28,4},{1,25},{... | collective-permute-start | bytes 59576 | tf_op jit(solution)/shard_map/ppermute | solution.py:1139
  453.7 4.2 collective-permute-start.57
  453.7 15.8 %collective-permute-start.65 = (bf16[1024,384]{1,0:T(8,128)(2,1)S(1)}, bf16[1024,384]{1,0:T(8,128)(2,1)}, u32[]{:S(2)}, u32[]{:S(2)}) collective-permute-start(bf16[1024,384]{1,0:T(8,128)(2,1)S(1)} %broadcast_select_fusion.4.refs_0_), channel_id=1, source_target_pairs={{0,4},{4,0},{8,12},{12,8},{16,20},{20,16},{24,28},{28,24},{1,5},{5... | collective-permute-start | bytes 2359304 | tf_op jit(solution)/shard_map/ppermute | solution.py:1131
  460.0 13.4 %collective-permute-start.64 = (bf16[768,384]{1,0:T(8,128)(2,1)}, bf16[768,384]{1,0:T(8,128)(2,1)}, u32[]{:S(2)}, u32[]{:S(2)}) collective-permute-start(bf16[768,384]{1,0:T(8,128)(2,1)} %broadcast_select_fusion.5.refs_0_), channel_id=1, source_target_pairs={{0,4},{4,0},{8,12},{12,8},{16,20},{20,16},{24,28},{28,24},{1,5},{5... | collective-permute-start | bytes 1769480 | tf_op jit(solution)/shard_map/ppermute | solution.py:1131
  462.8 6.0 %collective-permute-start.62 = (f32[1,384]{1,0:T(1,128)S(1)}, f32[1,384]{1,0:T(1,128)S(1)}, u32[]{:S(2)}, u32[]{:S(2)}) collective-permute-start(f32[1,384]{1,0:T(1,128)S(1)} %fusion.9), channel_id=1, source_target_pairs={{0,16},{4,20},{8,24},{12,28},{16,0},{20,4},{24,8},{28,12},{1,17},{... | collective-permute-start | bytes 4616 | tf_op jit(solution)/shard_map/ppermute | solution.py:1139
  463.6 5.4 %collective-permute-start.63 = (f32[1,384]{1,0:T(1,128)S(1)}, f32[1,384]{1,0:T(1,128)S(1)}, u32[]{:S(2)}, u32[]{:S(2)}) collective-permute-start(f32[1,384]{1,0:T(1,128)S(1)} %fusion.9), channel_id=1, source_target_pairs={{0,24},{4,28},{8,16},{12,20},{16,8},{20,12},{24,0},{28,4},{1,25},{... | collective-permute-start | bytes 4616 | tf_op jit(solution)/shard_map/ppermute | solution.py:1139
  464.9 4.0 collective-permute-start.61
  (35 other events, 259.4 us)
where the time goes:
time: 483 us; the launch traced here: 477 us
  Pallas kernels  225 us (47%)
  starting transfers between devices  81.7 us (17%)
  waiting for transfers between devices  69 us (14%)
  other arithmetic  56.2 us (12%)
  local copies, waits for them, and re-layouts  42.7 us (9%)
    pallas_call x18, Pallas kernels, call(): pl.pallas_call(body, name=name, grid_spec=pltpu.PrefetchScalarGridSpec(nu...  225 us
    ppermute x17, waiting for transfers between devices, hop(): return lax.ppermute(x, ('rep', 'shard'), pairs)  54 us
    ppermute x18, starting transfers between devices, along(): lax.ppermute(x, 'rep', [(2 * a + k, 2 * b + k) for a, b in pairs for k in...  43.8 us
    ppermute x17, starting transfers between devices, hop(): return lax.ppermute(x, ('rep', 'shard'), pairs)  22.4 us
    unnamed x72, local copies, waits for them, and re-layouts  12.3 us
    convert_element_type x4, other arithmetic, inward(): return (held, along(held.astype(BF), [(0, 1), (3, 2)]))  11.1 us
  transfers between devices with their start and end apart: 66, of which 17 were waited for; matrix products, arithmetic and copies ran while one was open for 16% of the time, Pallas kernels for 44%

commit v1 on v0

--- a/solution.py
+++ b/solution.py
@@ -340,24 +340,26 @@
             out[at : at + SPAN, lanes] += heads_together(dot(mixes[pair, span], value))
 
 
-def scan_forward(meta, signal, keys, columns, rows, skip):
+def scan_forward(meta, signal, keys, columns, rows, skip, first, count, filled):
     tokens = signal.shape[0]
+
+    def group(*shape):
+        return pl.BlockSpec((1,) + shape, lambda i, meta: (i + first, 0, 0))
+
     return call(
         scan_body, "scan_forward", meta, (signal, keys, columns, rows, skip),
         [
-            tiles(tokens, TILE), whole((tokens, TILE)),
-            pl.BlockSpec((1, tokens, PACK), lambda i, meta: (i, 0, 0)),
-            pl.BlockSpec((1, 2 * PER, tokens), lambda i, meta: (i, 0, 0)),
-            tiles(1, TILE),
+            tiles(tokens, TILE, first), whole((tokens, TILE)), group(tokens, PACK),
+            group(2 * PER, tokens), tiles(1, TILE, first),
         ],
         [shape_of((tokens, DI)), shape_of((GROUPS, DSTATE, TILE), BF)],
-        [tiles(tokens, TILE), pl.BlockSpec((1, DSTATE, TILE), lambda i, meta: (i, 0, 0))],
+        [tiles(tokens, TILE, first), group(DSTATE, TILE)],
         [
             pltpu.VMEM((2, SPAN, SPAN), F32), pltpu.VMEM((DSTATE, SPAN), BF),
             pltpu.VMEM((PER // 2, 2, 2 * SPAN, SPAN), BF), pltpu.VMEM((SPAN // 2, SPAN // 2), F32),
             pltpu.VMEM((2 * PER, TILE), BF),
         ],
-        GROUPS, 10 * 10**9, 12 * MIB,
+        count, 10**9 * count, count * MIB, dict(enumerate(filled)) if filled else None,
     )
 
 
@@ -1031,6 +1033,9 @@
 
     for grad, grad_first, steps, half, own, own_first, rest, rest_first, local_first in parts:
         columns = WIDE if half is not None else grad.shape[1]
+        if half is not None and steps == WIDES // 2:
+            columns, steps = steps * WIDE, 1
+            grad_first, local_first = (at // (WIDES // 2) for at in (grad_first, local_first))
         row_tile = 64 if columns == LANES else columns
         plan.append((step, steps, half))
         grads.append(grad)
@@ -1047,7 +1052,7 @@
         step += steps
     more, more_specs = (), []
     outs, out_specs = [shape_of((tokens, width))], [whole((tokens, width))]
-    scratch = [pltpu.VMEM((WIDE, width), BF)]
+    scratch = [pltpu.VMEM((WIDES // 2 * WIDE, width), BF)]
     if last is not None:
         more = tuple(last)
         more_specs = [whole((tokens, width))] * 2 + [whole((tokens, 1)), whole((1, width))]
@@ -1289,7 +1294,6 @@
         )
         for j in range(1, count)
     ]
-    piece, everyone = hold((piece, everyone))
     everyone = jnp.stack(everyone).astype(F32)
     order = [jnp.where(core == 0, j, mirrored(j, count)) for j in range(count)]
     whose = jnp.stack(order)[jnp.arange(count) ^ shard]
@@ -1353,13 +1357,19 @@
     if paired:
         gate_near, signal = hold((gate_near, signal))
         gate_own = [gate_piece, *gate_near, hop(gate_near[0], 2)]
-    mixed, entering = scan_forward(meta, signal, keys, columns, rows, skip_lanes)
+    kept = None
+    for first in range(0, GROUPS, GROUPS // 2):
+        kept = scan_forward(
+            meta, signal, keys, columns, rows, skip_lanes, first, GROUPS // 2, kept
+        )
+        if paired and first == 0:
+            gate_far, out_piece, kept = hold((gate_own[3], out_piece, kept))
+            gate_own[3] = gate_far
+            gate_rest = [swap(block) for block in gate_own[1:]]
+            out_near = hop(out_piece, 1), hop(out_piece, 2)
+    mixed, entering = kept
     if paired:
-        out_piece, gate_far, mixed = hold((out_piece, gate_own[3], mixed))
-        gate_own[3] = gate_far
-        gate_rest = [swap(block) for block in gate_own[1:]]
         rest_conv, rest_gate = [local] + conv_rest, [local] + gate_rest
-        out_near = hop(out_piece, 1), hop(out_piece, 2)
     gate, normed_out, out_theirs, scale = gate_forward(
         meta, normed, mixed, gain_two[None], gate_own, gate_rest, in_local
     )
@@ -1530,16 +1540,16 @@
     gain_row = add_up(group_rows(vector + swap(vector), shard, count))
     all_rows = local.shape[0]
     rows_so_far = place_rows(meta, gate_total, gate_other, DI // 2, 0, all_rows, None, False)
-    gain_row, row, far_arrived, rows_so_far = hold((gain_row, row, far_line[1], rows_so_far))
-    gain_row = chips_sum(gain_row)[0]
-    far_total = summed((far_done, far_arrived))
-    far_other = swap(far_total)
     near_total = summed((near_done, near_arrived))
     near_other = swap(near_total)
     wide = near // 2 * TILE
     rows_so_far = place_rows(
         meta, near_total, near_other, wide, DI // wide, all_rows, rows_so_far, False
     )
+    gain_row, row, far_arrived, rows_so_far = hold((gain_row, row, far_line[1], rows_so_far))
+    gain_row = chips_sum(gain_row)[0]
+    far_total = summed((far_done, far_arrived))
+    far_other = swap(far_total)
     wide = far // 2 * TILE
     rows_so_far = place_rows(
         meta, far_total, far_other, wide, (DI + near * TILE) // wide, all_rows, rows_so_far, True

time: 483 us -> 474 us (0.981)
  waiting for transfers between devices: 69 us -> 63.6 us
  local copies, waits for them, and re-layouts: 42.7 us -> 37.4 us
    ppermute x17, waiting for transfers between devices: 54 us -> 44.3 us  [hop(): return lax.ppermute(x, ('rep', 'shard'), pairs)]
    pallas_call x18 -> x19, Pallas kernels: 225 us -> 229 us  [call(): pl.pallas_call(body, name=name, grid_spec=pltpu.PrefetchScalarGridSpec(nu...]
    unnamed x72 -> x96, local copies, waits for them, and re-layouts: 12.3 us -> 11.7 us
  transfers between devices with their start and end apart: 66 -> 66, of which waited for: 17 -> 17; matrix products, arithmetic and copies ran while one was open for 16% -> 15% of each run, Pallas kernels for 44% -> 46%
where the time goes in v1:
time: 474 us; the launch traced here: 469 us
  Pallas kernels  229 us (48%)
  starting transfers between devices  80.6 us (17%)
  waiting for transfers between devices  63.6 us (13%)
  other arithmetic  54.5 us (11%)
  local copies, waits for them, and re-layouts  37.4 us (8%)
    pallas_call x19, Pallas kernels, call(): pl.pallas_call(body, name=name, grid_spec=pltpu.PrefetchScalarGridSpec(nu...  229 us
    ppermute x17, waiting for transfers between devices, hop(): return lax.ppermute(x, ('rep', 'shard'), pairs)  44.3 us
    ppermute x18, starting transfers between devices, along(): lax.ppermute(x, 'rep', [(2 * a + k, 2 * b + k) for a, b in pairs for k in...  43.6 us
    ppermute x17, starting transfers between devices, hop(): return lax.ppermute(x, ('rep', 'shard'), pairs)  22 us
    unnamed x96, local copies, waits for them, and re-layouts  11.7 us
    convert_element_type x4, other arithmetic, inward(): return (held, along(held.astype(BF), [(0, 1), (3, 2)]))  11 us
  transfers between devices with their start and end apart: 66, of which 17 were waited for; matrix products, arithmetic and copies ran while one was open for 15% of the time, Pallas kernels for 46%

profile of v1, /device:TPU:0, one launch (start us, length us, event | category | flops | bytes accessed | tf_op | source)
XLA Modules:
  0.0 468.7 jit_solution(10578506048121706890)
XLA Ops:
  1.6 2.9 dynamic-slice_bitcast_fusion
  5.0 3.0 collective-permute-start
  9.8 2.0 collective-permute-start.6
  14.0 25.6 %collective-permute-done.refs_1_.refs_9_.refs_13_.refs_5_.refs_21_.refs_4_.refs_8_ = bf16[1856,384]{1,0:T(8,128)(2,1)S(1)} collective-permute-done((bf16[1856,384]{1,0:T(8,128)(2,1)S(1)}, bf16[1856,384]{1,0:T(8,128)(2,1)S(1)}, u32[]{:S(2)}, u32[]{:S(2)}) %collective-permute-start) | collective-permute-done | bytes 1425440 | tf_op jit(solution)/shard_map/ppermute | solution.py:1132
  39.5 1.8 collective-permute-start.2
  41.4 1.8 fusion
  46.2 12.3 %collective-permute-done.2.refs_3_.refs_11_.refs_15_.refs_7_.refs_23_.refs_6_.refs_10_ = bf16[1856,384]{1,0:T(8,128)(2,1)} collective-permute-done((bf16[1856,384]{1,0:T(8,128)(2,1)S(1)}, bf16[1856,384]{1,0:T(8,128)(2,1)}, u32[]{:S(2)}, u32[]{:S(2)}) %collective-permute-start.2) | collective-permute-done | bytes 1425440 | tf_op jit(solution)/shard_map/ppermute | solution.py:1132
  59.7 2.5 collective-permute-start.3
  64.0 3.0 fusion.2.x.refs_2_.refs_4_
  68.1 24.5 %conv_forward.1 = (bf16[512,3072]{1,0:T(8,128)(2,1)}, bf16[512,3072]{1,0:T(8,128)(2,1)}, f32[512,3072]{1,0:T(8,128)}, bf16[512,256]{1,0:T(8,128)(2,1)}, bf16[512...) custom-call(s32[20]{0:T(128)} %stack.90.meta, ...), custom_call_target="tpu_custom_call" | custom-call | flops 5234491392 | bytes 25165824 | tf_op jit(solution)/shard_map/conv_forward/pallas_call | solution.py:91
  93.8 2.4 constant_dynamic-slice_fusion.8
  97.5 9.2 %scan_forward.2 = (f32[512,3072]{1,0:T(8,128)}, bf16[12,128,256]{2,1,0:T(8,128)(2,1)}) custom-call(s32[20]{0:T(128)} %stack.90.meta, bf16[512,3072]{1,0:T(8,128)(2,1)} %get-tuple-element.179.content.refs_0_, bf16[512,256]{1,0:T(8,128)(2,1)} %get-tuple-element.180.keys.refs_1_.refs_0_, f32[12,512,16]{2,1,0:T(8,128)} %get-tuple-element.181.columns.refs_2_, ...), custom_call_target="tpu_custom_call" | custom-call | flops 6000000000 | bytes 6291456 | tf_op jit(solution)/shard_map/scan_forward/pallas_call | solution.py:91
  106.7 2.5 collective-permute-done.11.refs_3_.refs_5_.refs_13_
  111.3 9.1 %scan_forward.3 = (f32[512,3072]{1,0:T(8,128)}, bf16[12,128,256]{2,1,0:T(8,128)(2,1)}) custom-call(s32[20]{0:T(128)} %stack.90.meta, bf16[512,3072]{1,0:T(8,128)(2,1)} %get-tuple-element.179.content.refs_0_, bf16[512,256]{1,0:T(8,128)(2,1)} %get-tuple-element.180.keys.refs_1_.refs_0_, ...), custom_call_target="tpu_custom_call", output_to_operand_aliasing={{0}: (6, {}), {1}: (7, {})} | custom-call | flops 6000000000 | bytes 6291456 | tf_op jit(solution)/shard_map/scan_forward/pallas_call | solution.py:91
  121.5 17.1 %gate_forward.1 = (bf16[512,3072]{1,0:T(8,128)(2,1)}, bf16[512,3072]{1,0:T(8,128)(2,1)}, bf16[512,1536]{1,0:T(8,128)(2,1)}, f32[512,1]{1,0:T(8,128)}) custom-call(s32[20]{0:T(128)} %stack.90.meta, bf16[512,1536]{1,0:T(8,128)(2,1)} %fusion.2.x.refs_2_.refs_4_, f32[512,3072]{1,0:T(8,128)} %get-tuple-element.188.mixed, f32[1,3072]{1,0:T(1,128)} %bitcast.76, ...), custom_call_target="tpu_custom_call" | custom-call | flops 4831838208 | bytes 29360128 | tf_op jit(solution)/shard_map/gate_forward/pallas_call | solution.py:91
  140.3 2.1 collective-permute-done.17.theirs
  142.4 11.1 %rows_product.1 = (bf16[2,384,1536]{2,1,0:T(8,128)(2,1)}, bf16[2,384,1536]{2,1,0:T(8,128)(2,1)}) custom-call(s32[20]{0:T(128)} %stack.90.meta, bf16[512,3072]{1,0:T(8,128)(2,1)} %get-tuple-element.196.mine.refs_0_.refs_1_, bf16[512,1536]{1,0:T(8,128)(2,1)} %collective-permute-done.17.theirs, bf16[512,1536]{1,0:T(8,128)(2,1)} %copy-done.12, ...), custom_call_target="tpu_custom_call" | custom-call | flops 4831838208 | bytes 12582912 | tf_op jit(solution)/shard_map/rows_product/pallas_call | solution.py:91
  155.8 1.9 collective-permute-done.20.refs_9_
  157.7 3.4 collective-permute-done.21.refs_10_
  162.1 21.5 %out_forward.1 = (bf16[512,1536]{1,0:T(8,128)(2,1)}, bf16[512,3072]{1,0:T(8,128)(2,1)}, f32[512,128]{1,0:T(8,128)}) custom-call(s32[20]{0:T(128)} %stack.90.meta, bf16[512,3072]{1,0:T(8,128)(2,1)} %get-tuple-element.196.mine.refs_0_.refs_1_, bf16[512,3072]{1,0:T(8,128)(2,1)} %get-tuple-element.196.mine.refs_0_.refs_1_, bf16[512,1536]{1,0:T(8,128)(2,1)} %copy-done.12, ...), custom_call_target="tpu_custom_call" | custom-call | flops 9663676416 | bytes 25165824 | tf_op jit(solution)/shard_map/out_forward/pallas_call | solution.py:91
  183.6 2.3 add_convert_fusion.1
  188.6 12.2 %norm_back.1 = (bf16[512,3072]{1,0:T(8,128)(2,1)}, bf16[512,1536]{1,0:T(8,128)(2,1)}, bf16[512,3072]{1,0:T(8,128)(2,1)}, f32[8,3072]{1,0:T(8,128)}) custom-call(s32[20]{0:T(128)} %stack.90.meta, bf16[512,3072]{1,0:T(8,128)(2,1)} %get-tuple-element.203.back, f32[512,128]{1,0:T(8,128)} %get-tuple-element.209.total, f32[512,3072]{1,0:T(8,128)} %get-tuple-element.188.mixed, ...), custom_call_target="tpu_custom_call" | custom-call | flops 1000000000 | bytes 25165824 | tf_op jit(solution)/shard_map/norm_back/pallas_call | solution.py:91
  200.8 2.5 collective-permute-done.24
  204.8 3.8 fusion.13
  212.4 10.7 %columns_product.3 = (bf16[2,1536,384]{2,1,0:T(8,128)(2,1)}, bf16[2,1536,384]{2,1,0:T(8,128)(2,1)}) custom-call(s32[20]{0:T(128)} %stack.90.meta, bf16[512,3072]{1,0:T(8,128)(2,1)} %get-tuple-element.274.refs_0_.refs_1_, bf16[512,1536]{1,0:T(8,128)(2,1)} %copy-done.13, bf16[512,1536]{1,0:T(8,128)(2,1)} %fusion.2.x.refs_2_.refs_4_, bf16[512,1536]{1,0:T(8,128)(2,1)} %copy-done.4), custom_call_target="tpu_custom_call" | custom-call | flops 1 | bytes 1 | tf_op jit(solution)/shard_map/columns_product/pallas_call | solution.py:91
  224.1 3.6 collective-permute-start.28
  229.2 22.7 %scan_backward.2 = (bf16[512,2048]{1,0:T(8,128)(2,1)}, bf16[512,1024]{1,0:T(8,128)(2,1)}, f32[8,2048]{1,0:T(8,128)}, f32[8,512,8]{2,1,0:T(8,128)}, f32[2,256,256...) custom-call(s32[20]{0:T(128)} %stack.90.meta, bf16[512,3072]{1,0:T(8,128)(2,1)} %get-tuple-element.179.content.refs_0_, ...), custom_call_target="tpu_custom_call" | custom-call | flops 24000000000 | bytes 8388608 | tf_op jit(solution)/shard_map/scan_backward/pallas_call | solution.py:91
  251.9 1.7 collective-permute-done.28
  254.6 2.2 add_convert_fusion
  259.7 1.7 collective-permute-start.36
  261.3 8.4 %columns_product.4 = (bf16[2,1024,384]{2,1,0:T(8,128)(2,1)}, bf16[2,1024,384]{2,1,0:T(8,128)(2,1)}) custom-call(s32[20]{0:T(128)} %stack.90.meta, bf16[512,2048]{1,0:T(8,128)(2,1)} %get-tuple-element.235.refs_0_.refs_1_, bf16[512,1024]{1,0:T(8,128)(2,1)} %collective-permute-done.29.refs_1_, bf16[512,1536]{1,0:T(8,128)(2,1)} %fusion.2.x.refs_2_.refs_4_, ...), custom_call_target="tpu_custom_call" | custom-call | flops 1 | bytes 1 | tf_op jit(solution)/shard_map/columns_product/pallas_call | solution.py:91
  270.8 13.2 %scan_backward.3 = (bf16[512,1024]{1,0:T(8,128)(2,1)}, bf16[512,512]{1,0:T(8,128)(2,1)}, f32[8,1024]{1,0:T(8,128)}, f32[4,512,8]{2,1,0:T(8,128)}, f32[2,256,256]...) custom-call(s32[20]{0:T(128)} %stack.90.meta, bf16[512,3072]{1,0:T(8,128)(2,1)} %get-tuple-element.179.content.refs_0_, ...), custom_call_target="tpu_custom_call" | custom-call | flops 12000000000 | bytes 4194304 | tf_op jit(solution)/shard_map/scan_backward/pallas_call | solution.py:91
  285.0 2.9 fusion.14
  287.9 7.2 %collective-permute-start.34 = (bf16[1536,384]{1,0:T(8,128)(2,1)}, bf16[1536,384]{1,0:T(8,128)(2,1)}, u32[]{:S(2)}, u32[]{:S(2)}) collective-permute-start(bf16[1536,384]{1,0:T(8,128)(2,1)} %get-tuple-element.339), channel_id=1, source_target_pairs={{0,8},{4,12},{24,16},{28,20},{1,9},{5,13},{25,17},{29,21},{2,10},{... | collective-permute-start | bytes 3538952 | tf_op jit(solution)/shard_map/ppermute | solution.py:1144
  295.1 6.6 %tail_backward.1 = (bf16[512,256]{1,0:T(8,128)(2,1)}, f32[8,256]{1,0:T(8,128)}, bf16[512,128]{1,0:T(8,128)(2,1)}, f32[8,128]{1,0:T(8,128)}, bf16[2,512,256]{2,1,0:T(8,128)(2,1)}) custom-call(s32[20]{0:T(128)} %stack.90.meta, bf16[512,256]{1,0:T(8,128)(2,1)} %get-tuple-element.180.keys.refs_1_.refs_0_, bf16[512,256]{1,0:T(8,128)(2,1)} %get-tuple-element.200.refs_1_, ...), custom_call_target="tpu_custom_call" | custom-call | flops 1 | bytes 1 | tf_op jit(solution)/shard_map/tail_backward/pallas_call | solution.py:91
  301.6 2.3 add_convert_fusion.2
  308.9 1.7 slice_bitcast_fusion.refs_1_
  310.6 7.5 %columns_product.5 = (bf16[2,768,384]{2,1,0:T(8,128)(2,1)}, bf16[2,768,384]{2,1,0:T(8,128)(2,1)}) custom-call(s32[20]{0:T(128)} %stack.90.meta, bf16[512,1024]{1,0:T(8,128)(2,1)} %get-tuple-element.257.refs_0_.refs_2_, bf16[512,256]{1,0:T(8,128)(2,1)} %slice_bitcast_fusion.refs_1_, bf16[512,512]{1,0:T(8,128)(2,1)} %collective-permute-done.33.refs_2_, ...), custom_call_target="tpu_custom_call" | custom-call | flops 1 | bytes 1 | tf_op jit(solution)/shard_map/columns_product/pallas_call | solution.py:91
  319.0 2.5 add_convert_fusion.6
  322.5 2.5 add_convert_fusion.5
  326.3 2.2 fusion.12
  328.6 7.0 %collective-permute-start.39 = (bf16[1024,384]{1,0:T(8,128)(2,1)}, bf16[1024,384]{1,0:T(8,128)(2,1)}, u32[]{:S(2)}, u32[]{:S(2)}) collective-permute-start(bf16[1024,384]{1,0:T(8,128)(2,1)} %get-tuple-element.347), channel_id=1, source_target_pairs={{0,8},{4,12},{24,16},{28,20},{1,9},{5,13},{25,17},{29,21},{2,10},{... | collective-permute-start | bytes 2359304 | tf_op jit(solution)/shard_map/ppermute | solution.py:1144
  335.6 16.0 %input_backward.3.refs_3_ = f32[512,1536]{1,0:T(8,128)} custom-call(s32[20]{0:T(128)} %stack.90.meta, bf16[512,3072]{1,0:T(8,128)(2,1)} %get-tuple-element.274.refs_0_.refs_1_, bf16[512,3072]{1,0:T(8,128)(2,1)} %get-tuple-element.274.refs_0_.refs_1_, bf16[1536,384]{1,0:T(8,128)(2,1)} %get-tuple-element.172.refs_0_.refs_2_.refs_10_, ...), custom_call_target="tpu_custom_call" | custom-call | flops 10000000000 | bytes 20971520 | tf_op jit(solution)/shard_map/input_backward/pallas_call | solution.py:91
  351.6 1.9 add_convert_fusion.4
  360.2 2.2 add_convert_fusion.9
  362.4 1.5 collective-permute-start.43
  364.7 2.0 fusion.11
  366.7 1.6 add_convert_fusion.3
  371.2 6.5 %collective-permute-start.42 = (bf16[768,384]{1,0:T(8,128)(2,1)}, bf16[768,384]{1,0:T(8,128)(2,1)}, u32[]{:S(2)}, u32[]{:S(2)}) collective-permute-start(bf16[768,384]{1,0:T(8,128)(2,1)} %get-tuple-element.351), channel_id=1, source_target_pairs={{0,8},{4,12},{24,16},{28,20},{1,9},{5,13},{25,17},{29,21},{2,10},{... | collective-permute-start | bytes 1769480 | tf_op jit(solution)/shard_map/ppermute | solution.py:1144
  377.9 17.7 %input_backward.4.refs_2_ = f32[512,1536]{1,0:T(8,128)} custom-call(s32[20]{0:T(128)} %stack.90.meta, bf16[512,2048]{1,0:T(8,128)(2,1)} %get-tuple-element.235.refs_0_.refs_1_, bf16[512,2048]{1,0:T(8,128)(2,1)} %get-tuple-element.235.refs_0_.refs_1_, bf16[512,1024]{1,0:T(8,128)(2,1)} %get-tuple-element.257.refs_0_.refs_2_, ...), custom_call_target="tpu_custom_call" | custom-call | flops 10000000000 | bytes 20971520 | tf_op jit(solution)/shard_map/input_backward/pallas_call | solution.py:91
  395.6 2.0 add_convert_fusion.11
  398.3 2.5 broadcast_select_fusion.2.own
  401.1 2.4 add_convert_fusion.8
  408.1 9.7 %input_backward.5 = (f32[512,1536]{1,0:T(8,128)}, f32[1,1536]{1,0:T(1,128)}) custom-call(s32[20]{0:T(128)} %stack.90.meta, bf16[512,256]{1,0:T(8,128)(2,1)} %get-tuple-element.255.refs_0_, bf16[512,128]{1,0:T(8,128)(2,1)} %get-tuple-element.256.refs_1_, f32[512,1536]{1,0:T(8,128)} %input_backward.4.refs_2_, bf16[1856,384]{1,0:T(8,128)(2,1)} %copy-done, ...), custom_call_target="tpu_custom_call" | custom-call | flops 99999997952 | bytes 20971520 | tf_op jit(solution)/shard_map/input_backward/pallas_call | solution.py:91
  421.1 2.2 collective-permute-done.51
  423.3 2.1 collective-permute-done.52
  425.4 2.0 add_convert_fusion.10
  430.8 1.6 collective-permute-start.54
  434.4 4.7 place_rows.3.refs_2_
  439.0 4.5 collective-permute-start.58
  445.3 3.8 collective-permute-done.59
  449.2 3.8 place_rows.4.refs_2_
  454.2 2.8 maximum_convert_fusion
  464.7 3.7 place_rows.5
  (289 shorter events, 81.3 us)
Async XLA Ops:
  5.0 34.5 %collective-permute-start = (bf16[1856,384]{1,0:T(8,128)(2,1)S(1)}, bf16[1856,384]{1,0:T(8,128)(2,1)S(1)}, u32[]{:S(2)}, u32[]{:S(2)}) collective-permute-start(bf16[1856,384]{1,0:T(8,128)(2,1)S(1)} %maximum_maximum_fusion.refs_0_.refs_8_.refs_12_.refs_4_.refs_20_.refs_3_.refs_7_), channel_id=1, source_target_pairs={{0,1},{1,0},{2,3},{3,2},{4,6},{5,7},{6,4},{7,5},{8,9},{9,8},{10,11... | collective-permute-start | bytes 4276232 | tf_op jit(solution)/shard_map/ppermute | solution.py:1132
  8.0 38.2 %collective-permute-start.1 = (bf16[1856,384]{1,0:T(8,128)(2,1)S(1)}, bf16[1856,384]{1,0:T(8,128)(2,1)}, u32[]{:S(2)}, u32[]{:S(2)}) collective-permute-start(bf16[1856,384]{1,0:T(8,128)(2,1)S(1)} %maximum_maximum_fusion.refs_0_.refs_8_.refs_12_.refs_4_.refs_20_.refs_3_.refs_7_), channel_id=1, source_target_pairs={{0,2},{1,3},{2,0},{3,1},{4,5},{5,4},{6,7},{7,6},{8,10},{9,11},{10,... | collective-permute-start | bytes 4276232 | tf_op jit(solution)/shard_map/ppermute | solution.py:1132
  9.8 35.5 %collective-permute-start.7 = (bf16[5348]{0:T(1024)(128)(2,1)S(1)}, bf16[5348]{0:T(1024)(128)(2,1)S(1)}, u32[]{:S(2)}, u32[]{:S(2)}) collective-permute-start(bf16[5348]{0:T(1024)(128)(2,1)S(1)} %concatenate.29), channel_id=1, source_target_pairs={{0,3},{1,2},{2,1},{3,0},{4,7},{5,6},{6,5},{7,4},{8,11},{9,10},{10,... | collective-permute-start | bytes 32096 | tf_op jit(solution)/shard_map/ppermute | solution.py:1287
  9.8 35.5 %collective-permute-start.6 = (bf16[5348]{0:T(1024)(128)(2,1)S(1)}, bf16[5348]{0:T(1024)(128)(2,1)S(1)}, u32[]{:S(2)}, u32[]{:S(2)}) collective-permute-start(bf16[5348]{0:T(1024)(128)(2,1)S(1)} %concatenate.29), channel_id=1, source_target_pairs={{0,2},{1,3},{2,0},{3,1},{4,5},{5,4},{6,7},{7,6},{8,10},{9,11},{10,... | collective-permute-start | bytes 32096 | tf_op jit(solution)/shard_map/ppermute | solution.py:1287
  11.8 33.6 %collective-permute-start.5 = (bf16[5348]{0:T(1024)(128)(2,1)S(1)}, bf16[5348]{0:T(1024)(128)(2,1)S(1)}, u32[]{:S(2)}, u32[]{:S(2)}) collective-permute-start(bf16[5348]{0:T(1024)(128)(2,1)S(1)} %concatenate.29), channel_id=1, source_target_pairs={{0,1},{1,0},{2,3},{3,2},{4,6},{5,7},{6,4},{7,5},{8,9},{9,8},{10,11... | collective-permute-start | bytes 32096 | tf_op jit(solution)/shard_map/ppermute | solution.py:1287
  39.5 18.9 %collective-permute-start.2 = (bf16[1856,384]{1,0:T(8,128)(2,1)S(1)}, bf16[1856,384]{1,0:T(8,128)(2,1)}, u32[]{:S(2)}, u32[]{:S(2)}) collective-permute-start(bf16[1856,384]{1,0:T(8,128)(2,1)S(1)} %collective-permute-done.refs_1_.refs_9_.refs_13_.refs_5_.refs_21_.refs_4_.refs_8_), channel_id=1, source_target_pairs={{0,2},{1,3},{2,0},{3,1},{4,5},{5,4},{6,7},{7,6},{8,10},{9,11},{10,... | collective-permute-start | bytes 4276232 | tf_op jit(solution)/shard_map/ppermute | solution.py:1132
  58.5 8.6 %collective-permute-start.8 = (bf16[1856,384]{1,0:T(8,128)(2,1)S(1)}, bf16[1856,384]{1,0:T(8,128)(2,1)S(1)}, u32[]{:S(2)}, u32[]{:S(2)}) collective-permute-start(bf16[1856,384]{1,0:T(8,128)(2,1)S(1)} %collective-permute-done.refs_1_.refs_9_.refs_13_.refs_5_.refs_21_.refs_4_.refs_8_), channel_id=1, source_target_pairs={{0,4},{4,0},{8,12},{12,8},{16,20},{20,16},{24,28},{28,24},{1,5},{5... | collective-permute-start | bytes 4276232 | tf_op jit(solution)/shard_map/ppermute | solution.py:1136
  58.5 8.6 %collective-permute-start.9 = (bf16[1856,384]{1,0:T(8,128)(2,1)}, bf16[1856,384]{1,0:T(8,128)(2,1)}, u32[]{:S(2)}, u32[]{:S(2)}) collective-permute-start(bf16[1856,384]{1,0:T(8,128)(2,1)} %collective-permute-done.1.refs_2_.refs_10_.refs_14_.refs_6_.refs_22_.refs_5_.refs_9_), channel_id=1, source_target_pairs={{0,4},{4,0},{8,12},{12,8},{16,20},{20,16},{24,28},{28,24},{1,5},{5... | collective-permute-start | bytes 4276232 | tf_op jit(solution)/shard_map/ppermute | solution.py:1136
  59.0 8.1 %collective-permute-start.10 = (bf16[1856,384]{1,0:T(8,128)(2,1)}, bf16[1856,384]{1,0:T(8,128)(2,1)}, u32[]{:S(2)}, u32[]{:S(2)}) collective-permute-start(bf16[1856,384]{1,0:T(8,128)(2,1)} %collective-permute-done.2.refs_3_.refs_11_.refs_15_.refs_7_.refs_23_.refs_6_.refs_10_), channel_id=1, source_target_pairs={{0,4},{4,0},{8,12},{12,8},{16,20},{20,16},{24,28},{28,24},{1,5},{5... | collective-permute-start | bytes 4276232 | tf_op jit(solution)/shard_map/ppermute | solution.py:1136
  59.7 32.9 %collective-permute-start.3 = (bf16[1536,384]{1,0:T(8,128)(2,1)}, bf16[1536,384]{1,0:T(8,128)(2,1)}, u32[]{:S(2)}, u32[]{:S(2)}) collective-permute-start(bf16[1536,384]{1,0:T(8,128)(2,1)} %get-tuple-element.172.refs_0_.refs_2_.refs_10_), channel_id=1, source_target_pairs={{0,1},{1,0},{2,3},{3,2},{4,6},{5,7},{6,4},{7,5},{8,9},{9,8},{10,11... | collective-permute-start | bytes 3538952 | tf_op jit(solution)/shard_map/ppermute | solution.py:1132
  62.2 30.5 %collective-permute-start.4 = (bf16[1536,384]{1,0:T(8,128)(2,1)}, bf16[1536,384]{1,0:T(8,128)(2,1)}, u32[]{:S(2)}, u32[]{:S(2)}) collective-permute-start(bf16[1536,384]{1,0:T(8,128)(2,1)} %get-tuple-element.172.refs_0_.refs_2_.refs_10_), channel_id=1, source_target_pairs={{0,2},{1,3},{2,0},{3,1},{4,5},{5,4},{6,7},{7,6},{8,10},{9,11},{10,... | collective-permute-start | bytes 3538952 | tf_op jit(solution)/shard_map/ppermute | solution.py:1132
  92.7 16.6 %collective-permute-start.11 = (bf16[1536,384]{1,0:T(8,128)(2,1)}, bf16[1536,384]{1,0:T(8,128)(2,1)}, u32[]{:S(2)}, u32[]{:S(2)}) collective-permute-start(bf16[1536,384]{1,0:T(8,128)(2,1)} %collective-permute-done.3.refs_1_.refs_3_.refs_11_), channel_id=1, source_target_pairs={{0,2},{1,3},{2,0},{3,1},{4,5},{5,4},{6,7},{7,6},{8,10},{9,11},{10,... | collective-permute-start | bytes 3538952 | tf_op jit(solution)/shard_map/ppermute | solution.py:1132
  97.0 23.5 %collective-permute-start.14 = (bf16[1536,384]{1,0:T(8,128)(2,1)}, bf16[1536,384]{1,0:T(8,128)(2,1)}, u32[]{:S(2)}, u32[]{:S(2)}) collective-permute-start(bf16[1536,384]{1,0:T(8,128)(2,1)} %collective-permute-done.3.refs_1_.refs_3_.refs_11_), channel_id=1, source_target_pairs={{0,4},{4,0},{8,12},{12,8},{16,20},{20,16},{24,28},{28,24},{1,5},{5... | collective-permute-start | bytes 3538952 | tf_op jit(solution)/shard_map/ppermute | solution.py:1136
  97.0 24.5 %collective-permute-start.15 = (bf16[1536,384]{1,0:T(8,128)(2,1)}, bf16[1536,384]{1,0:T(8,128)(2,1)}, u32[]{:S(2)}, u32[]{:S(2)}) collective-permute-start(bf16[1536,384]{1,0:T(8,128)(2,1)} %collective-permute-done.4.refs_2_.refs_4_.refs_12_), channel_id=1, source_target_pairs={{0,4},{4,0},{8,12},{12,8},{16,20},{20,16},{24,28},{28,24},{1,5},{5... | collective-permute-start | bytes 3538952 | tf_op jit(solution)/shard_map/ppermute | solution.py:1136
  109.3 12.2 %collective-permute-start.16 = (bf16[1536,384]{1,0:T(8,128)(2,1)}, bf16[1536,384]{1,0:T(8,128)(2,1)}, u32[]{:S(2)}, u32[]{:S(2)}) collective-permute-start(bf16[1536,384]{1,0:T(8,128)(2,1)} %collective-permute-done.11.refs_3_.refs_5_.refs_13_), channel_id=1, source_target_pairs={{0,4},{4,0},{8,12},{12,8},{16,20},{20,16},{24,28},{28,24},{1,5},{5... | collective-permute-start | bytes 3538952 | tf_op jit(solution)/shard_map/ppermute | solution.py:1136
  109.6 30.7 %collective-permute-start.18 = (bf16[512,1536]{1,0:T(8,128)(2,1)S(1)}, bf16[512,1536]{1,0:T(8,128)(2,1)S(1)}, u32[]{:S(2)}, u32[]{:S(2)}) collective-permute-start(bf16[512,1536]{1,0:T(8,128)(2,1)S(1)} %multiply_convert_fusion.pulled.refs_2_), channel_id=1, source_target_pairs={{0,4},{4,0},{8,12},{12,8},{16,20},{20,16},{24,28},{28,24},{1,5},{5... | collective-permute-start | bytes 4718600 | tf_op jit(solution)/shard_map/ppermute | solution.py:1136
  110.9 27.8 %collective-permute-start.12 = (bf16[384,1536]{1,0:T(8,128)(2,1)}, bf16[384,1536]{1,0:T(8,128)(2,1)}, u32[]{:S(2)}, u32[]{:S(2)}) collective-permute-start(bf16[384,1536]{1,0:T(8,128)(2,1)} %constant_dynamic-slice_fusion.8), channel_id=1, source_target_pairs={{0,1},{1,0},{2,3},{3,2},{4,6},{5,7},{6,4},{7,5},{8,9},{9,8},{10,11... | collective-permute-start | bytes 3538952 | tf_op jit(solution)/shard_map/ppermute | solution.py:1132
  120.5 18.8 %collective-permute-start.13 = (bf16[384,1536]{1,0:T(8,128)(2,1)}, bf16[384,1536]{1,0:T(8,128)(2,1)}, u32[]{:S(2)}, u32[]{:S(2)}) collective-permute-start(bf16[384,1536]{1,0:T(8,128)(2,1)} %constant_dynamic-slice_fusion.8), channel_id=1, source_target_pairs={{0,2},{1,3},{2,0},{3,1},{4,5},{5,4},{6,7},{7,6},{8,10},{9,11},{10,... | collective-permute-start | bytes 3538952 | tf_op jit(solution)/shard_map/ppermute | solution.py:1132
  138.6 3.8 collective-permute-start.17
  139.3 16.5 %collective-permute-start.19 = (bf16[384,1536]{1,0:T(8,128)(2,1)}, bf16[384,1536]{1,0:T(8,128)(2,1)}, u32[]{:S(2)}, u32[]{:S(2)}) collective-permute-start(bf16[384,1536]{1,0:T(8,128)(2,1)} %collective-permute-done.12.refs_5_), channel_id=1, source_target_pairs={{0,2},{1,3},{2,0},{3,1},{4,5},{5,4},{6,7},{7,6},{8,10},{9,11},{10,... | collective-permute-start | bytes 3538952 | tf_op jit(solution)/shard_map/ppermute | solution.py:1132
  153.6 30.0 %collective-permute-start.23 = (bf16[2,384,1536]{2,1,0:T(8,128)(2,1)}, bf16[2,384,1536]{2,1,0:T(8,128)(2,1)}, u32[]{:S(2)}, u32[]{:S(2)}) collective-permute-start(bf16[2,384,1536]{2,1,0:T(8,128)(2,1)} %get-tuple-element.205), channel_id=1, source_target_pairs={{0,2},{1,3},{2,0},{3,1},{4,5},{5,4},{6,7},{7,6},{8,10},{9,11},{10,... | collective-permute-start | bytes 7077896 | tf_op jit(solution)/shard_map/ppermute | solution.py:1132
  154.6 3.1 collective-permute-start.20
  155.0 6.1 %collective-permute-start.21 = (bf16[384,1536]{1,0:T(8,128)(2,1)}, bf16[384,1536]{1,0:T(8,128)(2,1)S(1)}, u32[]{:S(2)}, u32[]{:S(2)}) collective-permute-start(bf16[384,1536]{1,0:T(8,128)(2,1)} %collective-permute-done.13.refs_6_), channel_id=1, source_target_pairs={{0,4},{4,0},{8,12},{12,8},{16,20},{20,16},{24,28},{28,24},{1,5},{5... | collective-permute-start | bytes 3538952 | tf_op jit(solution)/shard_map/ppermute | solution.py:1136
  155.8 6.3 %collective-permute-start.22 = (bf16[384,1536]{1,0:T(8,128)(2,1)}, bf16[384,1536]{1,0:T(8,128)(2,1)}, u32[]{:S(2)}, u32[]{:S(2)}) collective-permute-start(bf16[384,1536]{1,0:T(8,128)(2,1)} %collective-permute-done.19.refs_7_), channel_id=1, source_target_pairs={{0,4},{4,0},{8,12},{12,8},{16,20},{20,16},{24,28},{28,24},{1,5},{5... | collective-permute-start | bytes 3538952 | tf_op jit(solution)/shard_map/ppermute | solution.py:1136
  187.1 16.2 %collective-permute-start.24 = (bf16[1,384,1536]{2,1,0:T(8,128)(2,1)S(1)}, bf16[1,384,1536]{2,1,0:T(8,128)(2,1)S(1)}, u32[]{:S(2)}, u32[]{:S(2)}) collective-permute-start(bf16[1,384,1536]{2,1,0:T(8,128)(2,1)S(1)} %get-tuple-element.345), channel_id=1, source_target_pairs={{0,1},{1,0},{2,3},{3,2},{4,6},{5,7},{6,4},{7,5},{8,9},{9,8},{10,11... | collective-permute-start | bytes 3538952 | tf_op jit(solution)/shard_map/ppermute | solution.py:1132
  204.3 5.8 %collective-permute-start.25 = (bf16[512,1536]{1,0:T(8,128)(2,1)}, bf16[512,1536]{1,0:T(8,128)(2,1)S(1)}, u32[]{:S(2)}, u32[]{:S(2)}) collective-permute-start(bf16[512,1536]{1,0:T(8,128)(2,1)} %get-tuple-element.216), channel_id=1, source_target_pairs={{0,4},{4,0},{8,12},{12,8},{16,20},{20,16},{24,28},{28,24},{1,5},{5... | collective-permute-start | bytes 4718600 | tf_op jit(solution)/shard_map/ppermute | solution.py:1136
  204.3 5.8 %collective-permute-start.26 = (bf16[512,1536]{1,0:T(8,128)(2,1)S(1)}, bf16[512,1536]{1,0:T(8,128)(2,1)S(1)}, u32[]{:S(2)}, u32[]{:S(2)}) collective-permute-start(bf16[512,1536]{1,0:T(8,128)(2,1)S(1)} %copy-done.1), channel_id=1, source_target_pairs={{0,4},{4,0},{8,12},{12,8},{16,20},{20,16},{24,28},{28,24},{1,5},{5... | collective-permute-start | bytes 4718600 | tf_op jit(solution)/shard_map/ppermute | solution.py:1136
  223.1 30.5 %collective-permute-start.27 = (bf16[2,1536,384]{2,1,0:T(8,128)(2,1)}, bf16[2,1536,384]{2,1,0:T(8,128)(2,1)}, u32[]{:S(2)}, u32[]{:S(2)}) collective-permute-start(bf16[2,1536,384]{2,1,0:T(8,128)(2,1)} %get-tuple-element.221), channel_id=1, source_target_pairs={{0,2},{1,3},{2,0},{3,1},{4,5},{5,4},{6,7},{7,6},{8,10},{9,11},{10,... | collective-permute-start | bytes 7077896 | tf_op jit(solution)/shard_map/ppermute | solution.py:1132
  224.1 29.5 %collective-permute-start.28 = (bf16[384,1536]{1,0:T(8,128)(2,1)}, bf16[384,1536]{1,0:T(8,128)(2,1)S(1)}, u32[]{:S(2)}, u32[]{:S(2)}) collective-permute-start(bf16[384,1536]{1,0:T(8,128)(2,1)} %get-tuple-element.343), channel_id=1, source_target_pairs={{0,8},{4,12},{24,16},{28,20},{1,9},{5,13},{25,17},{29,21},{2,10},{... | collective-permute-start | bytes 3538952 | tf_op jit(solution)/shard_map/ppermute | solution.py:1144
  253.6 7.7 %collective-permute-start.29 = (bf16[512,1024]{1,0:T(8,128)(2,1)}, bf16[512,1024]{1,0:T(8,128)(2,1)}, u32[]{:S(2)}, u32[]{:S(2)}) collective-permute-start(bf16[512,1024]{1,0:T(8,128)(2,1)} %get-tuple-element.227), channel_id=1, source_target_pairs={{0,4},{4,0},{8,12},{12,8},{16,20},{20,16},{24,28},{28,24},{1,5},{5... | collective-permute-start | bytes 3145736 | tf_op jit(solution)/shard_map/ppermute | solution.py:1136
  258.2 25.8 %collective-permute-start.30 = (bf16[1,1536,384]{2,1,0:T(8,128)(2,1)S(1)}, bf16[1,1536,384]{2,1,0:T(8,128)(2,1)S(1)}, u32[]{:S(2)}, u32[]{:S(2)}) collective-permute-start(bf16[1,1536,384]{2,1,0:T(8,128)(2,1)S(1)} %get-tuple-element.341), channel_id=1, source_target_pairs={{0,1},{1,0},{2,3},{3,2},{4,6},{5,7},{6,4},{7,5},{8,9},{9,8},{10,11... | collective-permute-start | bytes 3538952 | tf_op jit(solution)/shard_map/ppermute | solution.py:1132
  259.7 59.4 %collective-permute-start.36 = (bf16[384,1536]{1,0:T(8,128)(2,1)S(1)}, bf16[384,1536]{1,0:T(8,128)(2,1)}, u32[]{:S(2)}, u32[]{:S(2)}) collective-permute-start(bf16[384,1536]{1,0:T(8,128)(2,1)S(1)} %add_convert_fusion.7), channel_id=1, source_target_pairs={{8,16},{12,20},{16,8},{20,12},{9,17},{13,21},{17,9},{21,13},{10,18... | collective-permute-start | bytes 3538952 | tf_op jit(solution)/shard_map/ppermute | solution.py:1144
  269.7 31.9 %collective-permute-start.31 = (bf16[2,1024,384]{2,1,0:T(8,128)(2,1)}, bf16[2,1024,384]{2,1,0:T(8,128)(2,1)}, u32[]{:S(2)}, u32[]{:S(2)}) collective-permute-start(bf16[2,1024,384]{2,1,0:T(8,128)(2,1)} %get-tuple-element.259), channel_id=1, source_target_pairs={{0,2},{1,3},{2,0},{3,1},{4,5},{5,4},{6,7},{7,6},{8,10},{9,11},{10,... | collective-permute-start | bytes 4718600 | tf_op jit(solution)/shard_map/ppermute | solution.py:1132
  287.9 31.1 %collective-permute-start.34 = (bf16[1536,384]{1,0:T(8,128)(2,1)}, bf16[1536,384]{1,0:T(8,128)(2,1)}, u32[]{:S(2)}, u32[]{:S(2)}) collective-permute-start(bf16[1536,384]{1,0:T(8,128)(2,1)} %get-tuple-element.339), channel_id=1, source_target_pairs={{0,8},{4,12},{24,16},{28,20},{1,9},{5,13},{25,17},{29,21},{2,10},{... | collective-permute-start | bytes 3538952 | tf_op jit(solution)/shard_map/ppermute | solution.py:1144
  305.3 13.8 %collective-permute-start.35 = (bf16[1,1024,384]{2,1,0:T(8,128)(2,1)}, bf16[1,1024,384]{2,1,0:T(8,128)(2,1)}, u32[]{:S(2)}, u32[]{:S(2)}) collective-permute-start(bf16[1,1024,384]{2,1,0:T(8,128)(2,1)} %get-tuple-element.349), channel_id=1, source_target_pairs={{0,1},{1,0},{2,3},{3,2},{4,6},{5,7},{6,4},{7,5},{8,9},{9,8},{10,11... | collective-permute-start | bytes 2359304 | tf_op jit(solution)/shard_map/ppermute | solution.py:1132
  306.2 4.4 collective-permute-start.33
  318.0 33.6 %collective-permute-start.37 = (bf16[2,768,384]{2,1,0:T(8,128)(2,1)}, bf16[2,768,384]{2,1,0:T(8,128)(2,1)}, u32[]{:S(2)}, u32[]{:S(2)}) collective-permute-start(bf16[2,768,384]{2,1,0:T(8,128)(2,1)} %get-tuple-element.275), channel_id=1, source_target_pairs={{0,2},{1,3},{2,0},{3,1},{4,5},{5,4},{6,7},{7,6},{8,10},{9,11},{10,... | collective-permute-start | bytes 3538952 | tf_op jit(solution)/shard_map/ppermute | solution.py:1132
  321.6 45.1 %collective-permute-start.40 = (bf16[1536,384]{1,0:T(8,128)(2,1)}, bf16[1536,384]{1,0:T(8,128)(2,1)S(1)}, u32[]{:S(2)}, u32[]{:S(2)}) collective-permute-start(bf16[1536,384]{1,0:T(8,128)(2,1)} %add_convert_fusion.6), channel_id=1, source_target_pairs={{8,16},{12,20},{16,8},{20,12},{9,17},{13,21},{17,9},{21,13},{10,18... | collective-permute-start | bytes 3538952 | tf_op jit(solution)/shard_map/ppermute | solution.py:1144
  325.0 41.7 %collective-permute-start.41 = (bf16[384,1536]{1,0:T(8,128)(2,1)}, bf16[384,1536]{1,0:T(8,128)(2,1)}, u32[]{:S(2)}, u32[]{:S(2)}) collective-permute-start(bf16[384,1536]{1,0:T(8,128)(2,1)} %add_convert_fusion.5), channel_id=1, source_target_pairs={{8,0},{12,4},{16,24},{20,28},{9,1},{13,5},{17,25},{21,29},{10,2},{... | collective-permute-start | bytes 3538952 | tf_op jit(solution)/shard_map/ppermute | solution.py:1144
  328.6 27.4 %collective-permute-start.39 = (bf16[1024,384]{1,0:T(8,128)(2,1)}, bf16[1024,384]{1,0:T(8,128)(2,1)}, u32[]{:S(2)}, u32[]{:S(2)}) collective-permute-start(bf16[1024,384]{1,0:T(8,128)(2,1)} %get-tuple-element.347), channel_id=1, source_target_pairs={{0,8},{4,12},{24,16},{28,20},{1,9},{5,13},{25,17},{29,21},{2,10},{... | collective-permute-start | bytes 2359304 | tf_op jit(solution)/shard_map/ppermute | solution.py:1144
  354.5 10.2 %collective-permute-start.38 = (bf16[1,768,384]{2,1,0:T(8,128)(2,1)}, bf16[1,768,384]{2,1,0:T(8,128)(2,1)}, u32[]{:S(2)}, u32[]{:S(2)}) collective-permute-start(bf16[1,768,384]{2,1,0:T(8,128)(2,1)} %get-tuple-element.354), channel_id=1, source_target_pairs={{0,1},{1,0},{2,3},{3,2},{4,6},{5,7},{6,4},{7,5},{8,9},{9,8},{10,11... | collective-permute-start | bytes 1769480 | tf_op jit(solution)/shard_map/ppermute | solution.py:1132
  362.4 35.9 %collective-permute-start.43 = (bf16[1024,384]{1,0:T(8,128)(2,1)}, bf16[1024,384]{1,0:T(8,128)(2,1)}, u32[]{:S(2)}, u32[]{:S(2)}) collective-permute-start(bf16[1024,384]{1,0:T(8,128)(2,1)} %add_convert_fusion.9), channel_id=1, source_target_pairs={{8,16},{12,20},{16,8},{20,12},{9,17},{13,21},{17,9},{21,13},{10,18... | collective-permute-start | bytes 2359304 | tf_op jit(solution)/shard_map/ppermute | solution.py:1144
  368.3 30.0 %collective-permute-start.44 = (bf16[1536,384]{1,0:T(8,128)(2,1)S(1)}, bf16[1536,384]{1,0:T(8,128)(2,1)}, u32[]{:S(2)}, u32[]{:S(2)}) collective-permute-start(bf16[1536,384]{1,0:T(8,128)(2,1)S(1)} %add_convert_fusion.3), channel_id=1, source_target_pairs={{8,0},{12,4},{16,24},{20,28},{9,1},{13,5},{17,25},{21,29},{10,2},{... | collective-permute-start | bytes 3538952 | tf_op jit(solution)/shard_map/ppermute | solution.py:1144
  371.1 27.2 %collective-permute-start.45 = (bf16[384,1536]{1,0:T(8,128)(2,1)S(1)}, bf16[384,1536]{1,0:T(8,128)(2,1)}, u32[]{:S(2)}, u32[]{:S(2)}) collective-permute-start(bf16[384,1536]{1,0:T(8,128)(2,1)S(1)} %broadcast_select_fusion.3), channel_id=1, source_target_pairs={{0,4},{4,0},{8,12},{12,8},{16,20},{20,16},{24,28},{28,24},{1,5},{5... | collective-permute-start | bytes 3538952 | tf_op jit(solution)/shard_map/ppermute | solution.py:1136
  371.2 24.4 %collective-permute-start.42 = (bf16[768,384]{1,0:T(8,128)(2,1)}, bf16[768,384]{1,0:T(8,128)(2,1)}, u32[]{:S(2)}, u32[]{:S(2)}) collective-permute-start(bf16[768,384]{1,0:T(8,128)(2,1)} %get-tuple-element.351), channel_id=1, source_target_pairs={{0,8},{4,12},{24,16},{28,20},{1,9},{5,13},{25,17},{29,21},{2,10},{... | collective-permute-start | bytes 1769480 | tf_op jit(solution)/shard_map/ppermute | solution.py:1144
  377.7 20.6 %collective-permute-start.46 = (f32[4,4964]{1,0:T(4,128)S(1)}, f32[4,4964]{1,0:T(4,128)S(1)}, u32[]{:S(2)}, u32[]{:S(2)}) collective-permute-start(f32[4,4964]{1,0:T(4,128)S(1)} %copy-done.22), channel_id=1, source_target_pairs={{0,4},{4,0},{8,12},{12,8},{16,20},{20,16},{24,28},{28,24},{1,5},{5... | collective-permute-start | bytes 238280 | tf_op jit(solution)/shard_map/ppermute | solution.py:1136
  397.6 20.2 %collective-permute-start.47 = (bf16[768,384]{1,0:T(8,128)(2,1)}, bf16[768,384]{1,0:T(8,128)(2,1)S(1)}, u32[]{:S(2)}, u32[]{:S(2)}) collective-permute-start(bf16[768,384]{1,0:T(8,128)(2,1)} %add_convert_fusion.11), channel_id=1, source_target_pairs={{8,16},{12,20},{16,8},{20,12},{9,17},{13,21},{17,9},{21,13},{10,18... | collective-permute-start | bytes 1769480 | tf_op jit(solution)/shard_map/ppermute | solution.py:1144
  400.8 24.6 %collective-permute-start.48 = (bf16[1536,384]{1,0:T(8,128)(2,1)}, bf16[1536,384]{1,0:T(8,128)(2,1)}, u32[]{:S(2)}, u32[]{:S(2)}) collective-permute-start(bf16[1536,384]{1,0:T(8,128)(2,1)} %broadcast_select_fusion.2.own), channel_id=1, source_target_pairs={{0,4},{4,0},{8,12},{12,8},{16,20},{20,16},{24,28},{28,24},{1,5},{5... | collective-permute-start | bytes 3538952 | tf_op jit(solution)/shard_map/ppermute | solution.py:1136
  403.6 21.9 %collective-permute-start.52 = (bf16[1024,384]{1,0:T(8,128)(2,1)}, bf16[1024,384]{1,0:T(8,128)(2,1)}, u32[]{:S(2)}, u32[]{:S(2)}) collective-permute-start(bf16[1024,384]{1,0:T(8,128)(2,1)} %add_convert_fusion.8), channel_id=1, source_target_pairs={{8,0},{12,4},{16,24},{20,28},{9,1},{13,5},{17,25},{21,29},{10,2},{... | collective-permute-start | bytes 2359304 | tf_op jit(solution)/shard_map/ppermute | solution.py:1144
  405.6 15.5 %collective-permute-start.49 = (f32[1,4964]{1,0:T(1,128)S(1)}, f32[1,4964]{1,0:T(1,128)S(1)}, u32[]{:S(2)}, u32[]{:S(2)}) collective-permute-start(f32[1,4964]{1,0:T(1,128)S(1)} %get-tuple-element.362), channel_id=1, source_target_pairs={{0,1},{1,0},{2,3},{3,2},{4,5},{5,4},{6,7},{7,6},{8,9},{9,8},{10,11... | collective-permute-start | bytes 59576 | tf_op jit(solution)/shard_map/ppermute | solution.py:1140
  407.1 14.0 %collective-permute-start.50 = (f32[1,4964]{1,0:T(1,128)S(1)}, f32[1,4964]{1,0:T(1,128)S(1)}, u32[]{:S(2)}, u32[]{:S(2)}) collective-permute-start(f32[1,4964]{1,0:T(1,128)S(1)} %get-tuple-element.361), channel_id=1, source_target_pairs={{0,2},{1,3},{2,0},{3,1},{4,6},{5,7},{6,4},{7,5},{8,10},{9,11},{10,... | collective-permute-start | bytes 59576 | tf_op jit(solution)/shard_map/ppermute | solution.py:1140
  418.7 4.7 collective-permute-start.51
  427.5 25.5 %collective-permute-start.60 = (bf16[768,384]{1,0:T(8,128)(2,1)}, bf16[768,384]{1,0:T(8,128)(2,1)}, u32[]{:S(2)}, u32[]{:S(2)}) collective-permute-start(bf16[768,384]{1,0:T(8,128)(2,1)} %add_convert_fusion.10), channel_id=1, source_target_pairs={{8,0},{12,4},{16,24},{20,28},{9,1},{13,5},{17,25},{21,29},{10,2},{... | collective-permute-start | bytes 1769480 | tf_op jit(solution)/shard_map/ppermute | solution.py:1144
  430.2 19.0 %collective-permute-start.61 = (bf16[1024,384]{1,0:T(8,128)(2,1)S(1)}, bf16[1024,384]{1,0:T(8,128)(2,1)}, u32[]{:S(2)}, u32[]{:S(2)}) collective-permute-start(bf16[1024,384]{1,0:T(8,128)(2,1)S(1)} %broadcast_select_fusion.4.refs_0_), channel_id=1, source_target_pairs={{0,4},{4,0},{8,12},{12,8},{16,20},{20,16},{24,28},{28,24},{1,5},{5... | collective-permute-start | bytes 2359304 | tf_op jit(solution)/shard_map/ppermute | solution.py:1136
  430.8 8.3 %collective-permute-start.54 = (f32[1,384]{1,0:T(1,128)S(1)}, f32[1,384]{1,0:T(1,128)S(1)}, u32[]{:S(2)}, u32[]{:S(2)}) collective-permute-start(f32[1,384]{1,0:T(1,128)S(1)} %get-tuple-element.369), channel_id=1, source_target_pairs={{0,1},{1,0},{2,3},{3,2},{4,5},{5,4},{6,7},{7,6},{8,9},{9,8},{10,11... | collective-permute-start | bytes 4616 | tf_op jit(solution)/shard_map/ppermute | solution.py:1140
  432.3 11.2 %collective-permute-start.55 = (f32[1,384]{1,0:T(1,128)S(1)}, f32[1,384]{1,0:T(1,128)S(1)}, u32[]{:S(2)}, u32[]{:S(2)}) collective-permute-start(f32[1,384]{1,0:T(1,128)S(1)} %get-tuple-element.368), channel_id=1, source_target_pairs={{0,2},{1,3},{2,0},{3,1},{4,6},{5,7},{6,4},{7,5},{8,10},{9,11},{10,... | collective-permute-start | bytes 4616 | tf_op jit(solution)/shard_map/ppermute | solution.py:1140
  433.4 11.5 %collective-permute-start.56 = (f32[1,384]{1,0:T(1,128)S(1)}, f32[1,384]{1,0:T(1,128)S(1)}, u32[]{:S(2)}, u32[]{:S(2)}) collective-permute-start(f32[1,384]{1,0:T(1,128)S(1)} %get-tuple-element.367), channel_id=1, source_target_pairs={{0,3},{1,2},{2,1},{3,0},{4,7},{5,6},{6,5},{7,4},{8,11},{9,10},{10,... | collective-permute-start | bytes 4616 | tf_op jit(solution)/shard_map/ppermute | solution.py:1140
  439.0 6.2 %collective-permute-start.58 = (f32[1,4964]{1,0:T(1,128)S(1)}, f32[1,4964]{1,0:T(1,128)S(1)}, u32[]{:S(2)}, u32[]{:S(2)}) collective-permute-start(f32[1,4964]{1,0:T(1,128)S(1)} %add_add_fusion), channel_id=1, source_target_pairs={{0,16},{4,20},{8,24},{12,28},{16,0},{20,4},{24,8},{28,12},{1,17},{... | collective-permute-start | bytes 59576 | tf_op jit(solution)/shard_map/ppermute | solution.py:1144
  443.5 5.6 %collective-permute-start.59 = (f32[1,4964]{1,0:T(1,128)S(1)}, f32[1,4964]{1,0:T(1,128)S(1)}, u32[]{:S(2)}, u32[]{:S(2)}) collective-permute-start(f32[1,4964]{1,0:T(1,128)S(1)} %add_add_fusion), channel_id=1, source_target_pairs={{0,24},{4,28},{8,16},{12,20},{16,8},{20,12},{24,0},{28,4},{1,25},{... | collective-permute-start | bytes 59576 | tf_op jit(solution)/shard_map/ppermute | solution.py:1144
  444.9 4.2 collective-permute-start.57
  454.2 9.7 %collective-permute-start.65 = (bf16[768,384]{1,0:T(8,128)(2,1)S(1)}, bf16[768,384]{1,0:T(8,128)(2,1)S(1)}, u32[]{:S(2)}, u32[]{:S(2)}) collective-permute-start(bf16[768,384]{1,0:T(8,128)(2,1)S(1)} %broadcast_select_fusion.5.refs_0_), channel_id=1, source_target_pairs={{0,4},{4,0},{8,12},{12,8},{16,20},{20,16},{24,28},{28,24},{1,5},{5... | collective-permute-start | bytes 1769480 | tf_op jit(solution)/shard_map/ppermute | solution.py:1136
  457.1 6.0 %collective-permute-start.63 = (f32[1,384]{1,0:T(1,128)S(1)}, f32[1,384]{1,0:T(1,128)S(1)}, u32[]{:S(2)}, u32[]{:S(2)}) collective-permute-start(f32[1,384]{1,0:T(1,128)S(1)} %fusion.9), channel_id=1, source_target_pairs={{0,16},{4,20},{8,24},{12,28},{16,0},{20,4},{24,8},{28,12},{1,17},{... | collective-permute-start | bytes 4616 | tf_op jit(solution)/shard_map/ppermute | solution.py:1144
  457.9 5.4 %collective-permute-start.64 = (f32[1,384]{1,0:T(1,128)S(1)}, f32[1,384]{1,0:T(1,128)S(1)}, u32[]{:S(2)}, u32[]{:S(2)}) collective-permute-start(f32[1,384]{1,0:T(1,128)S(1)} %fusion.9), channel_id=1, source_target_pairs={{0,24},{4,28},{8,16},{12,20},{16,8},{20,12},{24,0},{28,4},{1,25},{... | collective-permute-start | bytes 4616 | tf_op jit(solution)/shard_map/ppermute | solution.py:1144
  459.2 4.0 collective-permute-start.62
  (47 other events, 303.6 us)

commit v2 on v1

--- a/solution.py
+++ b/solution.py
@@ -949,7 +949,7 @@
     step = pl.program_id(0)
 
     if last:
-        hidden, out_grad, scale, gain, result, gain_grad, weight, weight_dt, total, folded = refs
+        hidden, out_grad, scale, gain, result, weight, weight_dt, total = refs
     else:
         total, weight = refs
 
@@ -986,8 +986,6 @@
     @pl.when(step == pl.num_programs(0) - 1)
     def _():
         tokens, width = hidden.shape
-        folded[...] = jnp.zeros_like(folded)
-
         def finish(n, carry):
             rows = pl.ds(pl.multiple_of(n * 32, 32), 32)
             r = jnp.broadcast_to(scale[rows, :], (32, LANES))
@@ -995,7 +993,6 @@
             for at in range(0, width, LANES):
                 cut = slice(at, at + LANES)
                 both = total[rows, cut] * hidden[rows, cut].astype(F32)
-                folded[:, cut] += fold(both * r)
                 sums = sums + both * gain[:, cut]
             mean = jnp.sum(sums, axis=1, keepdims=True) / width
             factor = r * r * r * mean
@@ -1006,7 +1003,6 @@
             return carry
 
         lax.fori_loop(0, tokens // 32, finish, 0)
-        gain_grad[...] = jnp.sum(folded[...], axis=0, keepdims=True)
 
 
 def input_backward(meta, start, parts, tokens, width, last=None):
@@ -1056,11 +1052,8 @@
     if last is not None:
         more = tuple(last)
         more_specs = [whole((tokens, width))] * 2 + [whole((tokens, 1)), whole((1, width))]
-        outs.append(shape_of((1, width)))
-        out_specs.append(whole((1, width)))
         scratch += [
             pltpu.VMEM((LANES, width), BF), pltpu.VMEM((tokens, width), F32),
-            pltpu.VMEM((8, width), F32),
         ]
     first = start is None
     return call(
@@ -1073,17 +1066,29 @@
     )
 
 
-def place_body(halves, last, meta, own, other, out):
+def place_body(halves, last, meta, own, other, weight, out, sums):
     step = pl.program_id(0)
 
-    def put(which, row, rows, at):
+    @pl.when(step == 0)
+    def _():
+        sums[...] = jnp.zeros_like(sums)
+
+    def copy(source, row, rows, at, counted):
+        for k in range(0, rows, LANES):
+            part = source[row + k : row + k + LANES, :].astype(F32)
+            out[at + k : at + k + LANES, :] = part
+            some = min(counted, LANES)
+            part = part[:some] * weight[at + k : at + k + some, :].astype(F32)
+            sums[...] += fold(part)
+
+    def put(which, row, rows, at, counted=LANES):
         @pl.when(meta[0] == which)
         def _():
-            out[at : at + rows, :] = own[row : row + rows, :].astype(F32)
+            copy(own, row, rows, at, counted)
 
         @pl.when(meta[0] != which)
         def _():
-            out[at : at + rows, :] = other[row : row + rows, :].astype(F32)
+            copy(other, row, rows, at, counted)
 
     for half in range(2):
         @pl.when(step == half)
@@ -1095,17 +1100,18 @@
         def _():
             put(0, halves, LANES, 0)
             put(1, halves, LANES, LANES)
-            put(0, halves + LANES, LANES, 2 * LANES)
-
-
-def place_rows(meta, own, other, halves, first, total, filled, last):
+            put(0, halves + LANES, LANES, 2 * LANES, HEADS)
+
+
+def place_rows(meta, own, other, weight, halves, first, filled, last):
     length, width = own.shape
+    rows = pl.BlockSpec((halves, width), lambda i, meta: (first + i, 0))
     return call(
-        functools.partial(place_body, halves, last), "place_rows", meta, (own, other),
-        [whole((length, width)), whole((length, width))],
-        shape_of((total, width)),
-        pl.BlockSpec((halves, width), lambda i, meta: (first + i, 0)),
-        [], 3 if last else 2, 1, 1, None if filled is None else {0: filled},
+        functools.partial(place_body, halves, last), "place_rows", meta, (own, other, weight),
+        [whole((length, width)), whole((length, width)), rows],
+        [shape_of(weight.shape), shape_of((8, width))],
+        [rows, whole((8, width))],
+        [], 3 if last else 2, 10**10, 20 * MIB, None if filled is None else {0: filled},
     )
 
 
@@ -1521,8 +1527,15 @@
     near_line = outward((near_inner, near_arrived))
     gate_total = summed((gate_done, gate_arrived))
     gate_other = swap(gate_total)
-    far_inner, near_done, gate_total, partial = hold((far_inner, near_line[0], gate_total, partial))
-    hidden_grad, grad_gain_one = input_backward(
+    far_inner, near_done, gate_total, gate_other, partial = hold(
+        (far_inner, near_line[0], gate_total, gate_other, partial)
+    )
+    rows_so_far, sums_one = place_rows(meta, gate_total, gate_other, local, DI // 2, 0, None, False)
+    rows_so_far, far_arrived, spread_rows = hold((rows_so_far, far_line[1], spread_rows))
+    far_line = outward((far_inner, far_arrived))
+    far_done, partial, spread_rows = hold((far_line[0], partial, spread_rows))
+    row = chips_sum(add_up(spread_rows))[0]
+    (hidden_grad,) = input_backward(
         meta, partial,
         [
             (grad_keys, 0, 1, None, conv_own, DI // 2 // TILE, None, 0, 0),
@@ -1530,30 +1543,21 @@
         ],
         tokens, width, (hidden, out_grad, inv_rms, gain_one[None]),
     )
-    grad_gain_one, far_arrived, gate_other, spread_rows, near_arrived = hold(
-        (grad_gain_one, far_line[1], gate_other, spread_rows, near_line[1])
-    )
-    far_line = outward((far_inner, far_arrived))
-    row = chips_sum(add_up(spread_rows))[0]
-    far_done, grad_gain_one, gate_other = hold((far_line[0], grad_gain_one, gate_other))
-    vector = grad_gain_one[0].reshape(count, -1)
-    gain_row = add_up(group_rows(vector + swap(vector), shard, count))
-    all_rows = local.shape[0]
-    rows_so_far = place_rows(meta, gate_total, gate_other, DI // 2, 0, all_rows, None, False)
+    hidden_grad, near_arrived, row = hold((hidden_grad, near_line[1], row))
     near_total = summed((near_done, near_arrived))
     near_other = swap(near_total)
-    wide = near // 2 * TILE
-    rows_so_far = place_rows(
-        meta, near_total, near_other, wide, DI // wide, all_rows, rows_so_far, False
-    )
-    gain_row, row, far_arrived, rows_so_far = hold((gain_row, row, far_line[1], rows_so_far))
-    gain_row = chips_sum(gain_row)[0]
+    near_total, far_arrived = hold((near_total, far_line[1]))
     far_total = summed((far_done, far_arrived))
     far_other = swap(far_total)
+    wide = near // 2 * TILE
+    rows_so_far, sums_two = place_rows(
+        meta, near_total, near_other, local, wide, DI // wide, rows_so_far, False
+    )
     wide = far // 2 * TILE
-    rows_so_far = place_rows(
-        meta, far_total, far_other, wide, (DI + near * TILE) // wide, all_rows, rows_so_far, True
-    )
+    rows_so_far, sums_three = place_rows(
+        meta, far_total, far_other, local, wide, (DI + near * TILE) // wide, rows_so_far, True
+    )
+    gain_row = jnp.sum(sums_one + sums_two + sums_three, axis=0) / norm_gain.astype(F32)
     in_w_grad = rows_so_far.T
 
     out_w_grad = jnp.concatenate(

time: 474 us -> 463 us (0.977)
  starting transfers between devices: 80.6 us -> 73.8 us
  waiting for transfers between devices: 63.6 us -> 58 us
    ppermute x18 -> x15, starting transfers between devices: 43.6 us -> 40.8 us  [along(): lax.ppermute(x, 'rep', [(2 * a + k, 2 * b + k) for a, b in pairs for k in...]
    unnamed x96 -> x86, local copies, waits for them, and re-layouts: 11.7 us -> 11.9 us
  transfers between devices with their start and end apart: 66 -> 59, of which waited for: 17 -> 13; matrix products, arithmetic and copies ran while one was open for 15% -> 16% of each run, Pallas kernels for 46% -> 47%
where the time goes in v2:
time: 463 us; the launch traced here: 457 us
  Pallas kernels  231 us (50%)
  starting transfers between devices  73.8 us (16%)
  waiting for transfers between devices  58 us (13%)
  other arithmetic  54.2 us (12%)
  local copies, waits for them, and re-layouts  37.7 us (8%)
    pallas_call x19, Pallas kernels, call(): pl.pallas_call(body, name=name, grid_spec=pltpu.PrefetchScalarGridSpec(nu...  231 us
    ppermute x17, waiting for transfers between devices, hop(): return lax.ppermute(x, ('rep', 'shard'), pairs)  44.1 us
    ppermute x15, starting transfers between devices, along(): lax.ppermute(x, 'rep', [(2 * a + k, 2 * b + k) for a, b in pairs for k in...  40.8 us
    ppermute x17, starting transfers between devices, hop(): return lax.ppermute(x, ('rep', 'shard'), pairs)  22 us
    unnamed x86, local copies, waits for them, and re-layouts  11.9 us
    convert_element_type x4, other arithmetic, inward(): return (held, along(held.astype(BF), [(0, 1), (3, 2)]))  11 us
  transfers between devices with their start and end apart: 59, of which 13 were waited for; matrix products, arithmetic and copies ran while one was open for 16% of the time, Pallas kernels for 47%

profile of v2, /device:TPU:0, one launch (start us, length us, event | category | flops | bytes accessed | tf_op | source)
XLA Modules:
  0.0 457.3 jit_solution(7217475486756738635)
XLA Ops:
  1.6 2.9 dynamic-slice_bitcast_fusion
  5.0 3.0 collective-permute-start
  8.0 1.5 collective-permute-start.1
  9.8 2.0 collective-permute-start.6
  11.8 1.5 collective-permute-start.5
  14.0 25.6 %collective-permute-done.refs_1_.refs_9_.refs_13_.refs_5_.refs_21_.refs_4_.refs_8_ = bf16[1856,384]{1,0:T(8,128)(2,1)S(1)} collective-permute-done((bf16[1856,384]{1,0:T(8,128)(2,1)S(1)}, bf16[1856,384]{1,0:T(8,128)(2,1)S(1)}, u32[]{:S(2)}, u32[]{:S(2)}) %collective-permute-start) | collective-permute-done | bytes 1425440 | tf_op jit(solution)/shard_map/ppermute | solution.py:1138
  39.5 1.8 collective-permute-start.2
  41.4 1.8 fusion
  46.2 12.3 %collective-permute-done.2.refs_3_.refs_11_.refs_15_.refs_7_.refs_23_.refs_6_.refs_10_ = bf16[1856,384]{1,0:T(8,128)(2,1)} collective-permute-done((bf16[1856,384]{1,0:T(8,128)(2,1)S(1)}, bf16[1856,384]{1,0:T(8,128)(2,1)}, u32[]{:S(2)}, u32[]{:S(2)}) %collective-permute-start.2) | collective-permute-done | bytes 1425440 | tf_op jit(solution)/shard_map/ppermute | solution.py:1138
  59.7 2.5 collective-permute-start.3
  64.1 3.0 fusion.2.x.refs_2_.refs_4_
  68.1 24.5 %conv_forward.1 = (bf16[512,3072]{1,0:T(8,128)(2,1)}, bf16[512,3072]{1,0:T(8,128)(2,1)}, f32[512,3072]{1,0:T(8,128)}, bf16[512,256]{1,0:T(8,128)(2,1)}, bf16[512...) custom-call(s32[20]{0:T(128)} %stack.90.meta, ...), custom_call_target="tpu_custom_call" | custom-call | flops 5234491392 | bytes 25165824 | tf_op jit(solution)/shard_map/conv_forward/pallas_call | solution.py:91
  93.8 2.4 constant_dynamic-slice_fusion.4
  97.5 9.2 %scan_forward.2 = (f32[512,3072]{1,0:T(8,128)}, bf16[12,128,256]{2,1,0:T(8,128)(2,1)}) custom-call(s32[20]{0:T(128)} %stack.90.meta, bf16[512,3072]{1,0:T(8,128)(2,1)} %get-tuple-element.186.content.refs_0_, bf16[512,256]{1,0:T(8,128)(2,1)} %get-tuple-element.187.keys.refs_1_.refs_0_, f32[12,512,16]{2,1,0:T(8,128)} %get-tuple-element.188.columns.refs_2_, ...), custom_call_target="tpu_custom_call" | custom-call | flops 6000000000 | bytes 6291456 | tf_op jit(solution)/shard_map/scan_forward/pallas_call | solution.py:91
  106.8 2.5 collective-permute-done.11.refs_3_.refs_5_.refs_13_
  111.3 9.1 %scan_forward.3 = (f32[512,3072]{1,0:T(8,128)}, bf16[12,128,256]{2,1,0:T(8,128)(2,1)}) custom-call(s32[20]{0:T(128)} %stack.90.meta, bf16[512,3072]{1,0:T(8,128)(2,1)} %get-tuple-element.186.content.refs_0_, bf16[512,256]{1,0:T(8,128)(2,1)} %get-tuple-element.187.keys.refs_1_.refs_0_, ...), custom_call_target="tpu_custom_call", output_to_operand_aliasing={{0}: (6, {}), {1}: (7, {})} | custom-call | flops 6000000000 | bytes 6291456 | tf_op jit(solution)/shard_map/scan_forward/pallas_call | solution.py:91
  121.5 17.1 %gate_forward.1 = (bf16[512,3072]{1,0:T(8,128)(2,1)}, bf16[512,3072]{1,0:T(8,128)(2,1)}, bf16[512,1536]{1,0:T(8,128)(2,1)}, f32[512,1]{1,0:T(8,128)}) custom-call(s32[20]{0:T(128)} %stack.90.meta, bf16[512,1536]{1,0:T(8,128)(2,1)} %fusion.2.x.refs_2_.refs_4_, f32[512,3072]{1,0:T(8,128)} %get-tuple-element.195.mixed, f32[1,3072]{1,0:T(1,128)} %bitcast.78, ...), custom_call_target="tpu_custom_call" | custom-call | flops 4831838208 | bytes 29360128 | tf_op jit(solution)/shard_map/gate_forward/pallas_call | solution.py:91
  140.3 2.2 collective-permute-done.17.theirs
  142.5 11.1 %rows_product.1 = (bf16[2,384,1536]{2,1,0:T(8,128)(2,1)}, bf16[2,384,1536]{2,1,0:T(8,128)(2,1)}) custom-call(s32[20]{0:T(128)} %stack.90.meta, bf16[512,3072]{1,0:T(8,128)(2,1)} %get-tuple-element.203.mine.refs_0_.refs_1_, bf16[512,1536]{1,0:T(8,128)(2,1)} %collective-permute-done.17.theirs, bf16[512,1536]{1,0:T(8,128)(2,1)} %copy-done.10, ...), custom_call_target="tpu_custom_call" | custom-call | flops 4831838208 | bytes 12582912 | tf_op jit(solution)/shard_map/rows_product/pallas_call | solution.py:91
  155.8 1.9 collective-permute-done.20.refs_9_
  157.7 3.4 collective-permute-done.21.refs_10_
  162.1 21.5 %out_forward.1 = (bf16[512,1536]{1,0:T(8,128)(2,1)}, bf16[512,3072]{1,0:T(8,128)(2,1)}, f32[512,128]{1,0:T(8,128)}) custom-call(s32[20]{0:T(128)} %stack.90.meta, bf16[512,3072]{1,0:T(8,128)(2,1)} %get-tuple-element.203.mine.refs_0_.refs_1_, bf16[512,3072]{1,0:T(8,128)(2,1)} %get-tuple-element.203.mine.refs_0_.refs_1_, bf16[512,1536]{1,0:T(8,128)(2,1)} %copy-done.10, ...), custom_call_target="tpu_custom_call" | custom-call | flops 9663676416 | bytes 25165824 | tf_op jit(solution)/shard_map/out_forward/pallas_call | solution.py:91
  183.6 2.3 add_convert_fusion.1
  187.1 1.5 collective-permute-start.24
  188.6 12.1 %norm_back.1 = (bf16[512,3072]{1,0:T(8,128)(2,1)}, bf16[512,1536]{1,0:T(8,128)(2,1)}, bf16[512,3072]{1,0:T(8,128)(2,1)}, f32[8,3072]{1,0:T(8,128)}) custom-call(s32[20]{0:T(128)} %stack.90.meta, bf16[512,3072]{1,0:T(8,128)(2,1)} %get-tuple-element.210.back, f32[512,128]{1,0:T(8,128)} %get-tuple-element.216.total, f32[512,3072]{1,0:T(8,128)} %get-tuple-element.195.mixed, ...), custom_call_target="tpu_custom_call" | custom-call | flops 1000000000 | bytes 25165824 | tf_op jit(solution)/shard_map/norm_back/pallas_call | solution.py:91
  200.7 2.5 collective-permute-done.24
  204.8 3.8 fusion.11
  208.6 1.5 collective-permute-done.25.refs_1_
  212.4 10.7 %columns_product.3 = (bf16[2,1536,384]{2,1,0:T(8,128)(2,1)}, bf16[2,1536,384]{2,1,0:T(8,128)(2,1)}) custom-call(s32[20]{0:T(128)} %stack.90.meta, bf16[512,3072]{1,0:T(8,128)(2,1)} %get-tuple-element.281.refs_0_.refs_1_, bf16[512,1536]{1,0:T(8,128)(2,1)} %copy-done.11, bf16[512,1536]{1,0:T(8,128)(2,1)} %fusion.2.x.refs_2_.refs_4_, bf16[512,1536]{1,0:T(8,128)(2,1)} %copy-done.4), custom_call_target="tpu_custom_call" | custom-call | flops 1 | bytes 1 | tf_op jit(solution)/shard_map/columns_product/pallas_call | solution.py:91
  224.1 3.6 collective-permute-start.28
  229.2 22.7 %scan_backward.2 = (bf16[512,2048]{1,0:T(8,128)(2,1)}, bf16[512,1024]{1,0:T(8,128)(2,1)}, f32[8,2048]{1,0:T(8,128)}, f32[8,512,8]{2,1,0:T(8,128)}, f32[2,256,256...) custom-call(s32[20]{0:T(128)} %stack.90.meta, bf16[512,3072]{1,0:T(8,128)(2,1)} %get-tuple-element.186.content.refs_0_, ...), custom_call_target="tpu_custom_call" | custom-call | flops 24000000000 | bytes 8388608 | tf_op jit(solution)/shard_map/scan_backward/pallas_call | solution.py:91
  251.9 1.7 collective-permute-done.28
  254.7 2.2 add_convert_fusion
  259.7 1.7 collective-permute-start.36
  261.4 8.4 %columns_product.4 = (bf16[2,1024,384]{2,1,0:T(8,128)(2,1)}, bf16[2,1024,384]{2,1,0:T(8,128)(2,1)}) custom-call(s32[20]{0:T(128)} %stack.90.meta, bf16[512,2048]{1,0:T(8,128)(2,1)} %get-tuple-element.242.refs_0_.refs_1_, bf16[512,1024]{1,0:T(8,128)(2,1)} %collective-permute-done.29.refs_1_, bf16[512,1536]{1,0:T(8,128)(2,1)} %fusion.2.x.refs_2_.refs_4_, ...), custom_call_target="tpu_custom_call" | custom-call | flops 1 | bytes 1 | tf_op jit(solution)/shard_map/columns_product/pallas_call | solution.py:91
  270.7 13.2 %scan_backward.3 = (bf16[512,1024]{1,0:T(8,128)(2,1)}, bf16[512,512]{1,0:T(8,128)(2,1)}, f32[8,1024]{1,0:T(8,128)}, f32[4,512,8]{2,1,0:T(8,128)}, f32[2,256,256]...) custom-call(s32[20]{0:T(128)} %stack.90.meta, bf16[512,3072]{1,0:T(8,128)(2,1)} %get-tuple-element.186.content.refs_0_, ...), custom_call_target="tpu_custom_call" | custom-call | flops 12000000000 | bytes 4194304 | tf_op jit(solution)/shard_map/scan_backward/pallas_call | solution.py:91
  285.0 2.9 fusion.12
  287.9 7.2 %collective-permute-start.34 = (bf16[1536,384]{1,0:T(8,128)(2,1)}, bf16[1536,384]{1,0:T(8,128)(2,1)}, u32[]{:S(2)}, u32[]{:S(2)}) collective-permute-start(bf16[1536,384]{1,0:T(8,128)(2,1)} %get-tuple-element.353), channel_id=1, source_target_pairs={{0,8},{4,12},{24,16},{28,20},{1,9},{5,13},{25,17},{29,21},{2,10},{... | collective-permute-start | bytes 3538952 | tf_op jit(solution)/shard_map/ppermute | solution.py:1150
  295.1 6.6 %tail_backward.1 = (bf16[512,256]{1,0:T(8,128)(2,1)}, f32[8,256]{1,0:T(8,128)}, bf16[512,128]{1,0:T(8,128)(2,1)}, f32[8,128]{1,0:T(8,128)}, bf16[2,512,256]{2,1,0:T(8,128)(2,1)}) custom-call(s32[20]{0:T(128)} %stack.90.meta, bf16[512,256]{1,0:T(8,128)(2,1)} %get-tuple-element.187.keys.refs_1_.refs_0_, bf16[512,256]{1,0:T(8,128)(2,1)} %get-tuple-element.207.refs_1_, ...), custom_call_target="tpu_custom_call" | custom-call | flops 1 | bytes 1 | tf_op jit(solution)/shard_map/tail_backward/pallas_call | solution.py:91
  301.7 2.3 add_convert_fusion.2
  309.0 1.7 slice_bitcast_fusion.refs_1_
  310.6 7.5 %columns_product.5 = (bf16[2,768,384]{2,1,0:T(8,128)(2,1)}, bf16[2,768,384]{2,1,0:T(8,128)(2,1)}) custom-call(s32[20]{0:T(128)} %stack.90.meta, bf16[512,1024]{1,0:T(8,128)(2,1)} %get-tuple-element.264.refs_0_.refs_2_, bf16[512,256]{1,0:T(8,128)(2,1)} %slice_bitcast_fusion.refs_1_, bf16[512,512]{1,0:T(8,128)(2,1)} %collective-permute-done.33.refs_2_, ...), custom_call_target="tpu_custom_call" | custom-call | flops 1 | bytes 1 | tf_op jit(solution)/shard_map/columns_product/pallas_call | solution.py:91
  319.1 2.5 add_convert_fusion.6
  322.5 2.6 add_convert_fusion.5
  326.4 2.2 fusion.10
  328.6 6.9 %collective-permute-start.39 = (bf16[1024,384]{1,0:T(8,128)(2,1)}, bf16[1024,384]{1,0:T(8,128)(2,1)}, u32[]{:S(2)}, u32[]{:S(2)}) collective-permute-start(bf16[1024,384]{1,0:T(8,128)(2,1)} %get-tuple-element.361), channel_id=1, source_target_pairs={{0,8},{4,12},{24,16},{28,20},{1,9},{5,13},{25,17},{29,21},{2,10},{... | collective-permute-start | bytes 2359304 | tf_op jit(solution)/shard_map/ppermute | solution.py:1150
  335.5 16.1 %input_backward.3.refs_3_ = f32[512,1536]{1,0:T(8,128)} custom-call(s32[20]{0:T(128)} %stack.90.meta, bf16[512,3072]{1,0:T(8,128)(2,1)} %get-tuple-element.281.refs_0_.refs_1_, bf16[512,3072]{1,0:T(8,128)(2,1)} %get-tuple-element.281.refs_0_.refs_1_, bf16[1536,384]{1,0:T(8,128)(2,1)} %get-tuple-element.179.refs_0_.refs_2_.refs_10_, ...), custom_call_target="tpu_custom_call" | custom-call | flops 10000000000 | bytes 20971520 | tf_op jit(solution)/shard_map/input_backward/pallas_call | solution.py:91
  351.7 1.9 add_convert_fusion.4
  354.5 1.5 collective-permute-start.38
  360.3 2.2 add_convert_fusion.9
  362.4 1.5 collective-permute-start.43
  364.7 2.0 fusion.9
  366.8 1.6 add_convert_fusion.3
  371.1 6.4 %collective-permute-start.42 = (bf16[768,384]{1,0:T(8,128)(2,1)}, bf16[768,384]{1,0:T(8,128)(2,1)}, u32[]{:S(2)}, u32[]{:S(2)}) collective-permute-start(bf16[768,384]{1,0:T(8,128)(2,1)} %get-tuple-element.365), channel_id=1, source_target_pairs={{0,8},{4,12},{24,16},{28,20},{1,9},{5,13},{25,17},{29,21},{2,10},{... | collective-permute-start | bytes 1769480 | tf_op jit(solution)/shard_map/ppermute | solution.py:1150
  377.7 17.7 %input_backward.4.refs_2_ = f32[512,1536]{1,0:T(8,128)} custom-call(s32[20]{0:T(128)} %stack.90.meta, bf16[512,2048]{1,0:T(8,128)(2,1)} %get-tuple-element.242.refs_0_.refs_1_, bf16[512,2048]{1,0:T(8,128)(2,1)} %get-tuple-element.242.refs_0_.refs_1_, bf16[512,1024]{1,0:T(8,128)(2,1)} %get-tuple-element.264.refs_0_.refs_2_, ...), custom_call_target="tpu_custom_call" | custom-call | flops 10000000000 | bytes 20971520 | tf_op jit(solution)/shard_map/input_backward/pallas_call | solution.py:91
  401.7 1.5 collective-permute-start.49
  405.2 2.5 add_convert_fusion.8
  411.4 5.1 %place_rows.3 = (f32[6448,384]{1,0:T(8,128)}, f32[8,384]{1,0:T(8,128)}) custom-call(s32[20]{0:T(128)} %stack.90.meta, bf16[1536,384]{1,0:T(8,128)(2,1)} %copy-done.12, bf16[1536,384]{1,0:T(8,128)(2,1)} %copy-done.36, bf16[6448,384]{1,0:T(8,128)(2,1)} %bitcast.73), custom_call_target="tpu_custom_call" | custom-call | flops 10000000000 | bytes 20971520 | tf_op jit(solution)/shard_map/place_rows/pallas_call | solution.py:91
  418.5 4.6 %collective-permute-start.54 = (f32[1,4964]{1,0:T(1,128)S(1)}, f32[1,4964]{1,0:T(1,128)S(1)}, u32[]{:S(2)}, u32[]{:S(2)}) collective-permute-start(f32[1,4964]{1,0:T(1,128)S(1)} %add_add_fusion), channel_id=1, source_target_pairs={{0,16},{4,20},{8,24},{12,28},{16,0},{20,4},{24,8},{28,12},{1,17},{... | collective-permute-start | bytes 59576 | tf_op jit(solution)/shard_map/ppermute | solution.py:1150
  425.8 9.5 %input_backward.5 = f32[512,1536]{1,0:T(8,128)} custom-call(s32[20]{0:T(128)} %stack.90.meta, bf16[512,256]{1,0:T(8,128)(2,1)} %get-tuple-element.262.refs_0_, bf16[512,128]{1,0:T(8,128)(2,1)} %get-tuple-element.263.refs_1_, f32[512,1536]{1,0:T(8,128)} %input_backward.4.refs_2_, bf16[1856,384]{1,0:T(8,128)(2,1)} %copy-done, bf16[1856,384]{1,0:T(8,128)(2,1)} %copy-done.2, ...), custom_call_target="tpu_custom_call" | custom-call | flops 99999997952 | bytes 20971520 | tf_op jit(solution)/shard_map/input_backward/pallas_call | solution.py:91
  436.7 2.8 maximum_convert_fusion
  442.1 3.0 collective-permute-done.56
  446.4 4.1 place_rows.4
  451.4 4.4 place_rows.5
  (261 shorter events, 72.8 us)
Async XLA Ops:
  5.0 41.2 %copy-start = (bf16[1856,384]{1,0:T(8,128)(2,1)}, bf16[1856,384]{1,0:T(8,128)(2,1)S(1)}, u32[]{:S(2)}) copy-start(bf16[1856,384]{1,0:T(8,128)(2,1)S(1)} %maximum_maximum_fusion.refs_0_.refs_8_.refs_12_.refs_4_.refs_20_.refs_3_.refs_7_) | copy-start | bytes 4276228
  5.0 34.5 %collective-permute-start = (bf16[1856,384]{1,0:T(8,128)(2,1)S(1)}, bf16[1856,384]{1,0:T(8,128)(2,1)S(1)}, u32[]{:S(2)}, u32[]{:S(2)}) collective-permute-start(bf16[1856,384]{1,0:T(8,128)(2,1)S(1)} %maximum_maximum_fusion.refs_0_.refs_8_.refs_12_.refs_4_.refs_20_.refs_3_.refs_7_), channel_id=1, source_target_pairs={{0,1},{1,0},{2,3},{3,2},{4,6},{5,7},{6,4},{7,5},{8,9},{9,8},{10,11... | collective-permute-start | bytes 4276232 | tf_op jit(solution)/shard_map/ppermute | solution.py:1138
  8.0 38.2 %collective-permute-start.1 = (bf16[1856,384]{1,0:T(8,128)(2,1)S(1)}, bf16[1856,384]{1,0:T(8,128)(2,1)}, u32[]{:S(2)}, u32[]{:S(2)}) collective-permute-start(bf16[1856,384]{1,0:T(8,128)(2,1)S(1)} %maximum_maximum_fusion.refs_0_.refs_8_.refs_12_.refs_4_.refs_20_.refs_3_.refs_7_), channel_id=1, source_target_pairs={{0,2},{1,3},{2,0},{3,1},{4,5},{5,4},{6,7},{7,6},{8,10},{9,11},{10,... | collective-permute-start | bytes 4276232 | tf_op jit(solution)/shard_map/ppermute | solution.py:1138
  9.8 35.6 %collective-permute-start.7 = (bf16[5348]{0:T(1024)(128)(2,1)S(1)}, bf16[5348]{0:T(1024)(128)(2,1)S(1)}, u32[]{:S(2)}, u32[]{:S(2)}) collective-permute-start(bf16[5348]{0:T(1024)(128)(2,1)S(1)} %concatenate.29), channel_id=1, source_target_pairs={{0,3},{1,2},{2,1},{3,0},{4,7},{5,6},{6,5},{7,4},{8,11},{9,10},{10,... | collective-permute-start | bytes 32096 | tf_op jit(solution)/shard_map/ppermute | solution.py:1293
  9.8 35.6 %collective-permute-start.6 = (bf16[5348]{0:T(1024)(128)(2,1)S(1)}, bf16[5348]{0:T(1024)(128)(2,1)S(1)}, u32[]{:S(2)}, u32[]{:S(2)}) collective-permute-start(bf16[5348]{0:T(1024)(128)(2,1)S(1)} %concatenate.29), channel_id=1, source_target_pairs={{0,2},{1,3},{2,0},{3,1},{4,5},{5,4},{6,7},{7,6},{8,10},{9,11},{10,... | collective-permute-start | bytes 32096 | tf_op jit(solution)/shard_map/ppermute | solution.py:1293
  11.8 33.6 %collective-permute-start.5 = (bf16[5348]{0:T(1024)(128)(2,1)S(1)}, bf16[5348]{0:T(1024)(128)(2,1)S(1)}, u32[]{:S(2)}, u32[]{:S(2)}) collective-permute-start(bf16[5348]{0:T(1024)(128)(2,1)S(1)} %concatenate.29), channel_id=1, source_target_pairs={{0,1},{1,0},{2,3},{3,2},{4,6},{5,7},{6,4},{7,5},{8,9},{9,8},{10,11... | collective-permute-start | bytes 32096 | tf_op jit(solution)/shard_map/ppermute | solution.py:1293
  39.5 27.5 %copy-start.2 = (bf16[1856,384]{1,0:T(8,128)(2,1)}, bf16[1856,384]{1,0:T(8,128)(2,1)S(1)}, u32[]{:S(2)}) copy-start(bf16[1856,384]{1,0:T(8,128)(2,1)S(1)} %collective-permute-done.refs_1_.refs_9_.refs_13_.refs_5_.refs_21_.refs_4_.refs_8_) | copy-start | bytes 4276228
  39.5 18.9 %collective-permute-start.2 = (bf16[1856,384]{1,0:T(8,128)(2,1)S(1)}, bf16[1856,384]{1,0:T(8,128)(2,1)}, u32[]{:S(2)}, u32[]{:S(2)}) collective-permute-start(bf16[1856,384]{1,0:T(8,128)(2,1)S(1)} %collective-permute-done.refs_1_.refs_9_.refs_13_.refs_5_.refs_21_.refs_4_.refs_8_), channel_id=1, source_target_pairs={{0,2},{1,3},{2,0},{3,1},{4,5},{5,4},{6,7},{7,6},{8,10},{9,11},{10,... | collective-permute-start | bytes 4276232 | tf_op jit(solution)/shard_map/ppermute | solution.py:1138
  58.5 8.6 %collective-permute-start.8 = (bf16[1856,384]{1,0:T(8,128)(2,1)S(1)}, bf16[1856,384]{1,0:T(8,128)(2,1)S(1)}, u32[]{:S(2)}, u32[]{:S(2)}) collective-permute-start(bf16[1856,384]{1,0:T(8,128)(2,1)S(1)} %collective-permute-done.refs_1_.refs_9_.refs_13_.refs_5_.refs_21_.refs_4_.refs_8_), channel_id=1, source_target_pairs={{0,4},{4,0},{8,12},{12,8},{16,20},{20,16},{24,28},{28,24},{1,5},{5... | collective-permute-start | bytes 4276232 | tf_op jit(solution)/shard_map/ppermute | solution.py:1142
  58.5 8.6 %collective-permute-start.9 = (bf16[1856,384]{1,0:T(8,128)(2,1)}, bf16[1856,384]{1,0:T(8,128)(2,1)}, u32[]{:S(2)}, u32[]{:S(2)}) collective-permute-start(bf16[1856,384]{1,0:T(8,128)(2,1)} %collective-permute-done.1.refs_2_.refs_10_.refs_14_.refs_6_.refs_22_.refs_5_.refs_9_), channel_id=1, source_target_pairs={{0,4},{4,0},{8,12},{12,8},{16,20},{20,16},{24,28},{28,24},{1,5},{5... | collective-permute-start | bytes 4276232 | tf_op jit(solution)/shard_map/ppermute | solution.py:1142
  59.0 8.1 %collective-permute-start.10 = (bf16[1856,384]{1,0:T(8,128)(2,1)}, bf16[1856,384]{1,0:T(8,128)(2,1)}, u32[]{:S(2)}, u32[]{:S(2)}) collective-permute-start(bf16[1856,384]{1,0:T(8,128)(2,1)} %collective-permute-done.2.refs_3_.refs_11_.refs_15_.refs_7_.refs_23_.refs_6_.refs_10_), channel_id=1, source_target_pairs={{0,4},{4,0},{8,12},{12,8},{16,20},{20,16},{24,28},{28,24},{1,5},{5... | collective-permute-start | bytes 4276232 | tf_op jit(solution)/shard_map/ppermute | solution.py:1142
  59.7 32.9 %collective-permute-start.3 = (bf16[1536,384]{1,0:T(8,128)(2,1)}, bf16[1536,384]{1,0:T(8,128)(2,1)}, u32[]{:S(2)}, u32[]{:S(2)}) collective-permute-start(bf16[1536,384]{1,0:T(8,128)(2,1)} %get-tuple-element.179.refs_0_.refs_2_.refs_10_), channel_id=1, source_target_pairs={{0,1},{1,0},{2,3},{3,2},{4,6},{5,7},{6,4},{7,5},{8,9},{9,8},{10,11... | collective-permute-start | bytes 3538952 | tf_op jit(solution)/shard_map/ppermute | solution.py:1138
  62.2 30.4 %collective-permute-start.4 = (bf16[1536,384]{1,0:T(8,128)(2,1)}, bf16[1536,384]{1,0:T(8,128)(2,1)}, u32[]{:S(2)}, u32[]{:S(2)}) collective-permute-start(bf16[1536,384]{1,0:T(8,128)(2,1)} %get-tuple-element.179.refs_0_.refs_2_.refs_10_), channel_id=1, source_target_pairs={{0,2},{1,3},{2,0},{3,1},{4,5},{5,4},{6,7},{7,6},{8,10},{9,11},{10,... | collective-permute-start | bytes 3538952 | tf_op jit(solution)/shard_map/ppermute | solution.py:1138
  92.7 16.6 %collective-permute-start.11 = (bf16[1536,384]{1,0:T(8,128)(2,1)}, bf16[1536,384]{1,0:T(8,128)(2,1)}, u32[]{:S(2)}, u32[]{:S(2)}) collective-permute-start(bf16[1536,384]{1,0:T(8,128)(2,1)} %collective-permute-done.3.refs_1_.refs_3_.refs_11_), channel_id=1, source_target_pairs={{0,2},{1,3},{2,0},{3,1},{4,5},{5,4},{6,7},{7,6},{8,10},{9,11},{10,... | collective-permute-start | bytes 3538952 | tf_op jit(solution)/shard_map/ppermute | solution.py:1138
  97.0 23.5 %collective-permute-start.14 = (bf16[1536,384]{1,0:T(8,128)(2,1)}, bf16[1536,384]{1,0:T(8,128)(2,1)}, u32[]{:S(2)}, u32[]{:S(2)}) collective-permute-start(bf16[1536,384]{1,0:T(8,128)(2,1)} %collective-permute-done.3.refs_1_.refs_3_.refs_11_), channel_id=1, source_target_pairs={{0,4},{4,0},{8,12},{12,8},{16,20},{20,16},{24,28},{28,24},{1,5},{5... | collective-permute-start | bytes 3538952 | tf_op jit(solution)/shard_map/ppermute | solution.py:1142
  97.0 24.5 %collective-permute-start.15 = (bf16[1536,384]{1,0:T(8,128)(2,1)}, bf16[1536,384]{1,0:T(8,128)(2,1)}, u32[]{:S(2)}, u32[]{:S(2)}) collective-permute-start(bf16[1536,384]{1,0:T(8,128)(2,1)} %collective-permute-done.4.refs_2_.refs_4_.refs_12_), channel_id=1, source_target_pairs={{0,4},{4,0},{8,12},{12,8},{16,20},{20,16},{24,28},{28,24},{1,5},{5... | collective-permute-start | bytes 3538952 | tf_op jit(solution)/shard_map/ppermute | solution.py:1142
  109.3 12.3 %collective-permute-start.16 = (bf16[1536,384]{1,0:T(8,128)(2,1)}, bf16[1536,384]{1,0:T(8,128)(2,1)}, u32[]{:S(2)}, u32[]{:S(2)}) collective-permute-start(bf16[1536,384]{1,0:T(8,128)(2,1)} %collective-permute-done.11.refs_3_.refs_5_.refs_13_), channel_id=1, source_target_pairs={{0,4},{4,0},{8,12},{12,8},{16,20},{20,16},{24,28},{28,24},{1,5},{5... | collective-permute-start | bytes 3538952 | tf_op jit(solution)/shard_map/ppermute | solution.py:1142
  109.6 30.7 %collective-permute-start.18 = (bf16[512,1536]{1,0:T(8,128)(2,1)S(1)}, bf16[512,1536]{1,0:T(8,128)(2,1)S(1)}, u32[]{:S(2)}, u32[]{:S(2)}) collective-permute-start(bf16[512,1536]{1,0:T(8,128)(2,1)S(1)} %multiply_convert_fusion.pulled.refs_2_), channel_id=1, source_target_pairs={{0,4},{4,0},{8,12},{12,8},{16,20},{20,16},{24,28},{28,24},{1,5},{5... | collective-permute-start | bytes 4718600 | tf_op jit(solution)/shard_map/ppermute | solution.py:1142
  110.9 27.9 %collective-permute-start.12 = (bf16[384,1536]{1,0:T(8,128)(2,1)}, bf16[384,1536]{1,0:T(8,128)(2,1)}, u32[]{:S(2)}, u32[]{:S(2)}) collective-permute-start(bf16[384,1536]{1,0:T(8,128)(2,1)} %constant_dynamic-slice_fusion.4), channel_id=1, source_target_pairs={{0,1},{1,0},{2,3},{3,2},{4,6},{5,7},{6,4},{7,5},{8,9},{9,8},{10,11... | collective-permute-start | bytes 3538952 | tf_op jit(solution)/shard_map/ppermute | solution.py:1138
  120.5 18.8 %collective-permute-start.13 = (bf16[384,1536]{1,0:T(8,128)(2,1)}, bf16[384,1536]{1,0:T(8,128)(2,1)}, u32[]{:S(2)}, u32[]{:S(2)}) collective-permute-start(bf16[384,1536]{1,0:T(8,128)(2,1)} %constant_dynamic-slice_fusion.4), channel_id=1, source_target_pairs={{0,2},{1,3},{2,0},{3,1},{4,5},{5,4},{6,7},{7,6},{8,10},{9,11},{10,... | collective-permute-start | bytes 3538952 | tf_op jit(solution)/shard_map/ppermute | solution.py:1138
  138.7 3.8 collective-permute-start.17
  139.3 16.5 %collective-permute-start.19 = (bf16[384,1536]{1,0:T(8,128)(2,1)}, bf16[384,1536]{1,0:T(8,128)(2,1)}, u32[]{:S(2)}, u32[]{:S(2)}) collective-permute-start(bf16[384,1536]{1,0:T(8,128)(2,1)} %collective-permute-done.12.refs_5_), channel_id=1, source_target_pairs={{0,2},{1,3},{2,0},{3,1},{4,5},{5,4},{6,7},{7,6},{8,10},{9,11},{10,... | collective-permute-start | bytes 3538952 | tf_op jit(solution)/shard_map/ppermute | solution.py:1138
  153.6 30.0 %collective-permute-start.23 = (bf16[2,384,1536]{2,1,0:T(8,128)(2,1)}, bf16[2,384,1536]{2,1,0:T(8,128)(2,1)}, u32[]{:S(2)}, u32[]{:S(2)}) collective-permute-start(bf16[2,384,1536]{2,1,0:T(8,128)(2,1)} %get-tuple-element.212), channel_id=1, source_target_pairs={{0,2},{1,3},{2,0},{3,1},{4,5},{5,4},{6,7},{7,6},{8,10},{9,11},{10,... | collective-permute-start | bytes 7077896 | tf_op jit(solution)/shard_map/ppermute | solution.py:1138
  154.6 3.1 collective-permute-start.20
  155.0 6.1 %collective-permute-start.21 = (bf16[384,1536]{1,0:T(8,128)(2,1)}, bf16[384,1536]{1,0:T(8,128)(2,1)S(1)}, u32[]{:S(2)}, u32[]{:S(2)}) collective-permute-start(bf16[384,1536]{1,0:T(8,128)(2,1)} %collective-permute-done.13.refs_6_), channel_id=1, source_target_pairs={{0,4},{4,0},{8,12},{12,8},{16,20},{20,16},{24,28},{28,24},{1,5},{5... | collective-permute-start | bytes 3538952 | tf_op jit(solution)/shard_map/ppermute | solution.py:1142
  155.8 6.3 %collective-permute-start.22 = (bf16[384,1536]{1,0:T(8,128)(2,1)}, bf16[384,1536]{1,0:T(8,128)(2,1)}, u32[]{:S(2)}, u32[]{:S(2)}) collective-permute-start(bf16[384,1536]{1,0:T(8,128)(2,1)} %collective-permute-done.19.refs_7_), channel_id=1, source_target_pairs={{0,4},{4,0},{8,12},{12,8},{16,20},{20,16},{24,28},{28,24},{1,5},{5... | collective-permute-start | bytes 3538952 | tf_op jit(solution)/shard_map/ppermute | solution.py:1142
  162.1 21.5 %copy-start.7 = (bf16[2,384,1536]{2,1,0:T(8,128)(2,1)S(1)}, bf16[2,384,1536]{2,1,0:T(8,128)(2,1)}, u32[]{:S(2)}) copy-start(bf16[2,384,1536]{2,1,0:T(8,128)(2,1)} %get-tuple-element.211) | copy-start | bytes 7077892
  187.1 16.2 %collective-permute-start.24 = (bf16[1,384,1536]{2,1,0:T(8,128)(2,1)S(1)}, bf16[1,384,1536]{2,1,0:T(8,128)(2,1)S(1)}, u32[]{:S(2)}, u32[]{:S(2)}) collective-permute-start(bf16[1,384,1536]{2,1,0:T(8,128)(2,1)S(1)} %get-tuple-element.359), channel_id=1, source_target_pairs={{0,1},{1,0},{2,3},{3,2},{4,6},{5,7},{6,4},{7,5},{8,9},{9,8},{10,11... | collective-permute-start | bytes 3538952 | tf_op jit(solution)/shard_map/ppermute | solution.py:1138
  188.6 15.7 %copy-start.1 = (bf16[512,1536]{1,0:T(8,128)(2,1)S(1)}, bf16[512,1536]{1,0:T(8,128)(2,1)}, u32[]{:S(2)}) copy-start(bf16[512,1536]{1,0:T(8,128)(2,1)} %fusion.2.x.refs_2_.refs_4_) | copy-start | bytes 4718596
  204.3 5.8 %collective-permute-start.25 = (bf16[512,1536]{1,0:T(8,128)(2,1)}, bf16[512,1536]{1,0:T(8,128)(2,1)S(1)}, u32[]{:S(2)}, u32[]{:S(2)}) collective-permute-start(bf16[512,1536]{1,0:T(8,128)(2,1)} %get-tuple-element.223), channel_id=1, source_target_pairs={{0,4},{4,0},{8,12},{12,8},{16,20},{20,16},{24,28},{28,24},{1,5},{5... | collective-permute-start | bytes 4718600 | tf_op jit(solution)/shard_map/ppermute | solution.py:1142
  204.3 5.8 %collective-permute-start.26 = (bf16[512,1536]{1,0:T(8,128)(2,1)S(1)}, bf16[512,1536]{1,0:T(8,128)(2,1)S(1)}, u32[]{:S(2)}, u32[]{:S(2)}) collective-permute-start(bf16[512,1536]{1,0:T(8,128)(2,1)S(1)} %copy-done.1), channel_id=1, source_target_pairs={{0,4},{4,0},{8,12},{12,8},{16,20},{20,16},{24,28},{28,24},{1,5},{5... | collective-permute-start | bytes 4718600 | tf_op jit(solution)/shard_map/ppermute | solution.py:1142
  223.1 30.6 %collective-permute-start.27 = (bf16[2,1536,384]{2,1,0:T(8,128)(2,1)}, bf16[2,1536,384]{2,1,0:T(8,128)(2,1)}, u32[]{:S(2)}, u32[]{:S(2)}) collective-permute-start(bf16[2,1536,384]{2,1,0:T(8,128)(2,1)} %get-tuple-element.228), channel_id=1, source_target_pairs={{0,2},{1,3},{2,0},{3,1},{4,5},{5,4},{6,7},{7,6},{8,10},{9,11},{10,... | collective-permute-start | bytes 7077896 | tf_op jit(solution)/shard_map/ppermute | solution.py:1138
  224.1 29.5 %collective-permute-start.28 = (bf16[384,1536]{1,0:T(8,128)(2,1)}, bf16[384,1536]{1,0:T(8,128)(2,1)S(1)}, u32[]{:S(2)}, u32[]{:S(2)}) collective-permute-start(bf16[384,1536]{1,0:T(8,128)(2,1)} %get-tuple-element.357), channel_id=1, source_target_pairs={{0,8},{4,12},{24,16},{28,20},{1,9},{5,13},{25,17},{29,21},{2,10},{... | collective-permute-start | bytes 3538952 | tf_op jit(solution)/shard_map/ppermute | solution.py:1150
  229.2 25.4 %copy-start.8 = (bf16[2,1536,384]{2,1,0:T(8,128)(2,1)S(1)}, bf16[2,1536,384]{2,1,0:T(8,128)(2,1)}, u32[]{:S(2)}) copy-start(bf16[2,1536,384]{2,1,0:T(8,128)(2,1)} %get-tuple-element.235) | copy-start | bytes 7077892
  253.7 7.7 %collective-permute-start.29 = (bf16[512,1024]{1,0:T(8,128)(2,1)}, bf16[512,1024]{1,0:T(8,128)(2,1)}, u32[]{:S(2)}, u32[]{:S(2)}) collective-permute-start(bf16[512,1024]{1,0:T(8,128)(2,1)} %get-tuple-element.234), channel_id=1, source_target_pairs={{0,4},{4,0},{8,12},{12,8},{16,20},{20,16},{24,28},{28,24},{1,5},{5... | collective-permute-start | bytes 3145736 | tf_op jit(solution)/shard_map/ppermute | solution.py:1142
  258.2 25.7 %collective-permute-start.30 = (bf16[1,1536,384]{2,1,0:T(8,128)(2,1)S(1)}, bf16[1,1536,384]{2,1,0:T(8,128)(2,1)S(1)}, u32[]{:S(2)}, u32[]{:S(2)}) collective-permute-start(bf16[1,1536,384]{2,1,0:T(8,128)(2,1)S(1)} %get-tuple-element.355), channel_id=1, source_target_pairs={{0,1},{1,0},{2,3},{3,2},{4,6},{5,7},{6,4},{7,5},{8,9},{9,8},{10,11... | collective-permute-start | bytes 3538952 | tf_op jit(solution)/shard_map/ppermute | solution.py:1138
  259.7 59.4 %collective-permute-start.36 = (bf16[384,1536]{1,0:T(8,128)(2,1)S(1)}, bf16[384,1536]{1,0:T(8,128)(2,1)}, u32[]{:S(2)}, u32[]{:S(2)}) collective-permute-start(bf16[384,1536]{1,0:T(8,128)(2,1)S(1)} %add_convert_fusion.7), channel_id=1, source_target_pairs={{8,16},{12,20},{16,8},{20,12},{9,17},{13,21},{17,9},{21,13},{10,18... | collective-permute-start | bytes 3538952 | tf_op jit(solution)/shard_map/ppermute | solution.py:1150
  269.7 31.9 %collective-permute-start.31 = (bf16[2,1024,384]{2,1,0:T(8,128)(2,1)}, bf16[2,1024,384]{2,1,0:T(8,128)(2,1)}, u32[]{:S(2)}, u32[]{:S(2)}) collective-permute-start(bf16[2,1024,384]{2,1,0:T(8,128)(2,1)} %get-tuple-element.266), channel_id=1, source_target_pairs={{0,2},{1,3},{2,0},{3,1},{4,5},{5,4},{6,7},{7,6},{8,10},{9,11},{10,... | collective-permute-start | bytes 4718600 | tf_op jit(solution)/shard_map/ppermute | solution.py:1138
  287.9 31.2 %collective-permute-start.34 = (bf16[1536,384]{1,0:T(8,128)(2,1)}, bf16[1536,384]{1,0:T(8,128)(2,1)}, u32[]{:S(2)}, u32[]{:S(2)}) collective-permute-start(bf16[1536,384]{1,0:T(8,128)(2,1)} %get-tuple-element.353), channel_id=1, source_target_pairs={{0,8},{4,12},{24,16},{28,20},{1,9},{5,13},{25,17},{29,21},{2,10},{... | collective-permute-start | bytes 3538952 | tf_op jit(solution)/shard_map/ppermute | solution.py:1150
  305.3 13.8 %collective-permute-start.35 = (bf16[1,1024,384]{2,1,0:T(8,128)(2,1)}, bf16[1,1024,384]{2,1,0:T(8,128)(2,1)}, u32[]{:S(2)}, u32[]{:S(2)}) collective-permute-start(bf16[1,1024,384]{2,1,0:T(8,128)(2,1)} %get-tuple-element.363), channel_id=1, source_target_pairs={{0,1},{1,0},{2,3},{3,2},{4,6},{5,7},{6,4},{7,5},{8,9},{9,8},{10,11... | collective-permute-start | bytes 2359304 | tf_op jit(solution)/shard_map/ppermute | solution.py:1138
  306.2 4.4 collective-permute-start.33
  306.9 2.0 collective-permute-start.32
  318.1 33.6 %collective-permute-start.37 = (bf16[2,768,384]{2,1,0:T(8,128)(2,1)}, bf16[2,768,384]{2,1,0:T(8,128)(2,1)}, u32[]{:S(2)}, u32[]{:S(2)}) collective-permute-start(bf16[2,768,384]{2,1,0:T(8,128)(2,1)} %get-tuple-element.282), channel_id=1, source_target_pairs={{0,2},{1,3},{2,0},{3,1},{4,5},{5,4},{6,7},{7,6},{8,10},{9,11},{10,... | collective-permute-start | bytes 3538952 | tf_op jit(solution)/shard_map/ppermute | solution.py:1138
  321.6 45.1 %collective-permute-start.40 = (bf16[1536,384]{1,0:T(8,128)(2,1)}, bf16[1536,384]{1,0:T(8,128)(2,1)S(1)}, u32[]{:S(2)}, u32[]{:S(2)}) collective-permute-start(bf16[1536,384]{1,0:T(8,128)(2,1)} %add_convert_fusion.6), channel_id=1, source_target_pairs={{8,16},{12,20},{16,8},{20,12},{9,17},{13,21},{17,9},{21,13},{10,18... | collective-permute-start | bytes 3538952 | tf_op jit(solution)/shard_map/ppermute | solution.py:1150
  325.1 41.7 %collective-permute-start.41 = (bf16[384,1536]{1,0:T(8,128)(2,1)}, bf16[384,1536]{1,0:T(8,128)(2,1)}, u32[]{:S(2)}, u32[]{:S(2)}) collective-permute-start(bf16[384,1536]{1,0:T(8,128)(2,1)} %add_convert_fusion.5), channel_id=1, source_target_pairs={{8,0},{12,4},{16,24},{20,28},{9,1},{13,5},{17,25},{21,29},{10,2},{... | collective-permute-start | bytes 3538952 | tf_op jit(solution)/shard_map/ppermute | solution.py:1150
  328.6 27.5 %collective-permute-start.39 = (bf16[1024,384]{1,0:T(8,128)(2,1)}, bf16[1024,384]{1,0:T(8,128)(2,1)}, u32[]{:S(2)}, u32[]{:S(2)}) collective-permute-start(bf16[1024,384]{1,0:T(8,128)(2,1)} %get-tuple-element.361), channel_id=1, source_target_pairs={{0,8},{4,12},{24,16},{28,20},{1,9},{5,13},{25,17},{29,21},{2,10},{... | collective-permute-start | bytes 2359304 | tf_op jit(solution)/shard_map/ppermute | solution.py:1150
  354.5 10.2 %collective-permute-start.38 = (bf16[1,768,384]{2,1,0:T(8,128)(2,1)}, bf16[1,768,384]{2,1,0:T(8,128)(2,1)}, u32[]{:S(2)}, u32[]{:S(2)}) collective-permute-start(bf16[1,768,384]{2,1,0:T(8,128)(2,1)} %get-tuple-element.368), channel_id=1, source_target_pairs={{0,1},{1,0},{2,3},{3,2},{4,6},{5,7},{6,4},{7,5},{8,9},{9,8},{10,11... | collective-permute-start | bytes 1769480 | tf_op jit(solution)/shard_map/ppermute | solution.py:1138
  362.4 35.7 %collective-permute-start.43 = (bf16[1024,384]{1,0:T(8,128)(2,1)}, bf16[1024,384]{1,0:T(8,128)(2,1)}, u32[]{:S(2)}, u32[]{:S(2)}) collective-permute-start(bf16[1024,384]{1,0:T(8,128)(2,1)} %add_convert_fusion.9), channel_id=1, source_target_pairs={{8,16},{12,20},{16,8},{20,12},{9,17},{13,21},{17,9},{21,13},{10,18... | collective-permute-start | bytes 2359304 | tf_op jit(solution)/shard_map/ppermute | solution.py:1150
  368.3 29.8 %collective-permute-start.44 = (bf16[1536,384]{1,0:T(8,128)(2,1)S(1)}, bf16[1536,384]{1,0:T(8,128)(2,1)}, u32[]{:S(2)}, u32[]{:S(2)}) collective-permute-start(bf16[1536,384]{1,0:T(8,128)(2,1)S(1)} %add_convert_fusion.3), channel_id=1, source_target_pairs={{8,0},{12,4},{16,24},{20,28},{9,1},{13,5},{17,25},{21,29},{10,2},{... | collective-permute-start | bytes 3538952 | tf_op jit(solution)/shard_map/ppermute | solution.py:1150
  371.0 27.1 %collective-permute-start.45 = (bf16[384,1536]{1,0:T(8,128)(2,1)S(1)}, bf16[384,1536]{1,0:T(8,128)(2,1)}, u32[]{:S(2)}, u32[]{:S(2)}) collective-permute-start(bf16[384,1536]{1,0:T(8,128)(2,1)S(1)} %broadcast_select_fusion.3), channel_id=1, source_target_pairs={{0,4},{4,0},{8,12},{12,8},{16,20},{20,16},{24,28},{28,24},{1,5},{5... | collective-permute-start | bytes 3538952 | tf_op jit(solution)/shard_map/ppermute | solution.py:1142
  371.1 24.3 %collective-permute-start.42 = (bf16[768,384]{1,0:T(8,128)(2,1)}, bf16[768,384]{1,0:T(8,128)(2,1)}, u32[]{:S(2)}, u32[]{:S(2)}) collective-permute-start(bf16[768,384]{1,0:T(8,128)(2,1)} %get-tuple-element.365), channel_id=1, source_target_pairs={{0,8},{4,12},{24,16},{28,20},{1,9},{5,13},{25,17},{29,21},{2,10},{... | collective-permute-start | bytes 1769480 | tf_op jit(solution)/shard_map/ppermute | solution.py:1150
  377.5 20.6 %collective-permute-start.46 = (f32[4,4964]{1,0:T(4,128)}, f32[4,4964]{1,0:T(4,128)}, u32[]{:S(2)}, u32[]{:S(2)}) collective-permute-start(f32[4,4964]{1,0:T(4,128)} %concatenate.34), channel_id=1, source_target_pairs={{0,4},{4,0},{8,12},{12,8},{16,20},{20,16},{24,28},{28,24},{1,5},{5... | collective-permute-start | bytes 238280 | tf_op jit(solution)/shard_map/ppermute | solution.py:1142
  396.7 19.8 %collective-permute-start.48 = (bf16[768,384]{1,0:T(8,128)(2,1)S(1)}, bf16[768,384]{1,0:T(8,128)(2,1)}, u32[]{:S(2)}, u32[]{:S(2)}) collective-permute-start(bf16[768,384]{1,0:T(8,128)(2,1)S(1)} %add_convert_fusion.11), channel_id=1, source_target_pairs={{8,16},{12,20},{16,8},{20,12},{9,17},{13,21},{17,9},{21,13},{10,18... | collective-permute-start | bytes 1769480 | tf_op jit(solution)/shard_map/ppermute | solution.py:1150
  399.6 9.5 %collective-permute-start.47 = (bf16[1536,384]{1,0:T(8,128)(2,1)S(1)}, bf16[1536,384]{1,0:T(8,128)(2,1)S(1)}, u32[]{:S(2)}, u32[]{:S(2)}) collective-permute-start(bf16[1536,384]{1,0:T(8,128)(2,1)S(1)} %broadcast_select_fusion.2.own), channel_id=1, source_target_pairs={{0,4},{4,0},{8,12},{12,8},{16,20},{20,16},{24,28},{28,24},{1,5},{5... | collective-permute-start | bytes 3538952 | tf_op jit(solution)/shard_map/ppermute | solution.py:1142
  401.7 14.8 %collective-permute-start.49 = (f32[1,4964]{1,0:T(1,128)}, f32[1,4964]{1,0:T(1,128)}, u32[]{:S(2)}, u32[]{:S(2)}) collective-permute-start(f32[1,4964]{1,0:T(1,128)} %get-tuple-element.376), channel_id=1, source_target_pairs={{0,1},{1,0},{2,3},{3,2},{4,5},{5,4},{6,7},{7,6},{8,9},{9,8},{10,11... | collective-permute-start | bytes 59576 | tf_op jit(solution)/shard_map/ppermute | solution.py:1146
  403.2 13.3 %collective-permute-start.50 = (f32[1,4964]{1,0:T(1,128)}, f32[1,4964]{1,0:T(1,128)}, u32[]{:S(2)}, u32[]{:S(2)}) collective-permute-start(f32[1,4964]{1,0:T(1,128)} %get-tuple-element.375), channel_id=1, source_target_pairs={{0,2},{1,3},{2,0},{3,1},{4,6},{5,7},{6,4},{7,5},{8,10},{9,11},{10,... | collective-permute-start | bytes 59576 | tf_op jit(solution)/shard_map/ppermute | solution.py:1146
  404.2 12.3 %collective-permute-start.51 = (f32[1,4964]{1,0:T(1,128)}, f32[1,4964]{1,0:T(1,128)}, u32[]{:S(2)}, u32[]{:S(2)}) collective-permute-start(f32[1,4964]{1,0:T(1,128)} %get-tuple-element.374), channel_id=1, source_target_pairs={{0,3},{1,2},{2,1},{3,0},{4,7},{5,6},{6,5},{7,4},{8,11},{9,10},{10,... | collective-permute-start | bytes 59576 | tf_op jit(solution)/shard_map/ppermute | solution.py:1146
  410.1 25.3 %collective-permute-start.52 = (bf16[1024,384]{1,0:T(8,128)(2,1)}, bf16[1024,384]{1,0:T(8,128)(2,1)}, u32[]{:S(2)}, u32[]{:S(2)}) collective-permute-start(bf16[1024,384]{1,0:T(8,128)(2,1)} %add_convert_fusion.8), channel_id=1, source_target_pairs={{8,0},{12,4},{16,24},{20,28},{9,1},{13,5},{17,25},{21,29},{10,2},{... | collective-permute-start | bytes 2359304 | tf_op jit(solution)/shard_map/ppermute | solution.py:1150
  418.5 16.8 %collective-permute-start.54 = (f32[1,4964]{1,0:T(1,128)S(1)}, f32[1,4964]{1,0:T(1,128)S(1)}, u32[]{:S(2)}, u32[]{:S(2)}) collective-permute-start(f32[1,4964]{1,0:T(1,128)S(1)} %add_add_fusion), channel_id=1, source_target_pairs={{0,16},{4,20},{8,24},{12,28},{16,0},{20,4},{24,8},{28,12},{1,17},{... | collective-permute-start | bytes 59576 | tf_op jit(solution)/shard_map/ppermute | solution.py:1150
  423.1 12.2 %collective-permute-start.55 = (f32[1,4964]{1,0:T(1,128)S(1)}, f32[1,4964]{1,0:T(1,128)S(1)}, u32[]{:S(2)}, u32[]{:S(2)}) collective-permute-start(f32[1,4964]{1,0:T(1,128)S(1)} %add_add_fusion), channel_id=1, source_target_pairs={{0,24},{4,28},{8,16},{12,20},{16,8},{20,12},{24,0},{28,4},{1,25},{... | collective-permute-start | bytes 59576 | tf_op jit(solution)/shard_map/ppermute | solution.py:1150
  424.5 10.8 %collective-permute-start.53 = (f32[1,4964]{1,0:T(1,128)S(1)}, f32[1,4964]{1,0:T(1,128)S(1)}, u32[]{:S(2)}, u32[]{:S(2)}) collective-permute-start(f32[1,4964]{1,0:T(1,128)S(1)} %add_add_fusion), channel_id=1, source_target_pairs={{0,8},{4,12},{8,0},{12,4},{16,24},{20,28},{24,16},{28,20},{1,9},{5... | collective-permute-start | bytes 59576 | tf_op jit(solution)/shard_map/ppermute | solution.py:1150
  424.5 20.7 %collective-permute-start.56 = (bf16[768,384]{1,0:T(8,128)(2,1)S(1)}, bf16[768,384]{1,0:T(8,128)(2,1)}, u32[]{:S(2)}, u32[]{:S(2)}) collective-permute-start(bf16[768,384]{1,0:T(8,128)(2,1)S(1)} %add_convert_fusion.10), channel_id=1, source_target_pairs={{8,0},{12,4},{16,24},{20,28},{9,1},{13,5},{17,25},{21,29},{10,2},{... | collective-permute-start | bytes 1769480 | tf_op jit(solution)/shard_map/ppermute | solution.py:1150
  436.7 9.7 %collective-permute-start.57 = (bf16[1024,384]{1,0:T(8,128)(2,1)S(1)}, bf16[1024,384]{1,0:T(8,128)(2,1)}, u32[]{:S(2)}, u32[]{:S(2)}) collective-permute-start(bf16[1024,384]{1,0:T(8,128)(2,1)S(1)} %broadcast_select_fusion.4.refs_0_), channel_id=1, source_target_pairs={{0,4},{4,0},{8,12},{12,8},{16,20},{20,16},{24,28},{28,24},{1,5},{5... | collective-permute-start | bytes 2359304 | tf_op jit(solution)/shard_map/ppermute | solution.py:1142
  446.3 4.2 collective-permute-start.58
  (35 other events, 125.5 us)

commit v3 on v2

--- a/solution.py
+++ b/solution.py
@@ -1062,7 +1062,7 @@
         tuple(grads) + (() if first else (start,)) + tuple(blocks) + more,
         grad_specs + ([] if first else [whole((tokens, width))]) + block_specs + more_specs,
         outs, out_specs, scratch,
-        step, 10**10 if last is None else 10**11, 20 * MIB,
+        step, 10**11 if last is not None else 10**10 if first else 1, 20 * MIB if first else 1,
     )
 
 
@@ -1479,15 +1479,20 @@
     gate_line = middle((gate_held, gate_arrived))
     near_line = inward(finish_stages(*settle(near_keep, near_there)))
     out_line = outward((out_inner, out_arrived))
-    gate_inner, near_held, out_done, grad_gate = hold(
-        (gate_line[0], near_line[0], out_line[0], grad_gate)
-    )
+    gate_inner, near_held, out_done, far_keep, far_there = hold(
+        (gate_line[0], near_line[0], out_line[0], far_keep, far_there)
+    )
+    far_send, far_keep = settle(far_keep, far_there)
+    far_there = hop(far_send, upper // 2)
+    far_keep, grad_gate = hold((far_keep, grad_gate))
     (partial,) = input_backward(meta, None, gate_part(0) + gate_part(1), tokens, width)
     partial, far_there = hold((partial, far_there))
-    far_send, far_keep = settle(far_keep, far_there)
-    far_there = hop(far_send, upper // 2)
-    far_keep, near_arrived, small_grads = hold(
-        (far_keep, near_line[1], (sums_near, sums_far, sums_keys, grad_steps, grad_gain_two))
+    far_line = inward(finish_stages(*settle(far_keep, far_there)))
+    far_held, near_arrived, gate_arrived, out_arrived, small_grads = hold(
+        (
+            far_line[0], near_line[1], gate_line[1], out_line[1],
+            (sums_near, sums_far, sums_keys, grad_steps, grad_gain_two),
+        )
     )
     sums_near, sums_far, sums_keys, grad_steps, grad_gain_two = small_grads
     sums = jnp.concatenate([sums_near, sums_far, sums_keys], axis=1)
@@ -1500,10 +1505,7 @@
         jnp.sum(grad_gain_two, axis=0).reshape(count, -1),
     )
     vector = jnp.concatenate(grads, axis=1)
-    far_there, far_keep, partial, vector = hold((far_there, far_keep, partial, vector))
     vector_there = swap(vector)
-    far_line = inward(finish_stages(*settle(far_keep, far_there)))
-    far_held, gate_arrived, out_arrived = hold((far_line[0], gate_line[1], out_line[1]))
     gate_line = outward((gate_inner, gate_arrived))
     near_line = middle((near_held, near_arrived))
     out_total = summed((out_done, out_arrived))
@@ -1513,9 +1515,7 @@
     )
     (partial,) = input_backward(
         meta, partial,
-        conv_part(grad_near, 0, part, 0, 0)
-        + conv_part(grad_near, part, over, 1, 0)
-        + conv_part(grad_far, 0, part - over, 1, over),
+        conv_part(grad_near, 0, part, 0, 0),
         tokens, width,
     )
     partial, far_arrived = hold((partial, far_line[1]))
@@ -1537,7 +1537,9 @@
     row = chips_sum(add_up(spread_rows))[0]
     (hidden_grad,) = input_backward(
         meta, partial,
-        [
+        conv_part(grad_near, part, over, 1, 0)
+        + conv_part(grad_far, 0, part - over, 1, over)
+        + [
             (grad_keys, 0, 1, None, conv_own, DI // 2 // TILE, None, 0, 0),
             (grad_raw, 0, 1, None, conv_own, (DI // 2 + TILE) // 64, None, 0, 0),
         ],

time: 463 us -> 470 us (1.015)
  local copies, waits for them, and re-layouts: 37.7 us -> 45.9 us
    unnamed x86 -> x92, local copies, waits for them, and re-layouts: 11.9 us -> 12.1 us
  transfers between devices with their start and end apart: 59 -> 59, of which waited for: 13 -> 13; matrix products, arithmetic and copies ran while one was open for 16% -> 17% of each run, Pallas kernels for 47% -> 46%
where the time goes in v3:
time: 470 us; the launch traced here: 464 us
  Pallas kernels  231 us (49%)
  starting transfers between devices  69.4 us (15%)
  waiting for transfers between devices  62.6 us (13%)
  other arithmetic  52.4 us (11%)
  local copies, waits for them, and re-layouts  45.9 us (10%)
    pallas_call x19, Pallas kernels, call(): pl.pallas_call(body, name=name, grid_spec=pltpu.PrefetchScalarGridSpec(nu...  231 us
    ppermute x17, waiting for transfers between devices, hop(): return lax.ppermute(x, ('rep', 'shard'), pairs)  44.8 us
    ppermute x15, starting transfers between devices, along(): lax.ppermute(x, 'rep', [(2 * a + k, 2 * b + k) for a, b in pairs for k in...  36.3 us
    ppermute x17, starting transfers between devices, hop(): return lax.ppermute(x, ('rep', 'shard'), pairs)  21.6 us
    unnamed x92, local copies, waits for them, and re-layouts  12.1 us
    convert_element_type x4, other arithmetic, inward(): return (held, along(held.astype(BF), [(0, 1), (3, 2)]))  10.6 us
  transfers between devices with their start and end apart: 59, of which 13 were waited for; matrix products, arithmetic and copies ran while one was open for 17% of the time, Pallas kernels for 46%

profile of v3, /device:TPU:0, one launch (start us, length us, event | category | flops | bytes accessed | tf_op | source)
XLA Modules:
  0.0 464.1 jit_solution(8134268031933872013)
XLA Ops:
  1.6 2.9 dynamic-slice_bitcast_fusion
  5.0 3.0 collective-permute-start
  9.8 2.0 collective-permute-start.6
  14.0 25.6 %collective-permute-done.refs_1_.refs_9_.refs_13_.refs_3_.refs_6_.refs_14_.refs_22_.refs_26_ = bf16[1856,384]{1,0:T(8,128)(2,1)S(1)} collective-permute-done((bf16[1856,384]{1,0:T(8,128)(2,1)S(1)}, bf16[1856,384]{1,0:T(8,128)(2,1)S(1)}, u32[]{:S(2)}, u32[]{:S(2)}) %collective-permute-start) | collective-permute-done | bytes 1425440 | tf_op jit(solution)/shard_map/ppermute | solution.py:1138
  39.5 1.8 collective-permute-start.2
  41.3 1.8 fusion
  46.2 12.3 %collective-permute-done.2.refs_3_.refs_11_.refs_15_.refs_5_.refs_8_.refs_16_.refs_24_.refs_28_ = bf16[1856,384]{1,0:T(8,128)(2,1)} collective-permute-done((bf16[1856,384]{1,0:T(8,128)(2,1)S(1)}, bf16[1856,384]{1,0:T(8,128)(2,1)}, u32[]{:S(2)}, u32[]{:S(2)}) %collective-permute-start.2) | collective-permute-done | bytes 1425440 | tf_op jit(solution)/shard_map/ppermute | solution.py:1138
  59.7 2.5 collective-permute-start.3
  64.0 3.0 fusion.2.x.refs_2_.refs_4_
  68.2 24.5 %conv_forward.1 = (bf16[512,3072]{1,0:T(8,128)(2,1)}, bf16[512,3072]{1,0:T(8,128)(2,1)}, f32[512,3072]{1,0:T(8,128)}, bf16[512,256]{1,0:T(8,128)(2,1)}, bf16[512...) custom-call(s32[20]{0:T(128)} %stack.90.meta, ...), custom_call_target="tpu_custom_call" | custom-call | flops 5234491392 | bytes 25165824 | tf_op jit(solution)/shard_map/conv_forward/pallas_call | solution.py:91
  93.9 2.4 constant_dynamic-slice_fusion.4
  97.6 9.2 %scan_forward.2 = (f32[512,3072]{1,0:T(8,128)}, bf16[12,128,256]{2,1,0:T(8,128)(2,1)}) custom-call(s32[20]{0:T(128)} %stack.90.meta, bf16[512,3072]{1,0:T(8,128)(2,1)} %get-tuple-element.184.content.refs_0_, bf16[512,256]{1,0:T(8,128)(2,1)} %get-tuple-element.185.keys.refs_1_.refs_0_, f32[12,512,16]{2,1,0:T(8,128)} %get-tuple-element.186.columns.refs_2_, ...), custom_call_target="tpu_custom_call" | custom-call | flops 6000000000 | bytes 6291456 | tf_op jit(solution)/shard_map/scan_forward/pallas_call | solution.py:91
  106.8 2.5 collective-permute-done.11.refs_3_.refs_5_.refs_13_
  111.3 9.1 %scan_forward.3 = (f32[512,3072]{1,0:T(8,128)}, bf16[12,128,256]{2,1,0:T(8,128)(2,1)}) custom-call(s32[20]{0:T(128)} %stack.90.meta, bf16[512,3072]{1,0:T(8,128)(2,1)} %get-tuple-element.184.content.refs_0_, bf16[512,256]{1,0:T(8,128)(2,1)} %get-tuple-element.185.keys.refs_1_.refs_0_, ...), custom_call_target="tpu_custom_call", output_to_operand_aliasing={{0}: (6, {}), {1}: (7, {})} | custom-call | flops 6000000000 | bytes 6291456 | tf_op jit(solution)/shard_map/scan_forward/pallas_call | solution.py:91
  121.5 17.1 %gate_forward.1 = (bf16[512,3072]{1,0:T(8,128)(2,1)}, bf16[512,3072]{1,0:T(8,128)(2,1)}, bf16[512,1536]{1,0:T(8,128)(2,1)}, f32[512,1]{1,0:T(8,128)}) custom-call(s32[20]{0:T(128)} %stack.90.meta, bf16[512,1536]{1,0:T(8,128)(2,1)} %fusion.2.x.refs_2_.refs_4_, f32[512,3072]{1,0:T(8,128)} %get-tuple-element.193.mixed, f32[1,3072]{1,0:T(1,128)} %bitcast.78, ...), custom_call_target="tpu_custom_call" | custom-call | flops 4831838208 | bytes 29360128 | tf_op jit(solution)/shard_map/gate_forward/pallas_call | solution.py:91
  140.4 2.1 collective-permute-done.17.theirs
  142.4 11.2 %rows_product.1 = (bf16[2,384,1536]{2,1,0:T(8,128)(2,1)}, bf16[2,384,1536]{2,1,0:T(8,128)(2,1)}) custom-call(s32[20]{0:T(128)} %stack.90.meta, bf16[512,3072]{1,0:T(8,128)(2,1)} %get-tuple-element.201.mine.refs_0_.refs_1_, bf16[512,1536]{1,0:T(8,128)(2,1)} %collective-permute-done.17.theirs, bf16[512,1536]{1,0:T(8,128)(2,1)} %copy-done.12, ...), custom_call_target="tpu_custom_call" | custom-call | flops 4831838208 | bytes 12582912 | tf_op jit(solution)/shard_map/rows_product/pallas_call | solution.py:91
  155.8 2.1 collective-permute-done.20.refs_9_
  157.9 3.4 collective-permute-done.21.refs_10_
  162.3 21.5 %out_forward.1 = (bf16[512,1536]{1,0:T(8,128)(2,1)}, bf16[512,3072]{1,0:T(8,128)(2,1)}, f32[512,128]{1,0:T(8,128)}) custom-call(s32[20]{0:T(128)} %stack.90.meta, bf16[512,3072]{1,0:T(8,128)(2,1)} %get-tuple-element.201.mine.refs_0_.refs_1_, bf16[512,3072]{1,0:T(8,128)(2,1)} %get-tuple-element.201.mine.refs_0_.refs_1_, bf16[512,1536]{1,0:T(8,128)(2,1)} %copy-done.12, ...), custom_call_target="tpu_custom_call" | custom-call | flops 9663676416 | bytes 25165824 | tf_op jit(solution)/shard_map/out_forward/pallas_call | solution.py:91
  183.8 2.3 add_convert_fusion.1
  188.7 12.2 %norm_back.1 = (bf16[512,3072]{1,0:T(8,128)(2,1)}, bf16[512,1536]{1,0:T(8,128)(2,1)}, bf16[512,3072]{1,0:T(8,128)(2,1)}, f32[8,3072]{1,0:T(8,128)}) custom-call(s32[20]{0:T(128)} %stack.90.meta, bf16[512,3072]{1,0:T(8,128)(2,1)} %get-tuple-element.205.back, f32[512,128]{1,0:T(8,128)} %get-tuple-element.211.total, f32[512,3072]{1,0:T(8,128)} %get-tuple-element.193.mixed, ...), custom_call_target="tpu_custom_call" | custom-call | flops 1000000000 | bytes 25165824 | tf_op jit(solution)/shard_map/norm_back/pallas_call | solution.py:91
  201.0 2.5 collective-permute-done.24
  205.0 3.8 fusion.11
  212.7 10.7 %columns_product.3 = (bf16[2,1536,384]{2,1,0:T(8,128)(2,1)}, bf16[2,1536,384]{2,1,0:T(8,128)(2,1)}) custom-call(s32[20]{0:T(128)} %stack.90.meta, bf16[512,3072]{1,0:T(8,128)(2,1)} %get-tuple-element.283.refs_0_.refs_1_, bf16[512,1536]{1,0:T(8,128)(2,1)} %copy-done.13, bf16[512,1536]{1,0:T(8,128)(2,1)} %fusion.2.x.refs_2_.refs_4_, bf16[512,1536]{1,0:T(8,128)(2,1)} %copy-done.3), custom_call_target="tpu_custom_call" | custom-call | flops 1 | bytes 1 | tf_op jit(solution)/shard_map/columns_product/pallas_call | solution.py:91
  224.4 3.6 collective-permute-start.28
  229.5 22.7 %scan_backward.2 = (bf16[512,2048]{1,0:T(8,128)(2,1)}, bf16[512,1024]{1,0:T(8,128)(2,1)}, f32[8,2048]{1,0:T(8,128)}, f32[8,512,8]{2,1,0:T(8,128)}, f32[2,256,256...) custom-call(s32[20]{0:T(128)} %stack.90.meta, bf16[512,3072]{1,0:T(8,128)(2,1)} %get-tuple-element.184.content.refs_0_, ...), custom_call_target="tpu_custom_call" | custom-call | flops 24000000000 | bytes 8388608 | tf_op jit(solution)/shard_map/scan_backward/pallas_call | solution.py:91
  252.2 1.7 collective-permute-done.28
  254.9 2.2 add_convert_fusion
  259.9 1.7 collective-permute-start.36
  261.7 8.4 %columns_product.4 = (bf16[2,1024,384]{2,1,0:T(8,128)(2,1)}, bf16[2,1024,384]{2,1,0:T(8,128)(2,1)}) custom-call(s32[20]{0:T(128)} %stack.90.meta, bf16[512,2048]{1,0:T(8,128)(2,1)} %get-tuple-element.227.refs_0_, bf16[512,1024]{1,0:T(8,128)(2,1)} %collective-permute-done.29.refs_1_, bf16[512,1536]{1,0:T(8,128)(2,1)} %fusion.2.x.refs_2_.refs_4_, ...), custom_call_target="tpu_custom_call" | custom-call | flops 1 | bytes 1 | tf_op jit(solution)/shard_map/columns_product/pallas_call | solution.py:91
  271.0 13.2 %scan_backward.3 = (bf16[512,1024]{1,0:T(8,128)(2,1)}, bf16[512,512]{1,0:T(8,128)(2,1)}, f32[8,1024]{1,0:T(8,128)}, f32[4,512,8]{2,1,0:T(8,128)}, f32[2,256,256]...) custom-call(s32[20]{0:T(128)} %stack.90.meta, bf16[512,3072]{1,0:T(8,128)(2,1)} %get-tuple-element.184.content.refs_0_, ...), custom_call_target="tpu_custom_call" | custom-call | flops 12000000000 | bytes 4194304 | tf_op jit(solution)/shard_map/scan_backward/pallas_call | solution.py:91
  285.3 2.9 fusion.12
  288.2 7.1 %collective-permute-start.34 = (bf16[1536,384]{1,0:T(8,128)(2,1)}, bf16[1536,384]{1,0:T(8,128)(2,1)}, u32[]{:S(2)}, u32[]{:S(2)}) collective-permute-start(bf16[1536,384]{1,0:T(8,128)(2,1)} %get-tuple-element.349), channel_id=1, source_target_pairs={{0,8},{4,12},{24,16},{28,20},{1,9},{5,13},{25,17},{29,21},{2,10},{... | collective-permute-start | bytes 3538952 | tf_op jit(solution)/shard_map/ppermute | solution.py:1150
  295.3 6.6 %tail_backward.1 = (bf16[512,256]{1,0:T(8,128)(2,1)}, f32[8,256]{1,0:T(8,128)}, bf16[512,128]{1,0:T(8,128)(2,1)}, f32[8,128]{1,0:T(8,128)}, bf16[2,512,256]{2,1,0:T(8,128)(2,1)}) custom-call(s32[20]{0:T(128)} %stack.90.meta, bf16[512,256]{1,0:T(8,128)(2,1)} %get-tuple-element.185.keys.refs_1_.refs_0_, bf16[512,256]{1,0:T(8,128)(2,1)} %get-tuple-element.247.refs_1_, ...), custom_call_target="tpu_custom_call" | custom-call | flops 1 | bytes 1 | tf_op jit(solution)/shard_map/tail_backward/pallas_call | solution.py:91
  301.8 2.3 add_convert_fusion.2
  309.1 1.7 slice_bitcast_fusion.refs_1_
  310.8 7.5 %columns_product.5 = (bf16[2,768,384]{2,1,0:T(8,128)(2,1)}, bf16[2,768,384]{2,1,0:T(8,128)(2,1)}) custom-call(s32[20]{0:T(128)} %stack.90.meta, bf16[512,1024]{1,0:T(8,128)(2,1)} %get-tuple-element.246.refs_0_.refs_1_, bf16[512,256]{1,0:T(8,128)(2,1)} %slice_bitcast_fusion.refs_1_, bf16[512,512]{1,0:T(8,128)(2,1)} %collective-permute-done.33.refs_2_, ...), custom_call_target="tpu_custom_call" | custom-call | flops 1 | bytes 1 | tf_op jit(solution)/shard_map/columns_product/pallas_call | solution.py:91
  319.3 3.0 fusion.10
  322.2 4.4 collective-permute-start.39
  326.6 2.6 add_convert_fusion.6
  329.3 1.8 collective-permute-start.40
  331.1 1.5 add_convert_fusion.5
  336.3 16.2 %input_backward.3.refs_1_ = f32[512,1536]{1,0:T(8,128)} custom-call(s32[20]{0:T(128)} %stack.90.meta, bf16[512,3072]{1,0:T(8,128)(2,1)} %get-tuple-element.283.refs_0_.refs_1_, bf16[512,3072]{1,0:T(8,128)(2,1)} %get-tuple-element.283.refs_0_.refs_1_, bf16[1536,384]{1,0:T(8,128)(2,1)} %get-tuple-element.177.refs_0_.refs_2_.refs_10_, ...), custom_call_target="tpu_custom_call" | custom-call | flops 10000000000 | bytes 20971520 | tf_op jit(solution)/shard_map/input_backward/pallas_call | solution.py:91
  353.5 7.0 %collective-permute-done.41 = bf16[384,1536]{1,0:T(8,128)(2,1)} collective-permute-done((bf16[384,1536]{1,0:T(8,128)(2,1)S(1)}, bf16[384,1536]{1,0:T(8,128)(2,1)}, u32[]{:S(2)}, u32[]{:S(2)}) %collective-permute-start.41) | collective-permute-done | bytes 1179680 | tf_op jit(solution)/shard_map/ppermute | solution.py:1150
  360.5 2.3 collective-permute-start.42
  362.8 1.9 add_convert_fusion.3
  367.7 2.2 add_convert_fusion.9
  370.0 1.6 collective-permute-start.43
  372.8 1.5 reshape.170
  375.8 1.5 reshape.171
  385.1 1.6 concatenate.34
  387.2 10.8 %input_backward.4.refs_4_ = f32[512,1536]{1,0:T(8,128)} custom-call(s32[20]{0:T(128)} %stack.90.meta, bf16[512,2048]{1,0:T(8,128)(2,1)} %get-tuple-element.227.refs_0_, f32[512,1536]{1,0:T(8,128)} %input_backward.3.refs_1_, bf16[1856,384]{1,0:T(8,128)(2,1)} %copy-done.1, bf16[1856,384]{1,0:T(8,128)(2,1)} %copy-done.2, ...), custom_call_target="tpu_custom_call" | custom-call | flops 1 | bytes 1 | tf_op jit(solution)/shard_map/input_backward/pallas_call | solution.py:91
  398.0 2.0 add_convert_fusion.11
  400.0 1.6 collective-permute-start.48
  406.9 2.4 add_convert_fusion.8
  413.1 5.1 %place_rows.3 = (f32[6448,384]{1,0:T(8,128)}, f32[8,384]{1,0:T(8,128)}) custom-call(s32[20]{0:T(128)} %stack.90.meta, bf16[1536,384]{1,0:T(8,128)(2,1)} %copy-done.15, bf16[1536,384]{1,0:T(8,128)(2,1)} %copy-done.39, bf16[6448,384]{1,0:T(8,128)(2,1)} %bitcast.71), custom_call_target="tpu_custom_call" | custom-call | flops 10000000000 | bytes 20971520 | tf_op jit(solution)/shard_map/place_rows/pallas_call | solution.py:91
  419.7 4.5 collective-permute-start.54
  424.1 2.5 collective-permute-start.55
  427.9 16.1 %input_backward.5 = f32[512,1536]{1,0:T(8,128)} custom-call(s32[20]{0:T(128)} %stack.90.meta, bf16[512,2048]{1,0:T(8,128)(2,1)} %get-tuple-element.227.refs_0_, bf16[512,1024]{1,0:T(8,128)(2,1)} %get-tuple-element.246.refs_0_.refs_1_, bf16[512,256]{1,0:T(8,128)(2,1)} %get-tuple-element.261.refs_2_, bf16[512,128]{1,0:T(8,128)(2,1)} %get-tuple-element.262.refs_3_, ...), custom_call_target="tpu_custom_call" | custom-call | flops 99999997952 | bytes 1 | tf_op jit(solution)/shard_map/input_backward/pallas_call | solution.py:91
  444.2 2.1 broadcast_select_fusion.4.refs_0_
  446.3 2.8 maximum_convert_fusion
  453.1 4.1 place_rows.4
  458.1 4.4 place_rows.5
  (267 shorter events, 80.5 us)
Async XLA Ops:
  5.0 41.2 %copy-start.1 = (bf16[1856,384]{1,0:T(8,128)(2,1)}, bf16[1856,384]{1,0:T(8,128)(2,1)S(1)}, u32[]{:S(2)}) copy-start(bf16[1856,384]{1,0:T(8,128)(2,1)S(1)} %maximum_maximum_fusion.refs_0_.refs_8_.refs_12_.refs_2_.refs_5_.refs_13_.refs_21_.refs_25_) | copy-start | bytes 4276228
  5.0 34.5 %collective-permute-start = (bf16[1856,384]{1,0:T(8,128)(2,1)S(1)}, bf16[1856,384]{1,0:T(8,128)(2,1)S(1)}, u32[]{:S(2)}, u32[]{:S(2)}) collective-permute-start(bf16[1856,384]{1,0:T(8,128)(2,1)S(1)} %maximum_maximum_fusion.refs_0_.refs_8_.refs_12_.refs_2_.refs_5_.refs_13_.refs_21_.refs_25_), channel_id=1, source_target_pairs={{0,1},{1,0},{2,3},{3,2},{4,6},{5,7},{6,4},{7,5},{8,9},{9,8},{10,11... | collective-permute-start | bytes 4276232 | tf_op jit(solution)/shard_map/ppermute | solution.py:1138
  8.0 38.2 %collective-permute-start.1 = (bf16[1856,384]{1,0:T(8,128)(2,1)S(1)}, bf16[1856,384]{1,0:T(8,128)(2,1)}, u32[]{:S(2)}, u32[]{:S(2)}) collective-permute-start(bf16[1856,384]{1,0:T(8,128)(2,1)S(1)} %maximum_maximum_fusion.refs_0_.refs_8_.refs_12_.refs_2_.refs_5_.refs_13_.refs_21_.refs_25_), channel_id=1, source_target_pairs={{0,2},{1,3},{2,0},{3,1},{4,5},{5,4},{6,7},{7,6},{8,10},{9,11},{10,... | collective-permute-start | bytes 4276232 | tf_op jit(solution)/shard_map/ppermute | solution.py:1138
  9.7 35.6 %collective-permute-start.7 = (bf16[5348]{0:T(1024)(128)(2,1)S(1)}, bf16[5348]{0:T(1024)(128)(2,1)S(1)}, u32[]{:S(2)}, u32[]{:S(2)}) collective-permute-start(bf16[5348]{0:T(1024)(128)(2,1)S(1)} %concatenate.29), channel_id=1, source_target_pairs={{0,3},{1,2},{2,1},{3,0},{4,7},{5,6},{6,5},{7,4},{8,11},{9,10},{10,... | collective-permute-start | bytes 32096 | tf_op jit(solution)/shard_map/ppermute | solution.py:1293
  9.8 35.6 %collective-permute-start.6 = (bf16[5348]{0:T(1024)(128)(2,1)S(1)}, bf16[5348]{0:T(1024)(128)(2,1)S(1)}, u32[]{:S(2)}, u32[]{:S(2)}) collective-permute-start(bf16[5348]{0:T(1024)(128)(2,1)S(1)} %concatenate.29), channel_id=1, source_target_pairs={{0,2},{1,3},{2,0},{3,1},{4,5},{5,4},{6,7},{7,6},{8,10},{9,11},{10,... | collective-permute-start | bytes 32096 | tf_op jit(solution)/shard_map/ppermute | solution.py:1293
  11.7 33.6 %collective-permute-start.5 = (bf16[5348]{0:T(1024)(128)(2,1)S(1)}, bf16[5348]{0:T(1024)(128)(2,1)S(1)}, u32[]{:S(2)}, u32[]{:S(2)}) collective-permute-start(bf16[5348]{0:T(1024)(128)(2,1)S(1)} %concatenate.29), channel_id=1, source_target_pairs={{0,1},{1,0},{2,3},{3,2},{4,6},{5,7},{6,4},{7,5},{8,9},{9,8},{10,11... | collective-permute-start | bytes 32096 | tf_op jit(solution)/shard_map/ppermute | solution.py:1293
  39.5 27.5 %copy-start.2 = (bf16[1856,384]{1,0:T(8,128)(2,1)}, bf16[1856,384]{1,0:T(8,128)(2,1)S(1)}, u32[]{:S(2)}) copy-start(bf16[1856,384]{1,0:T(8,128)(2,1)S(1)} %collective-permute-done.refs_1_.refs_9_.refs_13_.refs_3_.refs_6_.refs_14_.refs_22_.refs_26_) | copy-start | bytes 4276228
  39.5 18.9 %collective-permute-start.2 = (bf16[1856,384]{1,0:T(8,128)(2,1)S(1)}, bf16[1856,384]{1,0:T(8,128)(2,1)}, u32[]{:S(2)}, u32[]{:S(2)}) collective-permute-start(bf16[1856,384]{1,0:T(8,128)(2,1)S(1)} %collective-permute-done.refs_1_.refs_9_.refs_13_.refs_3_.refs_6_.refs_14_.refs_22_.refs_26_), channel_id=1, source_target_pairs={{0,2},{1,3},{2,0},{3,1},{4,5},{5,4},{6,7},{7,6},{8,10},{9,11},{10,... | collective-permute-start | bytes 4276232 | tf_op jit(solution)/shard_map/ppermute | solution.py:1138
  58.5 8.6 %collective-permute-start.8 = (bf16[1856,384]{1,0:T(8,128)(2,1)S(1)}, bf16[1856,384]{1,0:T(8,128)(2,1)S(1)}, u32[]{:S(2)}, u32[]{:S(2)}) collective-permute-start(bf16[1856,384]{1,0:T(8,128)(2,1)S(1)} %collective-permute-done.refs_1_.refs_9_.refs_13_.refs_3_.refs_6_.refs_14_.refs_22_.refs_26_), channel_id=1, source_target_pairs={{0,4},{4,0},{8,12},{12,8},{16,20},{20,16},{24,28},{28,24},{1,5},{5... | collective-permute-start | bytes 4276232 | tf_op jit(solution)/shard_map/ppermute | solution.py:1142
  58.5 8.6 %collective-permute-start.9 = (bf16[1856,384]{1,0:T(8,128)(2,1)}, bf16[1856,384]{1,0:T(8,128)(2,1)}, u32[]{:S(2)}, u32[]{:S(2)}) collective-permute-start(bf16[1856,384]{1,0:T(8,128)(2,1)} %collective-permute-done.1.refs_2_.refs_10_.refs_14_.refs_4_.refs_7_.refs_15_.refs_23_.refs_27_), channel_id=1, source_target_pairs={{0,4},{4,0},{8,12},{12,8},{16,20},{20,16},{24,28},{28,24},{1,5},{5... | collective-permute-start | bytes 4276232 | tf_op jit(solution)/shard_map/ppermute | solution.py:1142
  59.0 8.1 %collective-permute-start.10 = (bf16[1856,384]{1,0:T(8,128)(2,1)}, bf16[1856,384]{1,0:T(8,128)(2,1)}, u32[]{:S(2)}, u32[]{:S(2)}) collective-permute-start(bf16[1856,384]{1,0:T(8,128)(2,1)} %collective-permute-done.2.refs_3_.refs_11_.refs_15_.refs_5_.refs_8_.refs_16_.refs_24_.refs_28_), channel_id=1, source_target_pairs={{0,4},{4,0},{8,12},{12,8},{16,20},{20,16},{24,28},{28,24},{1,5},{5... | collective-permute-start | bytes 4276232 | tf_op jit(solution)/shard_map/ppermute | solution.py:1142
  59.7 33.0 %collective-permute-start.3 = (bf16[1536,384]{1,0:T(8,128)(2,1)}, bf16[1536,384]{1,0:T(8,128)(2,1)}, u32[]{:S(2)}, u32[]{:S(2)}) collective-permute-start(bf16[1536,384]{1,0:T(8,128)(2,1)} %get-tuple-element.177.refs_0_.refs_2_.refs_10_), channel_id=1, source_target_pairs={{0,1},{1,0},{2,3},{3,2},{4,6},{5,7},{6,4},{7,5},{8,9},{9,8},{10,11... | collective-permute-start | bytes 3538952 | tf_op jit(solution)/shard_map/ppermute | solution.py:1138
  62.2 30.6 %collective-permute-start.4 = (bf16[1536,384]{1,0:T(8,128)(2,1)}, bf16[1536,384]{1,0:T(8,128)(2,1)}, u32[]{:S(2)}, u32[]{:S(2)}) collective-permute-start(bf16[1536,384]{1,0:T(8,128)(2,1)} %get-tuple-element.177.refs_0_.refs_2_.refs_10_), channel_id=1, source_target_pairs={{0,2},{1,3},{2,0},{3,1},{4,5},{5,4},{6,7},{7,6},{8,10},{9,11},{10,... | collective-permute-start | bytes 3538952 | tf_op jit(solution)/shard_map/ppermute | solution.py:1138
  92.8 16.6 %collective-permute-start.11 = (bf16[1536,384]{1,0:T(8,128)(2,1)}, bf16[1536,384]{1,0:T(8,128)(2,1)}, u32[]{:S(2)}, u32[]{:S(2)}) collective-permute-start(bf16[1536,384]{1,0:T(8,128)(2,1)} %collective-permute-done.3.refs_1_.refs_3_.refs_11_), channel_id=1, source_target_pairs={{0,2},{1,3},{2,0},{3,1},{4,5},{5,4},{6,7},{7,6},{8,10},{9,11},{10,... | collective-permute-start | bytes 3538952 | tf_op jit(solution)/shard_map/ppermute | solution.py:1138
  97.1 23.4 %collective-permute-start.14 = (bf16[1536,384]{1,0:T(8,128)(2,1)}, bf16[1536,384]{1,0:T(8,128)(2,1)}, u32[]{:S(2)}, u32[]{:S(2)}) collective-permute-start(bf16[1536,384]{1,0:T(8,128)(2,1)} %collective-permute-done.3.refs_1_.refs_3_.refs_11_), channel_id=1, source_target_pairs={{0,4},{4,0},{8,12},{12,8},{16,20},{20,16},{24,28},{28,24},{1,5},{5... | collective-permute-start | bytes 3538952 | tf_op jit(solution)/shard_map/ppermute | solution.py:1142
  97.1 24.4 %collective-permute-start.15 = (bf16[1536,384]{1,0:T(8,128)(2,1)}, bf16[1536,384]{1,0:T(8,128)(2,1)}, u32[]{:S(2)}, u32[]{:S(2)}) collective-permute-start(bf16[1536,384]{1,0:T(8,128)(2,1)} %collective-permute-done.4.refs_2_.refs_4_.refs_12_), channel_id=1, source_target_pairs={{0,4},{4,0},{8,12},{12,8},{16,20},{20,16},{24,28},{28,24},{1,5},{5... | collective-permute-start | bytes 3538952 | tf_op jit(solution)/shard_map/ppermute | solution.py:1142
  109.3 12.2 %collective-permute-start.16 = (bf16[1536,384]{1,0:T(8,128)(2,1)}, bf16[1536,384]{1,0:T(8,128)(2,1)}, u32[]{:S(2)}, u32[]{:S(2)}) collective-permute-start(bf16[1536,384]{1,0:T(8,128)(2,1)} %collective-permute-done.11.refs_3_.refs_5_.refs_13_), channel_id=1, source_target_pairs={{0,4},{4,0},{8,12},{12,8},{16,20},{20,16},{24,28},{28,24},{1,5},{5... | collective-permute-start | bytes 3538952 | tf_op jit(solution)/shard_map/ppermute | solution.py:1142
  109.7 30.7 %collective-permute-start.18 = (bf16[512,1536]{1,0:T(8,128)(2,1)S(1)}, bf16[512,1536]{1,0:T(8,128)(2,1)S(1)}, u32[]{:S(2)}, u32[]{:S(2)}) collective-permute-start(bf16[512,1536]{1,0:T(8,128)(2,1)S(1)} %multiply_convert_fusion.pulled.refs_2_), channel_id=1, source_target_pairs={{0,4},{4,0},{8,12},{12,8},{16,20},{20,16},{24,28},{28,24},{1,5},{5... | collective-permute-start | bytes 4718600 | tf_op jit(solution)/shard_map/ppermute | solution.py:1142
  110.9 27.8 %collective-permute-start.12 = (bf16[384,1536]{1,0:T(8,128)(2,1)}, bf16[384,1536]{1,0:T(8,128)(2,1)}, u32[]{:S(2)}, u32[]{:S(2)}) collective-permute-start(bf16[384,1536]{1,0:T(8,128)(2,1)} %constant_dynamic-slice_fusion.4), channel_id=1, source_target_pairs={{0,1},{1,0},{2,3},{3,2},{4,6},{5,7},{6,4},{7,5},{8,9},{9,8},{10,11... | collective-permute-start | bytes 3538952 | tf_op jit(solution)/shard_map/ppermute | solution.py:1138
  120.5 18.9 %collective-permute-start.13 = (bf16[384,1536]{1,0:T(8,128)(2,1)}, bf16[384,1536]{1,0:T(8,128)(2,1)}, u32[]{:S(2)}, u32[]{:S(2)}) collective-permute-start(bf16[384,1536]{1,0:T(8,128)(2,1)} %constant_dynamic-slice_fusion.4), channel_id=1, source_target_pairs={{0,2},{1,3},{2,0},{3,1},{4,5},{5,4},{6,7},{7,6},{8,10},{9,11},{10,... | collective-permute-start | bytes 3538952 | tf_op jit(solution)/shard_map/ppermute | solution.py:1138
  138.6 3.8 collective-permute-start.17
  139.3 16.5 %collective-permute-start.19 = (bf16[384,1536]{1,0:T(8,128)(2,1)}, bf16[384,1536]{1,0:T(8,128)(2,1)}, u32[]{:S(2)}, u32[]{:S(2)}) collective-permute-start(bf16[384,1536]{1,0:T(8,128)(2,1)} %collective-permute-done.12.refs_5_), channel_id=1, source_target_pairs={{0,2},{1,3},{2,0},{3,1},{4,5},{5,4},{6,7},{7,6},{8,10},{9,11},{10,... | collective-permute-start | bytes 3538952 | tf_op jit(solution)/shard_map/ppermute | solution.py:1138
  153.6 30.1 %collective-permute-start.23 = (bf16[2,384,1536]{2,1,0:T(8,128)(2,1)}, bf16[2,384,1536]{2,1,0:T(8,128)(2,1)}, u32[]{:S(2)}, u32[]{:S(2)}) collective-permute-start(bf16[2,384,1536]{2,1,0:T(8,128)(2,1)} %get-tuple-element.207), channel_id=1, source_target_pairs={{0,2},{1,3},{2,0},{3,1},{4,5},{5,4},{6,7},{7,6},{8,10},{9,11},{10,... | collective-permute-start | bytes 7077896 | tf_op jit(solution)/shard_map/ppermute | solution.py:1138
  154.7 3.2 collective-permute-start.20
  155.2 6.1 %collective-permute-start.21 = (bf16[384,1536]{1,0:T(8,128)(2,1)}, bf16[384,1536]{1,0:T(8,128)(2,1)S(1)}, u32[]{:S(2)}, u32[]{:S(2)}) collective-permute-start(bf16[384,1536]{1,0:T(8,128)(2,1)} %collective-permute-done.13.refs_6_), channel_id=1, source_target_pairs={{0,4},{4,0},{8,12},{12,8},{16,20},{20,16},{24,28},{28,24},{1,5},{5... | collective-permute-start | bytes 3538952 | tf_op jit(solution)/shard_map/ppermute | solution.py:1142
  155.8 6.5 %collective-permute-start.22 = (bf16[384,1536]{1,0:T(8,128)(2,1)}, bf16[384,1536]{1,0:T(8,128)(2,1)}, u32[]{:S(2)}, u32[]{:S(2)}) collective-permute-start(bf16[384,1536]{1,0:T(8,128)(2,1)} %collective-permute-done.19.refs_7_), channel_id=1, source_target_pairs={{0,4},{4,0},{8,12},{12,8},{16,20},{20,16},{24,28},{28,24},{1,5},{5... | collective-permute-start | bytes 3538952 | tf_op jit(solution)/shard_map/ppermute | solution.py:1142
  162.3 21.5 %copy-start.9 = (bf16[2,384,1536]{2,1,0:T(8,128)(2,1)S(1)}, bf16[2,384,1536]{2,1,0:T(8,128)(2,1)}, u32[]{:S(2)}) copy-start(bf16[2,384,1536]{2,1,0:T(8,128)(2,1)} %get-tuple-element.206) | copy-start | bytes 7077892
  187.2 16.2 %collective-permute-start.24 = (bf16[1,384,1536]{2,1,0:T(8,128)(2,1)S(1)}, bf16[1,384,1536]{2,1,0:T(8,128)(2,1)S(1)}, u32[]{:S(2)}, u32[]{:S(2)}) collective-permute-start(bf16[1,384,1536]{2,1,0:T(8,128)(2,1)S(1)} %get-tuple-element.355), channel_id=1, source_target_pairs={{0,1},{1,0},{2,3},{3,2},{4,6},{5,7},{6,4},{7,5},{8,9},{9,8},{10,11... | collective-permute-start | bytes 3538952 | tf_op jit(solution)/shard_map/ppermute | solution.py:1138
  188.7 15.7 %copy-start = (bf16[512,1536]{1,0:T(8,128)(2,1)S(1)}, bf16[512,1536]{1,0:T(8,128)(2,1)}, u32[]{:S(2)}) copy-start(bf16[512,1536]{1,0:T(8,128)(2,1)} %fusion.2.x.refs_2_.refs_4_) | copy-start | bytes 4718596
  204.5 5.8 %collective-permute-start.25 = (bf16[512,1536]{1,0:T(8,128)(2,1)}, bf16[512,1536]{1,0:T(8,128)(2,1)S(1)}, u32[]{:S(2)}, u32[]{:S(2)}) collective-permute-start(bf16[512,1536]{1,0:T(8,128)(2,1)} %get-tuple-element.218), channel_id=1, source_target_pairs={{0,4},{4,0},{8,12},{12,8},{16,20},{20,16},{24,28},{28,24},{1,5},{5... | collective-permute-start | bytes 4718600 | tf_op jit(solution)/shard_map/ppermute | solution.py:1142
  204.5 5.8 %collective-permute-start.26 = (bf16[512,1536]{1,0:T(8,128)(2,1)S(1)}, bf16[512,1536]{1,0:T(8,128)(2,1)S(1)}, u32[]{:S(2)}, u32[]{:S(2)}) collective-permute-start(bf16[512,1536]{1,0:T(8,128)(2,1)S(1)} %copy-done), channel_id=1, source_target_pairs={{0,4},{4,0},{8,12},{12,8},{16,20},{20,16},{24,28},{28,24},{1,5},{5... | collective-permute-start | bytes 4718600 | tf_op jit(solution)/shard_map/ppermute | solution.py:1142
  223.4 30.5 %collective-permute-start.27 = (bf16[2,1536,384]{2,1,0:T(8,128)(2,1)}, bf16[2,1536,384]{2,1,0:T(8,128)(2,1)}, u32[]{:S(2)}, u32[]{:S(2)}) collective-permute-start(bf16[2,1536,384]{2,1,0:T(8,128)(2,1)} %get-tuple-element.228), channel_id=1, source_target_pairs={{0,2},{1,3},{2,0},{3,1},{4,5},{5,4},{6,7},{7,6},{8,10},{9,11},{10,... | collective-permute-start | bytes 7077896 | tf_op jit(solution)/shard_map/ppermute | solution.py:1138
  224.4 29.5 %collective-permute-start.28 = (bf16[384,1536]{1,0:T(8,128)(2,1)}, bf16[384,1536]{1,0:T(8,128)(2,1)S(1)}, u32[]{:S(2)}, u32[]{:S(2)}) collective-permute-start(bf16[384,1536]{1,0:T(8,128)(2,1)} %get-tuple-element.353), channel_id=1, source_target_pairs={{0,8},{4,12},{24,16},{28,20},{1,9},{5,13},{25,17},{29,21},{2,10},{... | collective-permute-start | bytes 3538952 | tf_op jit(solution)/shard_map/ppermute | solution.py:1150
  229.5 25.4 %copy-start.10 = (bf16[2,1536,384]{2,1,0:T(8,128)(2,1)S(1)}, bf16[2,1536,384]{2,1,0:T(8,128)(2,1)}, u32[]{:S(2)}) copy-start(bf16[2,1536,384]{2,1,0:T(8,128)(2,1)} %get-tuple-element.231) | copy-start | bytes 7077892
  253.9 7.7 %collective-permute-start.29 = (bf16[512,1024]{1,0:T(8,128)(2,1)}, bf16[512,1024]{1,0:T(8,128)(2,1)}, u32[]{:S(2)}, u32[]{:S(2)}) collective-permute-start(bf16[512,1024]{1,0:T(8,128)(2,1)} %get-tuple-element.230), channel_id=1, source_target_pairs={{0,4},{4,0},{8,12},{12,8},{16,20},{20,16},{24,28},{28,24},{1,5},{5... | collective-permute-start | bytes 3145736 | tf_op jit(solution)/shard_map/ppermute | solution.py:1142
  258.4 25.8 %collective-permute-start.30 = (bf16[1,1536,384]{2,1,0:T(8,128)(2,1)S(1)}, bf16[1,1536,384]{2,1,0:T(8,128)(2,1)S(1)}, u32[]{:S(2)}, u32[]{:S(2)}) collective-permute-start(bf16[1,1536,384]{2,1,0:T(8,128)(2,1)S(1)} %get-tuple-element.351), channel_id=1, source_target_pairs={{0,1},{1,0},{2,3},{3,2},{4,6},{5,7},{6,4},{7,5},{8,9},{9,8},{10,11... | collective-permute-start | bytes 3538952 | tf_op jit(solution)/shard_map/ppermute | solution.py:1138
  259.9 59.3 %collective-permute-start.36 = (bf16[384,1536]{1,0:T(8,128)(2,1)S(1)}, bf16[384,1536]{1,0:T(8,128)(2,1)}, u32[]{:S(2)}, u32[]{:S(2)}) collective-permute-start(bf16[384,1536]{1,0:T(8,128)(2,1)S(1)} %add_convert_fusion.7), channel_id=1, source_target_pairs={{8,16},{12,20},{16,8},{20,12},{9,17},{13,21},{17,9},{21,13},{10,18... | collective-permute-start | bytes 3538952 | tf_op jit(solution)/shard_map/ppermute | solution.py:1150
  270.0 31.8 %collective-permute-start.31 = (bf16[2,1024,384]{2,1,0:T(8,128)(2,1)}, bf16[2,1024,384]{2,1,0:T(8,128)(2,1)}, u32[]{:S(2)}, u32[]{:S(2)}) collective-permute-start(bf16[2,1024,384]{2,1,0:T(8,128)(2,1)} %get-tuple-element.265), channel_id=1, source_target_pairs={{0,2},{1,3},{2,0},{3,1},{4,5},{5,4},{6,7},{7,6},{8,10},{9,11},{10,... | collective-permute-start | bytes 4718600 | tf_op jit(solution)/shard_map/ppermute | solution.py:1138
  288.2 31.1 %collective-permute-start.34 = (bf16[1536,384]{1,0:T(8,128)(2,1)}, bf16[1536,384]{1,0:T(8,128)(2,1)}, u32[]{:S(2)}, u32[]{:S(2)}) collective-permute-start(bf16[1536,384]{1,0:T(8,128)(2,1)} %get-tuple-element.349), channel_id=1, source_target_pairs={{0,8},{4,12},{24,16},{28,20},{1,9},{5,13},{25,17},{29,21},{2,10},{... | collective-permute-start | bytes 3538952 | tf_op jit(solution)/shard_map/ppermute | solution.py:1150
  305.5 13.8 %collective-permute-start.35 = (bf16[1,1024,384]{2,1,0:T(8,128)(2,1)}, bf16[1,1024,384]{2,1,0:T(8,128)(2,1)}, u32[]{:S(2)}, u32[]{:S(2)}) collective-permute-start(bf16[1,1024,384]{2,1,0:T(8,128)(2,1)} %get-tuple-element.359), channel_id=1, source_target_pairs={{0,1},{1,0},{2,3},{3,2},{4,6},{5,7},{6,4},{7,5},{8,9},{9,8},{10,11... | collective-permute-start | bytes 2359304 | tf_op jit(solution)/shard_map/ppermute | solution.py:1138
  306.4 4.4 collective-permute-start.33
  307.1 2.0 collective-permute-start.32
  318.3 16.4 %collective-permute-start.37 = (bf16[2,768,384]{2,1,0:T(8,128)(2,1)}, bf16[2,768,384]{2,1,0:T(8,128)(2,1)S(1)}, u32[]{:S(2)}, u32[]{:S(2)}) collective-permute-start(bf16[2,768,384]{2,1,0:T(8,128)(2,1)} %get-tuple-element.279), channel_id=1, source_target_pairs={{0,2},{1,3},{2,0},{3,1},{4,5},{5,4},{6,7},{7,6},{8,10},{9,11},{10,... | collective-permute-start | bytes 3538952 | tf_op jit(solution)/shard_map/ppermute | solution.py:1138
  322.2 31.3 %collective-permute-start.39 = (bf16[1024,384]{1,0:T(8,128)(2,1)}, bf16[1024,384]{1,0:T(8,128)(2,1)}, u32[]{:S(2)}, u32[]{:S(2)}) collective-permute-start(bf16[1024,384]{1,0:T(8,128)(2,1)} %get-tuple-element.357), channel_id=1, source_target_pairs={{0,8},{4,12},{24,16},{28,20},{1,9},{5,13},{25,17},{29,21},{2,10},{... | collective-permute-start | bytes 2359304 | tf_op jit(solution)/shard_map/ppermute | solution.py:1150
  329.3 24.3 %collective-permute-start.40 = (bf16[1536,384]{1,0:T(8,128)(2,1)}, bf16[1536,384]{1,0:T(8,128)(2,1)}, u32[]{:S(2)}, u32[]{:S(2)}) collective-permute-start(bf16[1536,384]{1,0:T(8,128)(2,1)} %add_convert_fusion.6), channel_id=1, source_target_pairs={{8,16},{12,20},{16,8},{20,12},{9,17},{13,21},{17,9},{21,13},{10,18... | collective-permute-start | bytes 3538952 | tf_op jit(solution)/shard_map/ppermute | solution.py:1150
  332.6 27.9 %collective-permute-start.41 = (bf16[384,1536]{1,0:T(8,128)(2,1)S(1)}, bf16[384,1536]{1,0:T(8,128)(2,1)}, u32[]{:S(2)}, u32[]{:S(2)}) collective-permute-start(bf16[384,1536]{1,0:T(8,128)(2,1)S(1)} %add_convert_fusion.5), channel_id=1, source_target_pairs={{8,0},{12,4},{16,24},{20,28},{9,1},{13,5},{17,25},{21,29},{10,2},{... | collective-permute-start | bytes 3538952 | tf_op jit(solution)/shard_map/ppermute | solution.py:1150
  335.1 17.4 %collective-permute-start.38 = (bf16[1,768,384]{2,1,0:T(8,128)(2,1)S(1)}, bf16[1,768,384]{2,1,0:T(8,128)(2,1)S(1)}, u32[]{:S(2)}, u32[]{:S(2)}) collective-permute-start(bf16[1,768,384]{2,1,0:T(8,128)(2,1)S(1)} %get-tuple-element.363), channel_id=1, source_target_pairs={{0,1},{1,0},{2,3},{3,2},{4,6},{5,7},{6,4},{7,5},{8,9},{9,8},{10,11... | collective-permute-start | bytes 1769480 | tf_op jit(solution)/shard_map/ppermute | solution.py:1138
  360.5 37.5 %collective-permute-start.42 = (bf16[768,384]{1,0:T(8,128)(2,1)}, bf16[768,384]{1,0:T(8,128)(2,1)}, u32[]{:S(2)}, u32[]{:S(2)}) collective-permute-start(bf16[768,384]{1,0:T(8,128)(2,1)} %get-tuple-element.361), channel_id=1, source_target_pairs={{0,8},{4,12},{24,16},{28,20},{1,9},{5,13},{25,17},{29,21},{2,10},{... | collective-permute-start | bytes 1769480 | tf_op jit(solution)/shard_map/ppermute | solution.py:1150
  364.7 36.9 %collective-permute-start.44 = (bf16[1536,384]{1,0:T(8,128)(2,1)S(1)}, bf16[1536,384]{1,0:T(8,128)(2,1)}, u32[]{:S(2)}, u32[]{:S(2)}) collective-permute-start(bf16[1536,384]{1,0:T(8,128)(2,1)S(1)} %add_convert_fusion.3), channel_id=1, source_target_pairs={{8,0},{12,4},{16,24},{20,28},{9,1},{13,5},{17,25},{21,29},{10,2},{... | collective-permute-start | bytes 3538952 | tf_op jit(solution)/shard_map/ppermute | solution.py:1150
  367.7 34.0 %collective-permute-start.45 = (bf16[384,1536]{1,0:T(8,128)(2,1)S(1)}, bf16[384,1536]{1,0:T(8,128)(2,1)}, u32[]{:S(2)}, u32[]{:S(2)}) collective-permute-start(bf16[384,1536]{1,0:T(8,128)(2,1)S(1)} %broadcast_select_fusion.3), channel_id=1, source_target_pairs={{0,4},{4,0},{8,12},{12,8},{16,20},{20,16},{24,28},{28,24},{1,5},{5... | collective-permute-start | bytes 3538952 | tf_op jit(solution)/shard_map/ppermute | solution.py:1142
  370.0 31.7 %collective-permute-start.43 = (bf16[1024,384]{1,0:T(8,128)(2,1)}, bf16[1024,384]{1,0:T(8,128)(2,1)}, u32[]{:S(2)}, u32[]{:S(2)}) collective-permute-start(bf16[1024,384]{1,0:T(8,128)(2,1)} %add_convert_fusion.9), channel_id=1, source_target_pairs={{8,16},{12,20},{16,8},{20,12},{9,17},{13,21},{17,9},{21,13},{10,18... | collective-permute-start | bytes 2359304 | tf_op jit(solution)/shard_map/ppermute | solution.py:1150
  386.7 15.0 %collective-permute-start.46 = (f32[4,4964]{1,0:T(4,128)}, f32[4,4964]{1,0:T(4,128)S(1)}, u32[]{:S(2)}, u32[]{:S(2)}) collective-permute-start(f32[4,4964]{1,0:T(4,128)} %concatenate.34), channel_id=1, source_target_pairs={{0,4},{4,0},{8,12},{12,8},{16,20},{20,16},{24,28},{28,24},{1,5},{5... | collective-permute-start | bytes 238280 | tf_op jit(solution)/shard_map/ppermute | solution.py:1142
  400.0 18.2 %collective-permute-start.48 = (bf16[768,384]{1,0:T(8,128)(2,1)}, bf16[768,384]{1,0:T(8,128)(2,1)}, u32[]{:S(2)}, u32[]{:S(2)}) collective-permute-start(bf16[768,384]{1,0:T(8,128)(2,1)} %add_convert_fusion.11), channel_id=1, source_target_pairs={{8,16},{12,20},{16,8},{20,12},{9,17},{13,21},{17,9},{21,13},{10,18... | collective-permute-start | bytes 1769480 | tf_op jit(solution)/shard_map/ppermute | solution.py:1150
  403.1 7.7 %collective-permute-start.47 = (bf16[1536,384]{1,0:T(8,128)(2,1)S(1)}, bf16[1536,384]{1,0:T(8,128)(2,1)S(1)}, u32[]{:S(2)}, u32[]{:S(2)}) collective-permute-start(bf16[1536,384]{1,0:T(8,128)(2,1)S(1)} %broadcast_select_fusion.2.own), channel_id=1, source_target_pairs={{0,4},{4,0},{8,12},{12,8},{16,20},{20,16},{24,28},{28,24},{1,5},{5... | collective-permute-start | bytes 3538952 | tf_op jit(solution)/shard_map/ppermute | solution.py:1142
  403.3 14.9 %collective-permute-start.49 = (f32[1,4964]{1,0:T(1,128)S(1)}, f32[1,4964]{1,0:T(1,128)S(1)}, u32[]{:S(2)}, u32[]{:S(2)}) collective-permute-start(f32[1,4964]{1,0:T(1,128)S(1)} %get-tuple-element.372), channel_id=1, source_target_pairs={{0,1},{1,0},{2,3},{3,2},{4,5},{5,4},{6,7},{7,6},{8,9},{9,8},{10,11... | collective-permute-start | bytes 59576 | tf_op jit(solution)/shard_map/ppermute | solution.py:1146
  404.7 13.5 %collective-permute-start.50 = (f32[1,4964]{1,0:T(1,128)S(1)}, f32[1,4964]{1,0:T(1,128)S(1)}, u32[]{:S(2)}, u32[]{:S(2)}) collective-permute-start(f32[1,4964]{1,0:T(1,128)S(1)} %get-tuple-element.371), channel_id=1, source_target_pairs={{0,2},{1,3},{2,0},{3,1},{4,6},{5,7},{6,4},{7,5},{8,10},{9,11},{10,... | collective-permute-start | bytes 59576 | tf_op jit(solution)/shard_map/ppermute | solution.py:1146
  405.8 12.4 %collective-permute-start.51 = (f32[1,4964]{1,0:T(1,128)S(1)}, f32[1,4964]{1,0:T(1,128)S(1)}, u32[]{:S(2)}, u32[]{:S(2)}) collective-permute-start(f32[1,4964]{1,0:T(1,128)S(1)} %get-tuple-element.370), channel_id=1, source_target_pairs={{0,3},{1,2},{2,1},{3,0},{4,7},{5,6},{6,5},{7,4},{8,11},{9,10},{10,... | collective-permute-start | bytes 59576 | tf_op jit(solution)/shard_map/ppermute | solution.py:1146
  411.8 32.3 %collective-permute-start.52 = (bf16[1024,384]{1,0:T(8,128)(2,1)}, bf16[1024,384]{1,0:T(8,128)(2,1)}, u32[]{:S(2)}, u32[]{:S(2)}) collective-permute-start(bf16[1024,384]{1,0:T(8,128)(2,1)} %add_convert_fusion.8), channel_id=1, source_target_pairs={{8,0},{12,4},{16,24},{20,28},{9,1},{13,5},{17,25},{21,29},{10,2},{... | collective-permute-start | bytes 2359304 | tf_op jit(solution)/shard_map/ppermute | solution.py:1150
  419.7 24.4 %collective-permute-start.54 = (f32[1,4964]{1,0:T(1,128)S(1)}, f32[1,4964]{1,0:T(1,128)S(1)}, u32[]{:S(2)}, u32[]{:S(2)}) collective-permute-start(f32[1,4964]{1,0:T(1,128)S(1)} %add_add_fusion), channel_id=1, source_target_pairs={{0,16},{4,20},{8,24},{12,28},{16,0},{20,4},{24,8},{28,12},{1,17},{... | collective-permute-start | bytes 59576 | tf_op jit(solution)/shard_map/ppermute | solution.py:1150
  424.1 19.9 %collective-permute-start.55 = (f32[1,4964]{1,0:T(1,128)S(1)}, f32[1,4964]{1,0:T(1,128)S(1)}, u32[]{:S(2)}, u32[]{:S(2)}) collective-permute-start(f32[1,4964]{1,0:T(1,128)S(1)} %add_add_fusion), channel_id=1, source_target_pairs={{0,24},{4,28},{8,16},{12,20},{16,8},{20,12},{24,0},{28,4},{1,25},{... | collective-permute-start | bytes 59576 | tf_op jit(solution)/shard_map/ppermute | solution.py:1150
  426.6 17.5 %collective-permute-start.53 = (f32[1,4964]{1,0:T(1,128)S(1)}, f32[1,4964]{1,0:T(1,128)S(1)}, u32[]{:S(2)}, u32[]{:S(2)}) collective-permute-start(f32[1,4964]{1,0:T(1,128)S(1)} %add_add_fusion), channel_id=1, source_target_pairs={{0,8},{4,12},{8,0},{12,4},{16,24},{20,28},{24,16},{28,20},{1,9},{5... | collective-permute-start | bytes 59576 | tf_op jit(solution)/shard_map/ppermute | solution.py:1150
  426.6 25.9 %collective-permute-start.56 = (bf16[768,384]{1,0:T(8,128)(2,1)S(1)}, bf16[768,384]{1,0:T(8,128)(2,1)S(1)}, u32[]{:S(2)}, u32[]{:S(2)}) collective-permute-start(bf16[768,384]{1,0:T(8,128)(2,1)S(1)} %add_convert_fusion.10), channel_id=1, source_target_pairs={{8,0},{12,4},{16,24},{20,28},{9,1},{13,5},{17,25},{21,29},{10,2},{... | collective-permute-start | bytes 1769480 | tf_op jit(solution)/shard_map/ppermute | solution.py:1150
  446.3 6.8 %collective-permute-start.57 = (bf16[1024,384]{1,0:T(8,128)(2,1)}, bf16[1024,384]{1,0:T(8,128)(2,1)}, u32[]{:S(2)}, u32[]{:S(2)}) collective-permute-start(bf16[1024,384]{1,0:T(8,128)(2,1)} %broadcast_select_fusion.4.refs_0_), channel_id=1, source_target_pairs={{0,4},{4,0},{8,12},{12,8},{16,20},{20,16},{24,28},{28,24},{1,5},{5... | collective-permute-start | bytes 2359304 | tf_op jit(solution)/shard_map/ppermute | solution.py:1142
  452.5 4.7 %collective-permute-start.58 = (bf16[768,384]{1,0:T(8,128)(2,1)S(1)}, bf16[768,384]{1,0:T(8,128)(2,1)S(1)}, u32[]{:S(2)}, u32[]{:S(2)}) collective-permute-start(bf16[768,384]{1,0:T(8,128)(2,1)S(1)} %broadcast_select_fusion.5.refs_0_), channel_id=1, source_target_pairs={{0,4},{4,0},{8,12},{12,8},{16,20},{20,16},{24,28},{28,24},{1,5},{5... | collective-permute-start | bytes 1769480 | tf_op jit(solution)/shard_map/ppermute | solution.py:1142
  (38 other events, 144.7 us)
